TPU v7x, 128 devices: a whole 4x4x4 slice. The times are simulated.
128 devices in a mesh: section: 16 (over y_hi, x, core), tp: 8 (over z, y_lo).
Axes of the slice: x: 4, y: 4 (y_hi: 2, y_lo: 2; y = y_hi * 2 + y_lo), z: 4, core: 2. Of those that a mesh axis runs over, the one named last changes fastest.
Arguments:
- inputs: bfloat16 [16, 1024, 3584], P('section', 'tp'), may hold values from -6 to 6
- norm_gain: float32 [16, 3584], P('section'), may hold values from 0.5 to 1.5
- incoming_grad: bfloat16 [16, 1024, 3584], P('section', 'tp'), may hold values from -6 to 6
- up_tiles: bfloat16 [16, 784, 128, 128], P('section', 'tp'), may hold values from -0.1875 to 0.1875
- up_index: int32 [16, 784, 2], P('section', 'tp'), may hold values from 0 to 27, as said below
- up_count: int32 [16, 8], P('section', 'tp'), may hold values from 49 to 98, as said below
- down_tiles: bfloat16 [16, 784, 128, 128], P('section', 'tp'), may hold values from -0.09375 to 0.09375
- down_index: int32 [16, 784, 2], P('section', 'tp'), may hold values from 0 to 27, as said below
- down_count: int32 [16, 8], P('section', 'tp'), may hold values from 49 to 98, as said below
Outputs:
- input_grad: bfloat16 [16, 1024, 3584], P('section', 'tp')
- up_grad: bfloat16 [16, 784, 128, 128], P('section', 'tp')
- down_grad: bfloat16 [16, 784, 128, 128], P('section', 'tp')
Inputs may be any that keep to these rules, and one draw needn't show every extreme that they name: `up_index`: each shard's list names 98 different blocks: column 0 a feature block below 28, column 1 a unit block below 14. `down_index`: each shard's list names 98 different blocks: column 0 a unit block below 14, column 1 a feature block below 28. Only the first up_count entries of a shard's list are kept blocks. In every section some shard has all 98. Only the first down_count entries of a shard's list are kept blocks. In every section some shard has all 98.
All inputs are finite; a program needn't handle non-finite values.
Results may differ from a plain program's by a relative error of at most 0.012.
Values may be sent and summed in bfloat16 or wider, within the bound.
No kernel may reach another device: no remote copies, remote signals or barrier semaphores. Data moves between devices by JAX's collectives and lax.ppermute only.
A program may use at most 256 MiB of HBM per device.

v0:
```python
import math

import jax
import jax.numpy as jnp
from jax import lax
from jax.sharding import PartitionSpec as P

FF = 14336


EPS = 1e-05
GELU_C = 0.7978845608028654


def passed_along(value, axis, steps):
    count = lax.axis_size(axis)
    pairs = [(source, (source + steps) % count) for source in range(count)]
    return lax.ppermute(value, axis, pairs)


def gelu_value(pre_act):
    inner = jnp.tanh(GELU_C * (pre_act + 0.044715 * pre_act * pre_act * pre_act))
    return 0.5 * pre_act * (1.0 + inner)


def gelu_slope(pre_act):
    inner = jnp.tanh(GELU_C * (pre_act + 0.044715 * pre_act * pre_act * pre_act))
    return 0.5 * (1.0 + inner) + 0.5 * pre_act * (1.0 - inner * inner) * GELU_C * (
        1.0 + 3.0 * 0.044715 * pre_act * pre_act
    )


def pick_columns(left, take_index, tile_side):
    return jnp.take(left.reshape(left.shape[0], -1, tile_side), take_index, axis=1)


def spread_rows(picked, tiles, put_index, block_count, form):
    row_count, tile_count, tile_side = picked.shape
    row_step = math.gcd(256, row_count)
    slabs = picked.reshape(row_count // row_step, row_step, tile_count, tile_side)

    def one_slab(slab):
        product = jnp.einsum(form, slab, tiles, preferred_element_type=jnp.float32)
        spread = jnp.zeros((row_step, block_count, tile_side), jnp.float32)
        spread = spread.at[:, put_index, :].add(product)
        return spread.reshape(row_step, block_count * tile_side)

    results = lax.map(one_slab, slabs)
    return results.reshape(row_count, block_count * tile_side)


def tile_outer(left_pick, right_pick, kept_mask):
    summed = jnp.einsum("tkb,tkc->kbc", left_pick, right_pick, preferred_element_type=jnp.float32)
    return jnp.where(kept_mask[:, None, None], summed, 0.0).astype(jnp.bfloat16)


def body(
    inputs,
    norm_gain,
    incoming_grad,
    up_tiles,
    up_index,
    up_count,
    down_tiles,
    down_index,
    down_count,
):
    tile_side = up_tiles.shape[-1]
    feature_count = inputs.shape[-1]
    feature_blocks = feature_count // tile_side
    unit_blocks = FF // lax.axis_size("tp") // tile_side
    gain = norm_gain[0][None, :]
    inputs_f = inputs[0].astype(jnp.float32)
    rms_inv = lax.rsqrt(jnp.mean(inputs_f * inputs_f, axis=-1, keepdims=True) + EPS)
    normed = inputs_f * rms_inv
    units = (normed * gain).astype(jnp.bfloat16)
    arriving = passed_along(incoming_grad[0], "section", -1)
    all_units = lax.all_gather(units, "tp", axis=0, tiled=True)
    all_grad = lax.all_gather(arriving, "tp", axis=0, tiled=True)
    up_i = up_index[0]
    up_kept = jnp.arange(up_tiles.shape[1], dtype=jnp.int32) < up_count[0, 0]
    up_live = jnp.where(up_kept[:, None, None], up_tiles[0], jnp.zeros((), jnp.bfloat16))
    down_i = down_index[0]
    down_kept = jnp.arange(down_tiles.shape[1], dtype=jnp.int32) < down_count[0, 0]
    down_live = jnp.where(down_kept[:, None, None], down_tiles[0], jnp.zeros((), jnp.bfloat16))
    grad_pick = pick_columns(all_grad, down_i[:, 1], tile_side)
    hidden_grad = spread_rows(grad_pick, down_live, down_i[:, 0], unit_blocks, "tkb,kcb->tkc")
    units_pick = pick_columns(all_units, up_i[:, 0], tile_side)
    pre = spread_rows(units_pick, up_live, up_i[:, 1], unit_blocks, "tkb,kbc->tkc")
    hidden = gelu_value(pre).astype(jnp.bfloat16)
    hidden_pick = pick_columns(hidden, down_i[:, 0], tile_side)
    down_grad = tile_outer(hidden_pick, grad_pick, down_kept)
    pre_grad = (hidden_grad * gelu_slope(pre)).astype(jnp.bfloat16)
    pre_grad_pick = pick_columns(pre_grad, up_i[:, 1], tile_side)
    up_grad = tile_outer(units_pick, pre_grad_pick, up_kept)
    unit_grad = lax.psum_scatter(
        spread_rows(pre_grad_pick, up_live, up_i[:, 0], feature_blocks, "tkb,kcb->tkc").astype(
            jnp.bfloat16
        ),
        "tp",
        scatter_dimension=0,
        tiled=True,
    ).astype(jnp.float32)
    scaled = unit_grad * gain
    normal_part = rms_inv * (scaled - normed * jnp.mean(scaled * normed, axis=-1, keepdims=True))
    input_grad = (arriving.astype(jnp.float32) + normal_part).astype(jnp.bfloat16)
    return (input_grad[None], up_grad[None], down_grad[None])


def solution(mesh):
    placed = (
        P("section", "tp", None),
        P("section", None),
        P("section", "tp", None),
        P("section", "tp", None, None),
        P("section", "tp", None),
        P("section", "tp"),
        P("section", "tp", None, None),
        P("section", "tp", None),
        P("section", "tp"),
    )
    return jax.shard_map(
        body,
        mesh=mesh,
        in_specs=placed,
        out_specs=(
            P("section", "tp", None),
            P("section", "tp", None, None),
            P("section", "tp", None, None),
        ),
        check_vma=False,
    )
```

profile of v0, /device:TPU:14, one launch (start us, length us, event | category | flops | bytes accessed | tf_op | source)
XLA Modules:
  0.0 1360.8 jit_solution(10501508838830312069)
XLA Ops:
  34.9 134.2 %all-gather.5.cloned.1.call-done = bf16[1024,3584]{0,1:T(8,128)(2,1)} async-done(((bf16[128,3584]{0,1:T(8,128)(2,1)}), bf16[1024,3584]{0,1:T(8,128)(2,1)}) %all-gather.5.cloned.1.call-update) | async-done | bytes 7340048 | tf_op jit(solution)/shard_map/all_gather | solution.py:78
  193.5 21.6 %broadcast_select_fusion.1 = bf16[98,1024,128]{2,1,0:T(8,128)(2,1)} fusion(bf16[98,1024,128]{2,1,0:T(8,128)(2,1)} %gather_fusion.1, pred[98]{0:T(512)(128)(4,1)S(1)} %get-tuple-element.167), kind=kLoop, calls=%fused_computation.35 | loop fusion | flops 12845056 | bytes 51380320 | tf_op jit(solution)/shard_map/jit(_take)/select_n | solution.py:34
  218.7 318.2 %while.31 = (s32[]{:T(128)}, f32[4,256,1792]{1,0,2:T(4,128)}, s32[98]{0:T(128)S(1)}, bf16[4,256,98,128]{3,1,0,2:T(8,128)(2,1)}, bf16[98,128,128]{2,1,0:T(8,128)(2,1)S(1)}, /*index=5*/s32[]{:T(128)}, f32[]{:T(128)}, s32[]{:T(128)}) while((s32[]{:T(128)}, f32[4,256,1792]{1,0,2:T(4,128)}, s32[98]{0:T(128)S(1)}, ...), condition=%wide.region_6.8_spmd, body=%wide.region_4.7_spmd.sunk | while | flops 825295168 | bytes 99550512 | solution.py:48
  229.8 20.7 %scatter_fusion.1 = f32[256,14,128]{2,0,1:T(8,128)S(1)} fusion(f32[256,14,128]{2,0,1:T(8,128)S(1)} %broadcast.222, s32[98]{0:T(128)S(1)} %fusion.74, f32[98,256,128]{2,1,0:T(8,128)} %fusion.75), kind=kCustom, calls=%fused_computation.5.clone.1 | custom fusion | flops 3211264 | bytes 38535560 | tf_op jit(solution)/shard_map/while/body/eval_jaxpr/scatter-add | solution.py:45
  258.5 39.8 %dynamic_update_slice.16 = f32[4,256,1792]{1,0,2:T(4,128)} dynamic-update-slice(f32[4,256,1792]{1,0,2:T(4,128)} %get-tuple-element.273, f32[1,256,1792]{1,0,2:T(1,128)} %copy.83, s32[]{:T(128)S(6)} %copy.93, s32[]{:T(128)} %constant.48.clone.1..sunk.1, s32[]{:T(128)} %constant.48.clone.1..sunk.1) | dynamic-update-slice | bytes 3670020 | tf_op jit(solution)/shard_map/while/body/jit(dynamic_update_index_in_dim)/dynamic_update_slice | solution.py:48
  309.5 20.6 %scatter_fusion.1 = f32[256,14,128]{2,0,1:T(8,128)S(1)} fusion(f32[256,14,128]{2,0,1:T(8,128)S(1)} %broadcast.222, s32[98]{0:T(128)S(1)} %fusion.74, f32[98,256,128]{2,1,0:T(8,128)} %fusion.75), kind=kCustom, calls=%fused_computation.5.clone.1 | custom fusion | flops 3211264 | bytes 38535560 | tf_op jit(solution)/shard_map/while/body/eval_jaxpr/scatter-add | solution.py:45
  338.1 39.8 %dynamic_update_slice.16 = f32[4,256,1792]{1,0,2:T(4,128)} dynamic-update-slice(f32[4,256,1792]{1,0,2:T(4,128)} %get-tuple-element.273, f32[1,256,1792]{1,0,2:T(1,128)} %copy.83, s32[]{:T(128)S(6)} %copy.93, s32[]{:T(128)} %constant.48.clone.1..sunk.1, s32[]{:T(128)} %constant.48.clone.1..sunk.1) | dynamic-update-slice | bytes 3670020 | tf_op jit(solution)/shard_map/while/body/jit(dynamic_update_index_in_dim)/dynamic_update_slice | solution.py:48
  417.6 39.8 %dynamic_update_slice.16 = f32[4,256,1792]{1,0,2:T(4,128)} dynamic-update-slice(f32[4,256,1792]{1,0,2:T(4,128)} %get-tuple-element.273, f32[1,256,1792]{1,0,2:T(1,128)} %copy.83, s32[]{:T(128)S(6)} %copy.93, s32[]{:T(128)} %constant.48.clone.1..sunk.1, s32[]{:T(128)} %constant.48.clone.1..sunk.1) | dynamic-update-slice | bytes 3670020 | tf_op jit(solution)/shard_map/while/body/jit(dynamic_update_index_in_dim)/dynamic_update_slice | solution.py:48
  497.1 39.8 %dynamic_update_slice.16 = f32[4,256,1792]{1,0,2:T(4,128)} dynamic-update-slice(f32[4,256,1792]{1,0,2:T(4,128)} %get-tuple-element.273, f32[1,256,1792]{1,0,2:T(1,128)} %copy.83, s32[]{:T(128)S(6)} %copy.93, s32[]{:T(128)} %constant.48.clone.1..sunk.1, s32[]{:T(128)} %constant.48.clone.1..sunk.1) | dynamic-update-slice | bytes 3670020 | tf_op jit(solution)/shard_map/while/body/jit(dynamic_update_index_in_dim)/dynamic_update_slice | solution.py:48
  579.7 21.5 %broadcast_select_fusion.2 = bf16[98,1024,128]{2,1,0:T(8,128)(2,1)} fusion(bf16[98,1024,128]{2,1,0:T(8,128)(2,1)} %gather_fusion, pred[98]{0:T(512)(128)(4,1)S(1)} %copy-done.18), kind=kLoop, calls=%fused_computation.36 | loop fusion | flops 12845056 | bytes 51380320 | tf_op jit(solution)/shard_map/jit(_take)/select_n | solution.py:34
  604.7 310.7 %while.30 = (s32[]{:T(128)}, f32[4,256,1792]{1,0,2:T(4,128)}, s32[98]{0:T(128)S(1)}, bf16[4,256,98,128]{3,1,0,2:T(8,128)(2,1)}, bf16[98,128,128]{2,1,0:T(8,128)(2,1)}, /*index=5*/s32[]{:T(128)}, f32[]{:T(128)}, s32[]{:T(128)}) while((s32[]{:T(128)}, f32[4,256,1792]{1,0,2:T(4,128)}, s32[98]{0:T(128)S(1)}, bf16[4,256,98,128]{3,1,0,2:T(8,128)(2,1)}, ...), condition=%wide.region_3.5_spmd, body=%wide.region_1.0_spmd.sunk | while | flops 825295168 | bytes 73860344 | solution.py:48
  642.8 39.6 %dynamic_update_slice.15 = f32[4,256,1792]{1,0,2:T(4,128)} dynamic-update-slice(f32[4,256,1792]{1,0,2:T(4,128)} %get-tuple-element.297, f32[1,256,1792]{1,0,2:T(1,128)S(1)} %copy.81, s32[]{:T(128)S(6)} %copy.99, s32[]{:T(128)} %constant.48.clone.1..sunk, s32[]{:T(128)} %constant.48.clone.1..sunk) | dynamic-update-slice | bytes 3670020 | tf_op jit(solution)/shard_map/while/body/jit(dynamic_update_index_in_dim)/dynamic_update_slice | solution.py:48
  720.4 39.6 %dynamic_update_slice.15 = f32[4,256,1792]{1,0,2:T(4,128)} dynamic-update-slice(f32[4,256,1792]{1,0,2:T(4,128)} %get-tuple-element.297, f32[1,256,1792]{1,0,2:T(1,128)S(1)} %copy.81, s32[]{:T(128)S(6)} %copy.99, s32[]{:T(128)} %constant.48.clone.1..sunk, s32[]{:T(128)} %constant.48.clone.1..sunk) | dynamic-update-slice | bytes 3670020 | tf_op jit(solution)/shard_map/while/body/jit(dynamic_update_index_in_dim)/dynamic_update_slice | solution.py:48
  798.1 39.6 %dynamic_update_slice.15 = f32[4,256,1792]{1,0,2:T(4,128)} dynamic-update-slice(f32[4,256,1792]{1,0,2:T(4,128)} %get-tuple-element.297, f32[1,256,1792]{1,0,2:T(1,128)S(1)} %copy.81, s32[]{:T(128)S(6)} %copy.99, s32[]{:T(128)} %constant.48.clone.1..sunk, s32[]{:T(128)} %constant.48.clone.1..sunk) | dynamic-update-slice | bytes 3670020 | tf_op jit(solution)/shard_map/while/body/jit(dynamic_update_index_in_dim)/dynamic_update_slice | solution.py:48
  875.8 39.6 %dynamic_update_slice.15 = f32[4,256,1792]{1,0,2:T(4,128)} dynamic-update-slice(f32[4,256,1792]{1,0,2:T(4,128)} %get-tuple-element.297, f32[1,256,1792]{1,0,2:T(1,128)S(1)} %copy.81, s32[]{:T(128)S(6)} %copy.99, s32[]{:T(128)} %constant.48.clone.1..sunk, s32[]{:T(128)} %constant.48.clone.1..sunk) | dynamic-update-slice | bytes 3670020 | tf_op jit(solution)/shard_map/while/body/jit(dynamic_update_index_in_dim)/dynamic_update_slice | solution.py:48
  958.4 21.9 %broadcast_select_fusion = bf16[98,1024,128]{2,1,0:T(8,128)(2,1)} fusion(bf16[98,1024,128]{2,1,0:T(8,128)(2,1)} %gather_fusion.2, pred[98]{0:T(512)(128)(4,1)S(1)} %copy-done.17), kind=kLoop, calls=%fused_computation.34 | loop fusion | flops 12845056 | bytes 51380320 | tf_op jit(solution)/shard_map/jit(_take)/select_n | solution.py:34
  980.3 207.0 %while.32 = (s32[]{:T(128)}, bf16[4,256,3584]{1,2,0:T(8,128)(2,1)}, s32[98]{0:T(128)S(1)}, bf16[4,256,98,128]{3,1,0,2:T(8,128)(2,1)}, bf16[98,128,128]{2,1,0:T(8,128)(2,1)S(1)}, /*index=5*/s32[]{:T(128)}, f32[]{:T(128)}) while((s32[]{:T(128)}, bf16[4,256,3584]{1,2,0:T(8,128)(2,1)}, s32[98]{0:T(128)S(1)}, ...), condition=%wide.region_9.12_spmd, body=%wide.region_7.11_spmd.sunk | while | flops 825295168 | bytes 73860336 | solution.py:48
  991.9 33.0 %scatter_fusion.2 = f32[256,28,128]{2,0,1:T(8,128)} fusion(f32[256,28,128]{2,0,1:T(8,128)} %broadcast.225, s32[98]{0:T(128)S(1)} %fusion.78, f32[98,256,128]{2,1,0:T(8,128)} %fusion.79), kind=kCustom, calls=%fused_computation.6.clone.1 | custom fusion | flops 3211264 | bytes 38535560 | tf_op jit(solution)/shard_map/while/body/eval_jaxpr/scatter-add | solution.py:45
  1043.6 33.0 %scatter_fusion.2 = f32[256,28,128]{2,0,1:T(8,128)} fusion(f32[256,28,128]{2,0,1:T(8,128)} %broadcast.225, s32[98]{0:T(128)S(1)} %fusion.78, f32[98,256,128]{2,1,0:T(8,128)} %fusion.79), kind=kCustom, calls=%fused_computation.6.clone.1 | custom fusion | flops 3211264 | bytes 38535560 | tf_op jit(solution)/shard_map/while/body/eval_jaxpr/scatter-add | solution.py:45
  1095.4 33.0 %scatter_fusion.2 = f32[256,28,128]{2,0,1:T(8,128)} fusion(f32[256,28,128]{2,0,1:T(8,128)} %broadcast.225, s32[98]{0:T(128)S(1)} %fusion.78, f32[98,256,128]{2,1,0:T(8,128)} %fusion.79), kind=kCustom, calls=%fused_computation.6.clone.1 | custom fusion | flops 3211264 | bytes 38535560 | tf_op jit(solution)/shard_map/while/body/eval_jaxpr/scatter-add | solution.py:45
  1147.1 33.0 %scatter_fusion.2 = f32[256,28,128]{2,0,1:T(8,128)} fusion(f32[256,28,128]{2,0,1:T(8,128)} %broadcast.225, s32[98]{0:T(128)S(1)} %fusion.78, f32[98,256,128]{2,1,0:T(8,128)} %fusion.79), kind=kCustom, calls=%fused_computation.6.clone.1 | custom fusion | flops 3211264 | bytes 38535560 | tf_op jit(solution)/shard_map/while/body/eval_jaxpr/scatter-add | solution.py:45
  1210.6 20.7 %fusion.31 = bf16[1,98,128,128]{3,2,1,0:T(8,128)(2,1)} fusion(pred[98]{0:T(512)(128)(4,1)S(1)} %copy-done.12, bf16[98,1024,128]{2,1,0:T(8,128)(2,1)} %bitcast.141, bf16[98,1024,128]{2,1,0:T(8,128)(2,1)} %bitcast.139), kind=kOutput, calls=%fused_computation.50 | convolution fusion | flops 3291545600 | bytes 54591584 | tf_op jit(solution)/shard_map/tkb,tkc->kbc/dot_general | solution.py:53
  1231.4 21.2 %fusion.32 = bf16[1,98,128,128]{3,2,1,0:T(8,128)(2,1)} fusion(pred[98]{0:T(512)(128)(4,1)S(1)} %copy-done.21, bf16[98,1024,128]{2,1,0:T(8,128)(2,1)} %bitcast.146, bf16[98,1024,128]{2,1,0:T(8,128)(2,1)} %gather_fusion.3, pred[98]{0:T(512)(128)(4,1)S(1)} %copy-done.22), kind=kOutput, calls=%fused_computation.51 | convolution fusion | flops 3304390656 | bytes 54591684 | tf_op jit(solution)/shard_map/tkb,tkc->kbc/dot_general | solution.py:53
  1252.6 94.9 %reduce-scatter.4.cloned.1.call-done = bf16[128,3584]{1,0:T(8,128)(2,1)} async-done(((bf16[1024,3584]{1,0:T(8,128)(2,1)}), bf16[128,3584]{1,0:T(8,128)(2,1)}) %reduce-scatter.4.cloned.1.call-update) | async-done | bytes 917520
  (175 shorter events, 517.7 us)
Async XLA Ops:
  7.2 20.0 %copy-start.19 = (s32[1,98,2]{1,2,0:T(2,128)S(1)}, s32[1,98,2]{1,2,0:T(2,128)}, u32[]{:S(2)}) copy-start(s32[1,98,2]{1,2,0:T(2,128)} %param.26) | copy-start | bytes 2356
  7.2 21.2 %copy-start.15 = (s32[1,98,2]{1,2,0:T(2,128)S(1)}, s32[1,98,2]{1,2,0:T(2,128)}, u32[]{:S(2)}) copy-start(s32[1,98,2]{1,2,0:T(2,128)} %param.23) | copy-start | bytes 2356
  7.2 161.9 %all-gather.5.cloned.1.call-start = ((), (), s32[]{:S(2)}) async-start(), calls=%async_computation.2 | async-start | bytes 8257536 | tf_op jit(solution)/shard_map/all_gather | solution.py:78
  8.8 21.4 %copy-start.4 = (bf16[1,128,3584]{1,2,0:T(8,128)(2,1)}, bf16[1,128,3584]{1,2,0:T(8,128)(2,1)S(1)}, u32[]{:S(2)}) copy-start(bf16[1,128,3584]{1,2,0:T(8,128)(2,1)S(1)} %copy.40) | copy-start | bytes 2752516
  11.6 543.8 %all-gather.3.cloned.1.call-start = ((), (), s32[]{:S(2)}) async-start(), calls=%async_computation.1 | async-start | bytes 8257536 | tf_op jit(solution)/shard_map/all_gather | solution.py:79
  13.2 11.2 collective-permute-start
  25.4 1322.1 %reduce-scatter.4.cloned.1.call-start = ((), (), s32[]{:S(2)}) async-start(), calls=%async_computation.3 | async-start | bytes 8257536
  25.5 7.5 copy-start.8
  252.2 46.1 %copy-start.1 = (bf16[98,128,128]{2,1,0:T(8,128)(2,1)S(1)}, bf16[98,128,128]{2,1,0:T(8,128)(2,1)}, u32[]{:S(2)}) copy-start(bf16[98,128,128]{2,1,0:T(8,128)(2,1)} %copy-done) | copy-start | bytes 9633796 | tf_op jit(solution)/shard_map/while
  331.8 46.1 %copy-start.1 = (bf16[98,128,128]{2,1,0:T(8,128)(2,1)S(1)}, bf16[98,128,128]{2,1,0:T(8,128)(2,1)}, u32[]{:S(2)}) copy-start(bf16[98,128,128]{2,1,0:T(8,128)(2,1)} %copy-done) | copy-start | bytes 9633796 | tf_op jit(solution)/shard_map/while
  411.3 46.1 %copy-start.1 = (bf16[98,128,128]{2,1,0:T(8,128)(2,1)S(1)}, bf16[98,128,128]{2,1,0:T(8,128)(2,1)}, u32[]{:S(2)}) copy-start(bf16[98,128,128]{2,1,0:T(8,128)(2,1)} %copy-done) | copy-start | bytes 9633796 | tf_op jit(solution)/shard_map/while
  490.8 46.1 %copy-start.1 = (bf16[98,128,128]{2,1,0:T(8,128)(2,1)S(1)}, bf16[98,128,128]{2,1,0:T(8,128)(2,1)}, u32[]{:S(2)}) copy-start(bf16[98,128,128]{2,1,0:T(8,128)(2,1)} %copy-done) | copy-start | bytes 9633796 | tf_op jit(solution)/shard_map/while
  536.9 28.9 %copy-start.2 = (bf16[98,128,128]{2,1,0:T(8,128)(2,1)}, bf16[98,128,128]{2,1,0:T(8,128)(2,1)S(1)}, u32[]{:S(2)}) copy-start(bf16[98,128,128]{2,1,0:T(8,128)(2,1)S(1)} %get-tuple-element.336) | copy-start | bytes 9633796
  565.8 14.0 %copy-start.18 = (pred[98]{0:T(512)(128)(4,1)S(1)}, pred[98]{0:T(512)(128)(4,1)}, u32[]{:S(2)}) copy-start(pred[98]{0:T(512)(128)(4,1)} %get-tuple-element.165) | copy-start | bytes 298
  945.6 12.9 copy-start.17
  958.4 21.9 %copy-start.3 = (bf16[98,128,128]{2,1,0:T(8,128)(2,1)S(1)}, bf16[98,128,128]{2,1,0:T(8,128)(2,1)}, u32[]{:S(2)}) copy-start(bf16[98,128,128]{2,1,0:T(8,128)(2,1)} %copy-done.2) | copy-start | bytes 9633796
  958.4 21.9 %copy-start.23 = (s32[98]{0:T(128)S(1)}, s32[98]{0:T(128)}, u32[]{:S(2)}) copy-start(s32[98]{0:T(128)} %get-tuple-element.314) | copy-start | bytes 1180
  1198.1 12.5 copy-start.12
  1210.6 20.7 %copy-start.21 = (pred[98]{0:T(512)(128)(4,1)S(1)}, pred[98]{0:T(512)(128)(4,1)}, u32[]{:S(2)}) copy-start(pred[98]{0:T(512)(128)(4,1)} %copy-done.20) | copy-start | bytes 298
  1210.6 20.7 %copy-start.22 = (pred[98]{0:T(512)(128)(4,1)S(1)}, pred[98]{0:T(512)(128)(4,1)}, u32[]{:S(2)}) copy-start(pred[98]{0:T(512)(128)(4,1)} %get-tuple-element.155) | copy-start | bytes 298
  1231.3 117.7 %copy-start.5 = (bf16[1,128,3584]{1,2,0:T(8,128)(2,1)S(1)}, bf16[1,128,3584]{1,2,0:T(8,128)(2,1)}, u32[]{:S(2)}) copy-start(bf16[1,128,3584]{1,2,0:T(8,128)(2,1)} %copy-done.4) | copy-start | bytes 2752516
  1231.4 117.7 %copy-start.10 = (f32[3584]{0:T(1024)S(1)}, f32[3584]{0:T(1024)}, u32[]{:S(2)}) copy-start(f32[3584]{0:T(1024)} %copy-done.9) | copy-start | bytes 43012
  1231.4 117.7 %copy-start.14 = (f32[128]{0:T(128)S(1)}, f32[128]{0:T(128)}, u32[]{:S(2)}) copy-start(f32[128]{0:T(128)} %copy-done.13) | copy-start | bytes 1540
  1231.4 118.3 %copy-start.7 = (bf16[128,3584]{0,1:T(8,128)(2,1)S(1)}, bf16[128,3584]{0,1:T(8,128)(2,1)}, u32[]{:S(2)}) copy-start(bf16[128,3584]{0,1:T(8,128)(2,1)} %copy-done.6) | copy-start | bytes 2752516
  (11 other events, 28.2 us)
Sparse Core Ops, SparseCore 0:
  11.7 157.3 all-gather.4
  170.7 148.3 all-gather.2
  1197.6 149.8 reduce-scatter.3
where the time goes:
time: 1370 us; the launch traced here: 1360 us
  local copies, waits for them, and re-layouts  561 us (41%)
  other arithmetic  386 us (28%)
  waiting for transfers between devices  240 us (18%)
  matrix products  157 us (11%)
  between operations  15.7 us (1%)
    dynamic_update_slice x20, local copies, waits for them, and re-layouts, spread_rows(): results = lax.map(one_slab, slabs)  376 us
    scatter-add x12, other arithmetic, one_slab(): spread = spread.at[:, put_index, :].add(product)  297 us
    all_gather x1, waiting for transfers between devices, body(): all_units = lax.all_gather(units, 'tp', axis=0, tiled=True)  134 us
    dot_general x12, matrix products, one_slab(): product = jnp.einsum(form, slab, tiles, preferred_element_type=jnp.float32)  115 us
    unnamed x4, waiting for transfers between devices  95 us
    select_n x3, other arithmetic, pick_columns(): jnp.take(left.reshape(left.shape[0], -1, tile_side), take_index, axis=1)  65 us
    gather x4, local copies, waits for them, and re-layouts, pick_columns(): jnp.take(left.reshape(left.shape[0], -1, tile_side), take_index, axis=1)  53.4 us
    dot_general x2, matrix products, tile_outer(): jnp.einsum('tkb,tkc->kbc', left_pick, right_pick, preferred_element_type=...  41.9 us
  transfers between devices with their start and end apart: 4, of which 3 were waited for; matrix products, arithmetic and copies ran while one was open for 33% of the time, Pallas kernels for 0%

commit v1 on v0

v1 whole, which is shorter than its diff:
```python
import functools

import jax
import jax.numpy as jnp
from jax import lax
from jax.experimental import pallas as pl
from jax.experimental.pallas import tpu as pltpu
from jax.sharding import PartitionSpec as P

FF = 14336
EPS = 1e-05
GELU_C = 0.7978845608028654
F32 = jnp.float32
BF16 = jnp.bfloat16
SIDE = 128
PAIR = 2
OFFSETS = (0, 1, -1, 2)
ANY = pl.BlockSpec(memory_space=pl.ANY)
VMEM = pl.BlockSpec(memory_space=pltpu.VMEM)
SMEM = pl.BlockSpec(memory_space=pltpu.SMEM)
ROOM = 60 * 1024 * 1024


def along_z(value, steps):
    count = lax.axis_size("tp")
    return lax.ppermute(value, "tp", [(i, (i + 2 * steps) % count) for i in range(count)])


def along_y(value):
    return lax.ppermute(value, "tp", [(i, i ^ 1) for i in range(lax.axis_size("tp"))])


def from_next_section(value):
    count = lax.axis_size("section")
    return lax.ppermute(value, "section", [(i, (i - 1) % count) for i in range(count)])


def plus(left, right):
    return (left.astype(F32) + right.astype(F32)).astype(BF16)


def lanes(block):
    return pl.ds(pl.multiple_of(block * SIDE, SIDE), SIDE)


def rounded_up(value, step):
    return -(-value // step) * step


def group_lists(index, count, key_column, width):
    length = index.shape[0]
    key, other = index[:, key_column], index[:, 1 - key_column]
    entry = jnp.arange(length, dtype=jnp.int32)
    live = entry < count
    same = (key[:, None] == key[None, :]) & live[None, :] & (entry[None, :] < entry[:, None])
    rank = jnp.sum(same.astype(jnp.int32), axis=1)
    opens = live & (rank % PAIR == 0)
    before = jnp.sum(((key[None, :] < key[:, None]) & opens[None, :]).astype(jnp.int32), axis=1)
    place = jnp.where(live, before * PAIR + rank, -1)
    at = jnp.arange(width, dtype=jnp.int32)
    empty = length * 32
    code = entry * 32 + other - empty
    codes = empty + jnp.sum(jnp.where(place[:, None] == at[None, :], code[:, None], 0), axis=0)
    keys = jnp.sum(jnp.where(place[:, None] == at[None, :] * PAIR, key[:, None], 0), axis=0)
    return codes, keys


def normed_kernel(inputs_ref, gain_ref, *unit_refs):
    rows = unit_refs[0].shape[0]
    for half, out_ref in enumerate(unit_refs):

        @pl.loop(0, rows // 16)
        def _(i):
            start = pl.multiple_of(i * 16, 16)
            value = inputs_ref[pl.ds(half * rows + start, 16), :].astype(F32)
            rms_inv = lax.rsqrt(jnp.mean(value * value, axis=-1, keepdims=True) + EPS)
            out_ref[pl.ds(start, 16), :] = (value * rms_inv * gain_ref[...]).astype(BF16)


def normed_units(inputs, gain, halves):
    rows, features = inputs.shape
    shape = jax.ShapeDtypeStruct((rows // halves, features), BF16)
    return pl.pallas_call(
        normed_kernel,
        out_shape=[shape] * halves,
        in_specs=[VMEM, VMEM],
        out_specs=[VMEM] * halves,
        compiler_params=pltpu.CompilerParams(vmem_limit_bytes=ROOM),
        cost_estimate=pl.CostEstimate(flops=0, bytes_accessed=4 * rows * features, transcendentals=0),
    )(inputs, gain)


def run_groups(count, unroll, one):
    whole = count // unroll

    @pl.loop(0, whole)
    def _(i):
        for j in range(unroll):
            one(i * unroll + j)

    for s in range(whole * unroll, count):
        one(s)


def start_tiles(tiles_ref, held, sem):
    count = tiles_ref.shape[0]
    copy = pltpu.make_async_copy(tiles_ref, held.at[pl.ds(0, count)], sem)
    copy.start()
    held[count] = jnp.zeros(held.shape[1:], BF16)
    return copy


def hidden_kernel(
    pieces, groups, codes_ref, keys_ref, *refs
):
    (unit_refs, grad_refs) = refs[: 2 * pieces], refs[2 * pieces : 3 * pieces]
    up_ref, down_ref, hidden_ref, pre_grad_ref = refs[3 * pieces : 3 * pieces + 4]
    units, grads, up, down, pre, hidden_grad, sems = refs[3 * pieces + 4 :]
    rows = unit_refs[0].shape[0]
    width = codes_ref.shape[1]
    copies = [start_tiles(up_ref, up, sems.at[0])]
    for i, ref in enumerate(unit_refs):
        copies.append(pltpu.make_async_copy(ref, units.at[pl.ds(i * rows, rows)], sems.at[1 + i]))
        copies[-1].start()
    late = [start_tiles(down_ref, down, sems.at[1 + 2 * pieces])]
    for i, ref in enumerate(grad_refs):
        for j in range(2):
            late.append(
                pltpu.make_async_copy(
                    ref.at[pl.ds(j * rows, rows)],
                    grads.at[pl.ds((j * pieces + i) * rows, rows)],
                    sems.at[2 + 2 * pieces + 2 * i + j],
                )
            )
            late[-1].start()
    pre[...] = jnp.zeros_like(pre)
    hidden_grad[...] = jnp.zeros_like(hidden_grad)
    for copy in copies:
        copy.wait()

    def add_pre(s):
        codes = [codes_ref[0, s * PAIR + i] for i in range(PAIR)]
        left = jnp.concatenate([units[:, lanes(code & 31)] for code in codes], axis=1)
        right = jnp.concatenate([up[code >> 5] for code in codes], axis=0)
        pre[:, lanes(keys_ref[0, s])] += jnp.dot(left, right, preferred_element_type=F32)

    run_groups(groups, 8, add_pre)
    for copy in late:
        copy.wait()

    def add_hidden_grad(s):
        codes = [codes_ref[1, s * PAIR + i] for i in range(PAIR)]
        left = jnp.concatenate([grads[:, lanes(code & 31)] for code in codes], axis=1)
        right = jnp.concatenate([down[code >> 5] for code in codes], axis=1)
        hidden_grad[:, lanes(keys_ref[1, s])] += lax.dot_general(
            left, right, (((1,), (1,)), ((), ())), preferred_element_type=F32
        )

    run_groups(groups, 8, add_hidden_grad)

    @pl.loop(0, pre.shape[0] // 32)
    def _(i):
        at = pl.ds(pl.multiple_of(i * 32, 32), 32)
        z = pre[at, :]
        square = z * z
        inner = jnp.tanh(GELU_C * (z + 0.044715 * square * z))
        hidden_ref[at, :] = (0.5 * z * (1.0 + inner)).astype(BF16)
        slope = 0.5 * (1.0 + inner) + 0.5 * z * (1.0 - inner * inner) * GELU_C * (
            1.0 + 3.0 * 0.044715 * square
        )
        pre_grad_ref[at, :] = (hidden_grad[at, :] * slope).astype(BF16)


def hidden_of(codes, keys, units, grads, up_tiles, down_tiles, unit_blocks, groups):
    pieces = len(grads)
    rows, features = units[0].shape
    tokens, wide = 2 * pieces * rows, unit_blocks * SIDE
    held = (up_tiles.shape[0] + 1,) + up_tiles.shape[1:]
    shape = jax.ShapeDtypeStruct((tokens, wide), BF16)
    flops = 4 * groups * PAIR * tokens * SIDE * SIDE
    return pl.pallas_call(
        functools.partial(hidden_kernel, pieces, groups),
        out_shape=[shape, shape],
        in_specs=[SMEM, SMEM] + [ANY] * (3 * pieces + 2),
        out_specs=[VMEM, VMEM],
        scratch_shapes=[
            pltpu.VMEM((tokens, features), BF16),
            pltpu.VMEM((tokens, features), BF16),
            pltpu.VMEM(held, BF16),
            pltpu.VMEM(held, BF16),
            pltpu.VMEM((tokens, wide), F32),
            pltpu.VMEM((tokens, wide), F32),
            pltpu.SemaphoreType.DMA((2 + 4 * pieces,)),
        ],
        compiler_params=pltpu.CompilerParams(vmem_limit_bytes=ROOM),
        cost_estimate=pl.CostEstimate(
            flops=4 * flops, bytes_accessed=4 * tokens * features, transcendentals=tokens * wide
        ),
    )(codes, keys, *units, *grads, up_tiles, down_tiles)


def unit_grad_kernel(groups, spans, codes_ref, keys_ref, pre_grad_ref, up_ref, *refs):
    out_refs = refs[: len(spans)]
    up, total, sem = refs[len(spans) :]
    copy = start_tiles(up_ref, up, sem.at[0])
    total[...] = jnp.zeros_like(total)
    copy.wait()

    def add(s):
        codes = [codes_ref[2, s * PAIR + i] for i in range(PAIR)]
        left = jnp.concatenate([pre_grad_ref[:, lanes(code & 31)] for code in codes], axis=1)
        right = jnp.concatenate([up[code >> 5] for code in codes], axis=1)
        total[:, lanes(keys_ref[2, s])] += lax.dot_general(
            left, right, (((1,), (1,)), ((), ())), preferred_element_type=F32
        )

    run_groups(groups, 9, add)
    for out_ref, parts in zip(out_refs, spans, strict=True):
        done = 0
        for start, size in parts:

            @pl.loop(0, size // 16)
            def _(i):
                step = pl.multiple_of(i * 16, 16)
                out_ref[pl.ds(done + step, 16), :] = total[pl.ds(start + step, 16), :].astype(BF16)

            done += size


def unit_grad_of(codes, keys, pre_grad, up_tiles, features, groups, spans):
    tokens = pre_grad.shape[0]
    held = (up_tiles.shape[0] + 1,) + up_tiles.shape[1:]
    flops = 2 * groups * PAIR * tokens * SIDE * SIDE
    return pl.pallas_call(
        functools.partial(unit_grad_kernel, groups, spans),
        out_shape=[
            jax.ShapeDtypeStruct((sum(size for _, size in parts), features), BF16) for parts in spans
        ],
        in_specs=[SMEM, SMEM, VMEM, ANY],
        out_specs=[VMEM] * len(spans),
        scratch_shapes=[
            pltpu.VMEM(held, BF16),
            pltpu.VMEM((tokens, features), F32),
            pltpu.SemaphoreType.DMA((1,)),
        ],
        compiler_params=pltpu.CompilerParams(vmem_limit_bytes=ROOM),
        cost_estimate=pl.CostEstimate(
            flops=4 * flops, bytes_accessed=2 * tokens * features, transcendentals=0
        ),
    )(codes, keys, pre_grad, up_tiles)


def up_grad_kernel(pieces, groups, codes_ref, keys_ref, *refs):
    unit_refs, slope_refs = refs[:pieces], refs[pieces : pieces + 2]
    out_ref, units, slopes, held, sems = refs[pieces + 2 :]
    rows, half = unit_refs[0].shape[0], slope_refs[0].shape[0]
    copies = []
    for i, ref in enumerate(unit_refs):
        copies.append(pltpu.make_async_copy(ref, units.at[pl.ds(i * rows, rows)], sems.at[i]))
    for i, ref in enumerate(slope_refs):
        copies.append(
            pltpu.make_async_copy(ref, slopes.at[pl.ds(i * half, half)], sems.at[pieces + i])
        )
    for copy in copies:
        copy.start()
    held[...] = jnp.zeros_like(held)
    for copy in copies:
        copy.wait()

    def one(s):
        codes = [codes_ref[0, s * PAIR + i] for i in range(PAIR)]
        left = jnp.concatenate([units[:, lanes(code & 31)] for code in codes], axis=1)
        summed = lax.dot_general(
            left,
            slopes[:, lanes(keys_ref[0, s])],
            (((0,), (0,)), ((), ())),
            preferred_element_type=F32,
        ).astype(BF16)
        for i, code in enumerate(codes):
            held[code >> 5] = summed[i * SIDE : (i + 1) * SIDE]

    run_groups(groups, 8, one)
    copy = pltpu.make_async_copy(held.at[pl.ds(0, out_ref.shape[0])], out_ref, sems.at[0])
    copy.start()
    copy.wait()


def up_grad_of(codes, keys, units, slopes, count, groups):
    pieces = len(units)
    rows, features = units[0].shape
    tokens, wide = pieces * rows, slopes[0].shape[1]
    flops = 2 * groups * PAIR * tokens * SIDE * SIDE
    return pl.pallas_call(
        functools.partial(up_grad_kernel, pieces, groups),
        out_shape=jax.ShapeDtypeStruct((count, SIDE, SIDE), BF16),
        in_specs=[SMEM, SMEM] + [ANY] * (pieces + 2),
        out_specs=ANY,
        scratch_shapes=[
            pltpu.VMEM((tokens, features), BF16),
            pltpu.VMEM((tokens, wide), BF16),
            pltpu.VMEM((count + 1, SIDE, SIDE), BF16),
            pltpu.SemaphoreType.DMA((pieces + 2,)),
        ],
        compiler_params=pltpu.CompilerParams(vmem_limit_bytes=ROOM),
        cost_estimate=pl.CostEstimate(
            flops=4 * flops, bytes_accessed=2 * tokens * features, transcendentals=0
        ),
    )(codes, keys, *units, *slopes)


def down_grad_kernel(pieces, groups, codes_ref, keys_ref, *refs):
    grad_refs, hidden_refs = refs[:pieces], refs[pieces : pieces + 2]
    out_ref, grads, hidden, turned, held, sems = refs[pieces + 2 :]
    rows, half = grad_refs[0].shape[0] // 2, hidden_refs[0].shape[0]
    each = pieces // 2
    copies = []
    for i, ref in enumerate(hidden_refs):
        copies.append(pltpu.make_async_copy(ref, hidden.at[pl.ds(i * half, half)], sems.at[i]))
    late = []
    for i, ref in enumerate(grad_refs):
        for j in range(2):
            at = (i // each) * half + (j * each + i % each) * rows
            late.append(
                pltpu.make_async_copy(
                    ref.at[pl.ds(j * rows, rows)],
                    grads.at[pl.ds(at, rows)],
                    sems.at[2 + 2 * i + j],
                )
            )
    for copy in copies + late:
        copy.start()
    held[...] = jnp.zeros_like(held)
    for copy in copies:
        copy.wait()

    @pl.loop(0, turned.shape[0])
    def _(c):
        turned[c] = hidden[:, lanes(c)].T

    for copy in late:
        copy.wait()

    def one(s):
        codes = [codes_ref[1, s * PAIR + i] for i in range(PAIR)]
        right = jnp.concatenate([grads[:, lanes(code & 31)] for code in codes], axis=1)
        summed = jnp.dot(turned[keys_ref[1, s]], right, preferred_element_type=F32).astype(BF16)
        for i, code in enumerate(codes):
            held[code >> 5] = summed[:, i * SIDE : (i + 1) * SIDE]

    run_groups(groups, 8, one)
    copy = pltpu.make_async_copy(held.at[pl.ds(0, out_ref.shape[0])], out_ref, sems.at[0])
    copy.start()
    copy.wait()


def down_grad_of(codes, keys, grads, hidden, count, groups):
    pieces = len(grads)
    rows, features = grads[0].shape
    tokens, wide = pieces * rows, hidden[0].shape[1]
    flops = 2 * groups * PAIR * tokens * SIDE * SIDE
    return pl.pallas_call(
        functools.partial(down_grad_kernel, pieces, groups),
        out_shape=jax.ShapeDtypeStruct((count, SIDE, SIDE), BF16),
        in_specs=[SMEM, SMEM] + [ANY] * (pieces + 2),
        out_specs=ANY,
        scratch_shapes=[
            pltpu.VMEM((tokens, features), BF16),
            pltpu.VMEM((tokens, wide), BF16),
            pltpu.VMEM((wide // SIDE, SIDE, tokens), BF16),
            pltpu.VMEM((count + 1, SIDE, SIDE), BF16),
            pltpu.SemaphoreType.DMA((2 + 2 * pieces,)),
        ],
        compiler_params=pltpu.CompilerParams(vmem_limit_bytes=ROOM),
        cost_estimate=pl.CostEstimate(
            flops=4 * flops, bytes_accessed=2 * tokens * features, transcendentals=0
        ),
    )(codes, keys, *grads, *hidden)


def input_grad_kernel(terms, inputs_ref, gain_ref, *refs):
    halves = len(terms)
    grad_refs, out_ref = refs[:halves], refs[-1]
    used = halves
    rows = grad_refs[0].shape[0]
    for half, count in enumerate(terms):
        term_refs = refs[used : used + count]
        used += count

        @pl.loop(0, rows // 16)
        def _(i):
            start = pl.multiple_of(i * 16, 16)
            here = pl.ds(start, 16)
            value = inputs_ref[pl.ds(half * rows + start, 16), :].astype(F32)
            rms_inv = lax.rsqrt(jnp.mean(value * value, axis=-1, keepdims=True) + EPS)
            normed = value * rms_inv
            unit_grad = term_refs[0][here, :].astype(F32)
            for ref in term_refs[1:]:
                unit_grad = unit_grad + ref[here, :].astype(F32)
            scaled = unit_grad * gain_ref[...]
            mean = jnp.mean(scaled * normed, axis=-1, keepdims=True)
            result = grad_refs[half][here, :].astype(F32) + rms_inv * (scaled - normed * mean)
            out_ref[pl.ds(half * rows + start, 16), :] = result.astype(BF16)


def input_grad_of(inputs, gain, arriving, terms):
    rows, features = inputs.shape
    flat = [term for half in terms for term in half]
    return pl.pallas_call(
        functools.partial(input_grad_kernel, tuple(len(half) for half in terms)),
        out_shape=jax.ShapeDtypeStruct((rows, features), BF16),
        in_specs=[VMEM] * (2 + len(arriving) + len(flat)),
        out_specs=VMEM,
        compiler_params=pltpu.CompilerParams(vmem_limit_bytes=ROOM),
        cost_estimate=pl.CostEstimate(flops=0, bytes_accessed=8 * rows * features, transcendentals=0),
    )(inputs, gain, *arriving, *flat)


def gathered_units(own, way):
    ahead, behind = along_z(own, -1), along_z(own, 1)
    far = along_z(behind, 1) if way > 0 else along_z(ahead, -1)
    same = [own, ahead, behind, far]
    return same + [along_y(piece) for piece in same]


def gathered_grads(own, way):
    both = jnp.concatenate([own, along_y(own)], axis=0)
    ahead, behind = along_z(both, -1), along_z(both, 1)
    far = along_z(behind, 1) if way > 0 else along_z(ahead, -1)
    return [both, ahead, behind, far]


def summed_along_z(parts, way):
    here, ahead, behind, far = parts
    if way > 0:
        one = along_z(plus(ahead, along_z(far, 1)), 1)
        two = along_z(behind, -1)
    else:
        one = along_z(plus(behind, along_z(far, -1)), -1)
        two = along_z(ahead, 1)
    return [here, one, two]


def body(
    inputs,
    norm_gain,
    incoming_grad,
    up_tiles,
    up_index,
    up_count,
    down_tiles,
    down_index,
    down_count,
):
    up, down = up_tiles[0], down_tiles[0]
    rows, features = inputs.shape[1:]
    count = up.shape[0]
    feature_blocks = features // SIDE
    unit_blocks = FF // lax.axis_size("tp") // SIDE
    by_unit = (count + unit_blocks * (PAIR - 1)) // PAIR
    by_feature = (count + feature_blocks * (PAIR - 1)) // PAIR
    width = rounded_up(PAIR * by_feature, SIDE)
    half = rows // 2
    halves = range(2)

    arriving = [from_next_section(incoming_grad[0, h * half : (h + 1) * half]) for h in halves]
    own_units = normed_units(inputs[0], norm_gain, 2)
    lists = [
        group_lists(up_index[0], up_count[0, 0], 1, width),
        group_lists(down_index[0], down_count[0, 0], 0, width),
        group_lists(up_index[0], up_count[0, 0], 0, width),
    ]
    codes = jnp.stack([pair[0] for pair in lists])
    keys = jnp.stack([pair[1] for pair in lists])

    units = [gathered_units(own_units[h], 1 - 2 * h) for h in halves]
    grads = [gathered_grads(arriving[h], 2 * h - 1) for h in halves]
    hidden, pre_grad, terms = [], [], []
    pieces = len(OFFSETS)
    for h in halves:
        one, two = hidden_of(codes, keys, units[h], grads[h], up, down, unit_blocks, by_unit)
        hidden.append(one)
        pre_grad.append(two)
        if h == 0:
            spans = [((pieces * half, pieces * half),)]
            spans += [((i * half, half),) for i in range(pieces)]
            sent, *kept = unit_grad_of(codes, keys, two, up, features, by_feature, tuple(spans))
            came = along_y(sent)
            parts = [plus(kept[i], came[i * half : (i + 1) * half]) for i in range(pieces)]
            terms.append(summed_along_z(parts, 1))
        else:
            spans = [((i * half, half), ((pieces + i) * half, half)) for i in range(pieces)]
            parts = unit_grad_of(codes, keys, two, up, features, by_feature, tuple(spans))
            sums = summed_along_z(parts, -1)
            other = (
                sums[0][half:].astype(F32) + sums[1][half:].astype(F32) + sums[2][half:].astype(F32)
            )
            terms.append([value[:half] for value in sums] + [along_y(other.astype(BF16))])
    up_grad = up_grad_of(codes, keys, units[0] + units[1], pre_grad, count, by_unit)
    down_grad = down_grad_of(codes, keys, grads[0] + grads[1], hidden, count, by_unit)
    input_grad = input_grad_of(inputs[0], norm_gain, arriving, terms)
    return (input_grad[None], up_grad[None], down_grad[None])


def solution(mesh):
    placed = (
        P("section", "tp", None),
        P("section", None),
        P("section", "tp", None),
        P("section", "tp", None, None),
        P("section", "tp", None),
        P("section", "tp"),
        P("section", "tp", None, None),
        P("section", "tp", None),
        P("section", "tp"),
    )
    return jax.shard_map(
        body,
        mesh=mesh,
        in_specs=placed,
        out_specs=(
            P("section", "tp", None),
            P("section", "tp", None, None),
            P("section", "tp", None, None),
        ),
        check_vma=False,
    )
```

time: 1370 us -> 253 us (0.18)
  local copies, waits for them, and re-layouts: 561 us -> 6.49 us
  other arithmetic: 386 us -> 6.78 us
  matrix products: 157 us -> 0 us
  waiting for transfers between devices: 240 us -> 94.5 us
  Pallas kernels: 0 us -> 101 us
  starting transfers between devices: 0.46 us -> 37.8 us
    dynamic_update_slice x20 -> x0, local copies, waits for them, and re-layouts: 376 us -> none  [spread_rows(): results = lax.map(one_slab, slabs)]
    scatter-add x12 -> x0, other arithmetic: 297 us -> none  [one_slab(): spread = spread.at[:, put_index, :].add(product)]
    dot_general x14 -> x0, matrix products: 157 us -> none  [the longest x12 115 us: one_slab(): product = jnp.einsum(form, slab, tiles, preferred_element_type=jnp.float32)]
    all_gather x2 -> x0, waiting for transfers between devices: 134 us -> none  [the longest x1 134 us: body(): all_units = lax.all_gather(units, 'tp', axis=0, tiled=True)]
    pallas_call x0 -> x8, Pallas kernels: none -> 101 us  [the longest x2 38.9 us: hidden_of(): pl.pallas_call(functools.partial(hidden_kernel, pieces, groups), out_shap...]
    unnamed x4 -> x0, waiting for transfers between devices: 95 us -> none
    ppermute x1 -> x32, waiting for transfers between devices: 10.9 us -> 94.5 us  [the longest x12 64.4 us: along_y(): lax.ppermute(value, 'tp', [(i, i ^ 1) for i in range(lax.axis_size('tp'))])]
    select_n x17 -> x3, other arithmetic: 69.2 us -> 0.02 us  [group_lists(): place = jnp.where(live, before * PAIR + rank, -1)]
  transfers between devices with their start and end apart: 4 -> 32, of which waited for: 3 -> 11; matrix products, arithmetic and copies ran while one was open for 33% -> 4% of each run, Pallas kernels for 0% -> 37%
where the time goes in v1:
time: 253 us; the launch traced here: 249 us
  Pallas kernels  101 us (40%)
  waiting for transfers between devices  94.5 us (37%)
  starting transfers between devices  37.8 us (15%)
  other arithmetic  6.78 us (3%)
  local copies, waits for them, and re-layouts  6.49 us (3%)
    ppermute x12, waiting for transfers between devices, along_y(): lax.ppermute(value, 'tp', [(i, i ^ 1) for i in range(lax.axis_size('tp'))])  64.4 us
    pallas_call x2, Pallas kernels, hidden_of(): pl.pallas_call(functools.partial(hidden_kernel, pieces, groups), out_shap...  38.9 us
    ppermute x18, starting transfers between devices, along_z(): lax.ppermute(value, 'tp', [(i, (i + 2 * steps) % count) for i in range(co...  25.3 us
    pallas_call x2, Pallas kernels, unit_grad_of(): pl.pallas_call(functools.partial(unit_grad_kernel, groups, spans), out_sh...  24.8 us
    ppermute x18, waiting for transfers between devices, along_z(): lax.ppermute(value, 'tp', [(i, (i + 2 * steps) % count) for i in range(co...  23.9 us
    pallas_call x1, Pallas kernels, up_grad_of(): pl.pallas_call(functools.partial(up_grad_kernel, pieces, groups), out_sha...  15.9 us
    pallas_call x1, Pallas kernels, down_grad_of(): pl.pallas_call(functools.partial(down_grad_kernel, pieces, groups), out_s...  13 us
    ppermute x12, starting transfers between devices, along_y(): lax.ppermute(value, 'tp', [(i, i ^ 1) for i in range(lax.axis_size('tp'))])  11.5 us
  transfers between devices with their start and end apart: 32, of which 11 were waited for; matrix products, arithmetic and copies ran while one was open for 4% of the time, Pallas kernels for 37%

profile of v1, /device:TPU:14, one launch (start us, length us, event | category | flops | bytes accessed | tf_op | source)
XLA Modules:
  0.0 249.3 jit_solution(2121303654822908711)
XLA Ops:
  0.7 3.1 %shard_map.112 = (bf16[64,3584]{1,0:T(8,128)(2,1)}, bf16[64,3584]{1,0:T(8,128)(2,1)}) custom-call(bf16[128,3584]{1,0:T(8,128)(2,1)} %bitcast.43, f32[1,3584]{1,0:T(1,128)} %gain_ref.3), custom_call_target="tpu_custom_call" | custom-call | bytes 1835008 | tf_op jit(solution)/shard_map/pallas_call | solution.py:83
  3.7 4.0 %collective-permute-start.17 = (bf16[64,3584]{1,0:T(8,128)(2,1)}, bf16[64,3584]{1,0:T(8,128)(2,1)S(1)}, u32[]{:S(2)}, u32[]{:S(2)}) collective-permute-start(bf16[64,3584]{1,0:T(8,128)(2,1)} %get-tuple-element.25.refs_0_.refs_8_), channel_id=1, source_target_pairs={{0,6},{1,7},{2,0},{3,1},{4,2},{5,3},{6,4},{7,5},{8,14},{9,15},{10,... | collective-permute-start | bytes 1376264 | tf_op jit(solution)/shard_map/ppermute | solution.py:26
  12.7 2.9 %collective-permute-done.1.refs_1_ = bf16[64,3584]{1,0:T(8,128)(2,1)S(1)} collective-permute-done((bf16[64,3584]{1,0:T(8,128)(2,1)S(1)}, bf16[64,3584]{1,0:T(8,128)(2,1)S(1)}, u32[]{:S(2)}, u32[]{:S(2)}) %collective-permute-start.1) | collective-permute-done | bytes 458784 | tf_op jit(solution)/shard_map/ppermute | solution.py:35
  17.1 3.3 %collective-permute-done.refs_0_ = bf16[64,3584]{1,0:T(8,128)(2,1)S(1)} collective-permute-done((bf16[64,3584]{1,0:T(8,128)(2,1)S(1)}, bf16[64,3584]{1,0:T(8,128)(2,1)S(1)}, u32[]{:S(2)}, u32[]{:S(2)}) %collective-permute-start) | collective-permute-done | bytes 458784 | tf_op jit(solution)/shard_map/ppermute | solution.py:35
  22.1 19.0 %collective-permute-done.24 = bf16[64,3584]{1,0:T(8,128)(2,1)S(1)} collective-permute-done((bf16[64,3584]{1,0:T(8,128)(2,1)S(1)}, bf16[64,3584]{1,0:T(8,128)(2,1)S(1)}, u32[]{:S(2)}, u32[]{:S(2)}) %collective-permute-start.24) | collective-permute-done | bytes 458784 | tf_op jit(solution)/shard_map/ppermute | solution.py:30
  44.7 4.7 %collective-permute-done.9 = bf16[64,3584]{1,0:T(8,128)(2,1)S(1)} collective-permute-done((bf16[64,3584]{1,0:T(8,128)(2,1)S(1)}, bf16[64,3584]{1,0:T(8,128)(2,1)S(1)}, u32[]{:S(2)}, u32[]{:S(2)}) %collective-permute-start.9) | collective-permute-done | bytes 458784 | tf_op jit(solution)/shard_map/ppermute | solution.py:30
  50.0 3.0 %collective-permute-start.25 = (bf16[128,3584]{1,0:T(8,128)(2,1)S(1)}, bf16[128,3584]{1,0:T(8,128)(2,1)S(1)}, u32[]{:S(2)}, u32[]{:S(2)}) collective-permute-start(bf16[128,3584]{1,0:T(8,128)(2,1)S(1)} %constant_dynamic-update-slice_fusion.2.refs_8_.refs_4_), channel_id=1, source_target_pairs={{0,6},{1,7},{2,0},{3,1},{4,2},{5,3},{6,4},{7,5},{8,14},{9,15},{10,... | collective-permute-start | bytes 2752520 | tf_op jit(solution)/shard_map/ppermute | solution.py:26
  53.0 18.8 %collective-permute-done.3.refs_2_ = bf16[64,3584]{1,0:T(8,128)(2,1)} collective-permute-done((bf16[64,3584]{1,0:T(8,128)(2,1)S(1)}, bf16[64,3584]{1,0:T(8,128)(2,1)}, u32[]{:S(2)}, u32[]{:S(2)}) %collective-permute-start.3) | collective-permute-done | bytes 458784 | tf_op jit(solution)/shard_map/ppermute | solution.py:26
  71.8 2.9 %collective-permute-start.10 = (bf16[128,3584]{1,0:T(8,128)(2,1)S(1)}, bf16[128,3584]{1,0:T(8,128)(2,1)}, u32[]{:S(2)}, u32[]{:S(2)}) collective-permute-start(bf16[128,3584]{1,0:T(8,128)(2,1)S(1)} %constant_dynamic-update-slice_fusion.refs_8_.refs_0_), channel_id=1, source_target_pairs={{0,6},{1,7},{2,0},{3,1},{4,2},{5,3},{6,4},{7,5},{8,14},{9,15},{10,... | collective-permute-start | bytes 2752520 | tf_op jit(solution)/shard_map/ppermute | solution.py:26
  78.2 8.9 %collective-permute-done.22.refs_6_.refs_14_ = bf16[64,3584]{1,0:T(8,128)(2,1)S(1)} collective-permute-done((bf16[64,3584]{1,0:T(8,128)(2,1)S(1)}, bf16[64,3584]{1,0:T(8,128)(2,1)S(1)}, u32[]{:S(2)}, u32[]{:S(2)}) %collective-permute-start.22) | collective-permute-done | bytes 458784 | tf_op jit(solution)/shard_map/ppermute | solution.py:30
  87.2 2.1 collective-permute-start.2
  89.2 6.2 %collective-permute-done.23.refs_7_.refs_15_ = bf16[64,3584]{1,0:T(8,128)(2,1)S(1)} collective-permute-done((bf16[64,3584]{1,0:T(8,128)(2,1)S(1)}, bf16[64,3584]{1,0:T(8,128)(2,1)S(1)}, u32[]{:S(2)}, u32[]{:S(2)}) %collective-permute-start.23) | collective-permute-done | bytes 458784 | tf_op jit(solution)/shard_map/ppermute | solution.py:30
  100.4 19.5 %shard_map.115 = (bf16[512,1792]{1,0:T(8,128)(2,1)}, bf16[512,1792]{1,0:T(8,128)(2,1)}) custom-call(s32[3,128]{1,0:T(4,128)} %pad_add_fusion.codes_ref, s32[3,128]{1,0:T(4,128)} %pad_add_fusion.1.keys_ref, bf16[64,3584]{1,0:T(8,128)(2,1)} %get-tuple-element.25.refs_0_.refs_8_, bf16[64,3584]{1,0:T(8,128)(2,1)} %copy-done.20, bf16[64,3584]{1,0:T(8,128)(2,1)} %copy-done.21, ...), custom_call_target="tpu_custom_call" | custom-call | flops 15032385536 | bytes 7340032 | tf_op jit(solution)/shard_map/pallas_call | solution.py:181
  123.5 12.4 %shard_map.116 = (bf16[128,3584]{1,0:T(8,128)(2,1)}, bf16[128,3584]{1,0:T(8,128)(2,1)}, bf16[128,3584]{1,0:T(8,128)(2,1)}, bf16[128,3584]{1,0:T(8,128)(2,1)}) custom-call(s32[3,128]{1,0:T(4,128)} %pad_add_fusion.codes_ref, s32[3,128]{1,0:T(4,128)} %pad_add_fusion.1.keys_ref, bf16[512,1792]{1,0:T(8,128)(2,1)} %get-tuple-element.26.pre_grad_ref.refs_17_, ...), custom_call_target="tpu_custom_call" | custom-call | flops 8455716864 | bytes 3670016 | tf_op jit(solution)/shard_map/pallas_call | solution.py:234
  135.9 2.1 collective-permute-start.28
  139.9 4.9 %collective-permute-done.8.refs_7_ = bf16[64,3584]{1,0:T(8,128)(2,1)S(1)} collective-permute-done((bf16[64,3584]{1,0:T(8,128)(2,1)}, bf16[64,3584]{1,0:T(8,128)(2,1)S(1)}, u32[]{:S(2)}, u32[]{:S(2)}) %collective-permute-start.8) | collective-permute-done | bytes 458784 | tf_op jit(solution)/shard_map/ppermute | solution.py:30
  145.6 19.5 %shard_map.113 = (bf16[512,1792]{1,0:T(8,128)(2,1)}, bf16[512,1792]{1,0:T(8,128)(2,1)}) custom-call(s32[3,128]{1,0:T(4,128)} %pad_add_fusion.codes_ref, s32[3,128]{1,0:T(4,128)} %pad_add_fusion.1.keys_ref, bf16[64,3584]{1,0:T(8,128)(2,1)} %get-tuple-element.18.refs_0_, bf16[64,3584]{1,0:T(8,128)(2,1)} %collective-permute-done.2.refs_1_, ...), custom_call_target="tpu_custom_call" | custom-call | flops 15032385536 | bytes 7340032 | tf_op jit(solution)/shard_map/pallas_call | solution.py:181
  165.1 12.4 %shard_map.114 = (bf16[256,3584]{1,0:T(8,128)(2,1)}, bf16[64,3584]{1,0:T(8,128)(2,1)}, bf16[64,3584]{1,0:T(8,128)(2,1)}, bf16[64,3584]{1,0:T(8,128)(2,1)}, bf16[64,3584]{1,0:T(8,128)(2,1)}) custom-call(s32[3,128]{1,0:T(4,128)} %pad_add_fusion.codes_ref, s32[3,128]{1,0:T(4,128)} %pad_add_fusion.1.keys_ref, ...), custom_call_target="tpu_custom_call" | custom-call | flops 8455716864 | bytes 3670016 | tf_op jit(solution)/shard_map/pallas_call | solution.py:234
  178.0 15.9 %shard_map.118 = bf16[98,128,128]{2,1,0:T(8,128)(2,1)} custom-call(s32[3,128]{1,0:T(4,128)} %pad_add_fusion.codes_ref, s32[3,128]{1,0:T(4,128)} %pad_add_fusion.1.keys_ref, bf16[64,3584]{1,0:T(8,128)(2,1)} %get-tuple-element.18.refs_0_, bf16[64,3584]{1,0:T(8,128)(2,1)} %collective-permute-done.2.refs_1_, bf16[64,3584]{1,0:T(8,128)(2,1)} %collective-permute-done.3.refs_2_, ...), custom_call_target="tpu_custom_call" | custom-call | flops 15032385536 | bytes 7340032 | tf_op jit(solution)/shard_map/pallas_call | solution.py:293
  196.8 18.7 %collective-permute-done.13 = bf16[256,3584]{1,0:T(8,128)(2,1)S(1)} collective-permute-done((bf16[256,3584]{1,0:T(8,128)(2,1)}, bf16[256,3584]{1,0:T(8,128)(2,1)S(1)}, u32[]{:S(2)}, u32[]{:S(2)}) %collective-permute-start.13) | collective-permute-done | bytes 1835040 | tf_op jit(solution)/shard_map/ppermute | solution.py:30
  218.6 2.8 %collective-permute-start.16 = (bf16[64,3584]{1,0:T(8,128)(2,1)}, bf16[64,3584]{1,0:T(8,128)(2,1)}, u32[]{:S(2)}, u32[]{:S(2)}) collective-permute-start(bf16[64,3584]{1,0:T(8,128)(2,1)} %get-tuple-element.41), channel_id=1, source_target_pairs={{0,6},{1,7},{2,0},{3,1},{4,2},{5,3},{6,4},{7,5},{8,14},{9,15},{10,... | collective-permute-start | bytes 1376264 | tf_op jit(solution)/shard_map/ppermute | solution.py:26
  221.4 5.1 %collective-permute-done.14 = bf16[64,3584]{1,0:T(8,128)(2,1)S(1)} collective-permute-done((bf16[64,3584]{1,0:T(8,128)(2,1)S(1)}, bf16[64,3584]{1,0:T(8,128)(2,1)S(1)}, u32[]{:S(2)}, u32[]{:S(2)}) %collective-permute-start.14) | collective-permute-done | bytes 458784 | tf_op jit(solution)/shard_map/ppermute | solution.py:26
  227.4 13.0 %shard_map.119 = bf16[98,128,128]{2,1,0:T(8,128)(2,1)} custom-call(s32[3,128]{1,0:T(4,128)} %pad_add_fusion.codes_ref, s32[3,128]{1,0:T(4,128)} %pad_add_fusion.1.keys_ref, bf16[128,3584]{1,0:T(8,128)(2,1)} %copy-done.12, bf16[128,3584]{1,0:T(8,128)(2,1)} %collective-permute-done.10.refs_9_.refs_1_, ...), custom_call_target="tpu_custom_call" | custom-call | flops 15032385536 | bytes 7340032 | tf_op jit(solution)/shard_map/pallas_call | solution.py:361
  243.8 5.5 %shard_map.117 = bf16[128,3584]{1,0:T(8,128)(2,1)} custom-call(bf16[128,3584]{1,0:T(8,128)(2,1)} %bitcast.44, f32[1,3584]{1,0:T(1,128)} %gain_ref.3, bf16[64,3584]{1,0:T(8,128)(2,1)} %copy-done.1, bf16[64,3584]{1,0:T(8,128)(2,1)} %copy-done, bf16[64,3584]{1,0:T(8,128)(2,1)} %get-tuple-element.43.refs_2_, bf16[64,3584]{1,0:T(8,128)(2,1)} %copy-done.7, ...), custom_call_target="tpu_custom_call" | custom-call | bytes 3670016 | tf_op jit(solution)/shard_map/pallas_call | solution.py:408
  (139 shorter events, 36.0 us)
Async XLA Ops:
  3.7 37.5 %collective-permute-start.17 = (bf16[64,3584]{1,0:T(8,128)(2,1)}, bf16[64,3584]{1,0:T(8,128)(2,1)S(1)}, u32[]{:S(2)}, u32[]{:S(2)}) collective-permute-start(bf16[64,3584]{1,0:T(8,128)(2,1)} %get-tuple-element.25.refs_0_.refs_8_), channel_id=1, source_target_pairs={{0,6},{1,7},{2,0},{3,1},{4,2},{5,3},{6,4},{7,5},{8,14},{9,15},{10,... | collective-permute-start | bytes 1376264 | tf_op jit(solution)/shard_map/ppermute | solution.py:26
  7.8 35.4 %collective-permute-start.18 = (bf16[64,3584]{1,0:T(8,128)(2,1)}, bf16[64,3584]{1,0:T(8,128)(2,1)S(1)}, u32[]{:S(2)}, u32[]{:S(2)}) collective-permute-start(bf16[64,3584]{1,0:T(8,128)(2,1)} %get-tuple-element.25.refs_0_.refs_8_), channel_id=1, source_target_pairs={{0,2},{1,3},{2,4},{3,5},{4,6},{5,7},{6,0},{7,1},{8,10},{9,11},{10,... | collective-permute-start | bytes 1376264 | tf_op jit(solution)/shard_map/ppermute | solution.py:26
  7.8 42.2 %collective-permute-start.20 = (bf16[64,3584]{1,0:T(8,128)(2,1)}, bf16[64,3584]{1,0:T(8,128)(2,1)}, u32[]{:S(2)}, u32[]{:S(2)}) collective-permute-start(bf16[64,3584]{1,0:T(8,128)(2,1)} %get-tuple-element.25.refs_0_.refs_8_), channel_id=1, source_target_pairs={{0,1},{1,0},{2,3},{3,2},{4,5},{5,4},{6,7},{7,6},{8,9},{9,8},{10,11... | collective-permute-start | bytes 1376264 | tf_op jit(solution)/shard_map/ppermute | solution.py:30
  15.5 25.6 %collective-permute-start.24 = (bf16[64,3584]{1,0:T(8,128)(2,1)S(1)}, bf16[64,3584]{1,0:T(8,128)(2,1)S(1)}, u32[]{:S(2)}, u32[]{:S(2)}) collective-permute-start(bf16[64,3584]{1,0:T(8,128)(2,1)S(1)} %collective-permute-done.1.refs_1_), channel_id=1, source_target_pairs={{0,1},{1,0},{2,3},{3,2},{4,5},{5,4},{6,7},{7,6},{8,9},{9,8},{10,11... | collective-permute-start | bytes 1376264 | tf_op jit(solution)/shard_map/ppermute | solution.py:30
  20.4 29.0 %collective-permute-start.9 = (bf16[64,3584]{1,0:T(8,128)(2,1)S(1)}, bf16[64,3584]{1,0:T(8,128)(2,1)S(1)}, u32[]{:S(2)}, u32[]{:S(2)}) collective-permute-start(bf16[64,3584]{1,0:T(8,128)(2,1)S(1)} %collective-permute-done.refs_0_), channel_id=1, source_target_pairs={{0,1},{1,0},{2,3},{3,2},{4,5},{5,4},{6,7},{7,6},{8,9},{9,8},{10,11... | collective-permute-start | bytes 1376264 | tf_op jit(solution)/shard_map/ppermute | solution.py:30
  41.1 33.6 %collective-permute-start.26 = (bf16[128,3584]{1,0:T(8,128)(2,1)S(1)}, bf16[128,3584]{1,0:T(8,128)(2,1)S(1)}, u32[]{:S(2)}, u32[]{:S(2)}) collective-permute-start(bf16[128,3584]{1,0:T(8,128)(2,1)S(1)} %constant_dynamic-update-slice_fusion.2.refs_8_.refs_4_), channel_id=1, source_target_pairs={{0,2},{1,3},{2,4},{3,5},{4,6},{5,7},{6,0},{7,1},{8,10},{9,11},{10,... | collective-permute-start | bytes 2752520 | tf_op jit(solution)/shard_map/ppermute | solution.py:26
  41.3 30.5 %collective-permute-start.3 = (bf16[64,3584]{1,0:T(8,128)(2,1)S(1)}, bf16[64,3584]{1,0:T(8,128)(2,1)}, u32[]{:S(2)}, u32[]{:S(2)}) collective-permute-start(bf16[64,3584]{1,0:T(8,128)(2,1)S(1)} %copy-done.19), channel_id=1, source_target_pairs={{0,2},{1,3},{2,4},{3,5},{4,6},{5,7},{6,0},{7,1},{8,10},{9,11},{10,... | collective-permute-start | bytes 1376264 | tf_op jit(solution)/shard_map/ppermute | solution.py:26
  43.2 31.8 %collective-permute-start.19 = (bf16[64,3584]{1,0:T(8,128)(2,1)S(1)}, bf16[64,3584]{1,0:T(8,128)(2,1)S(1)}, u32[]{:S(2)}, u32[]{:S(2)}) collective-permute-start(bf16[64,3584]{1,0:T(8,128)(2,1)S(1)} %collective-permute-done.17.refs_1_.refs_9_), channel_id=1, source_target_pairs={{0,6},{1,7},{2,0},{3,1},{4,2},{5,3},{6,4},{7,5},{8,14},{9,15},{10,... | collective-permute-start | bytes 1376264 | tf_op jit(solution)/shard_map/ppermute | solution.py:26
  49.5 26.1 %collective-permute-start.21 = (bf16[64,3584]{1,0:T(8,128)(2,1)S(1)}, bf16[64,3584]{1,0:T(8,128)(2,1)S(1)}, u32[]{:S(2)}, u32[]{:S(2)}) collective-permute-start(bf16[64,3584]{1,0:T(8,128)(2,1)S(1)} %collective-permute-done.17.refs_1_.refs_9_), channel_id=1, source_target_pairs={{0,1},{1,0},{2,3},{3,2},{4,5},{5,4},{6,7},{7,6},{8,9},{9,8},{10,11... | collective-permute-start | bytes 1376264 | tf_op jit(solution)/shard_map/ppermute | solution.py:30
  50.0 45.9 %collective-permute-start.25 = (bf16[128,3584]{1,0:T(8,128)(2,1)S(1)}, bf16[128,3584]{1,0:T(8,128)(2,1)S(1)}, u32[]{:S(2)}, u32[]{:S(2)}) collective-permute-start(bf16[128,3584]{1,0:T(8,128)(2,1)S(1)} %constant_dynamic-update-slice_fusion.2.refs_8_.refs_4_), channel_id=1, source_target_pairs={{0,6},{1,7},{2,0},{3,1},{4,2},{5,3},{6,4},{7,5},{8,14},{9,15},{10,... | collective-permute-start | bytes 2752520 | tf_op jit(solution)/shard_map/ppermute | solution.py:26
  71.8 24.1 %collective-permute-start.10 = (bf16[128,3584]{1,0:T(8,128)(2,1)S(1)}, bf16[128,3584]{1,0:T(8,128)(2,1)}, u32[]{:S(2)}, u32[]{:S(2)}) collective-permute-start(bf16[128,3584]{1,0:T(8,128)(2,1)S(1)} %constant_dynamic-update-slice_fusion.refs_8_.refs_0_), channel_id=1, source_target_pairs={{0,6},{1,7},{2,0},{3,1},{4,2},{5,3},{6,4},{7,5},{8,14},{9,15},{10,... | collective-permute-start | bytes 2752520 | tf_op jit(solution)/shard_map/ppermute | solution.py:26
  74.7 23.0 %collective-permute-start.27 = (bf16[128,3584]{1,0:T(8,128)(2,1)S(1)}, bf16[128,3584]{1,0:T(8,128)(2,1)S(1)}, u32[]{:S(2)}, u32[]{:S(2)}) collective-permute-start(bf16[128,3584]{1,0:T(8,128)(2,1)S(1)} %collective-permute-done.26.refs_10_.refs_6_), channel_id=1, source_target_pairs={{0,2},{1,3},{2,4},{3,5},{4,6},{5,7},{6,0},{7,1},{8,10},{9,11},{10,... | collective-permute-start | bytes 2752520 | tf_op jit(solution)/shard_map/ppermute | solution.py:26
  87.2 32.8 %collective-permute-start.2 = (bf16[64,3584]{1,0:T(8,128)(2,1)S(1)}, bf16[64,3584]{1,0:T(8,128)(2,1)}, u32[]{:S(2)}, u32[]{:S(2)}) collective-permute-start(bf16[64,3584]{1,0:T(8,128)(2,1)S(1)} %copy-done.19), channel_id=1, source_target_pairs={{0,6},{1,7},{2,0},{3,1},{4,2},{5,3},{6,4},{7,5},{8,14},{9,15},{10,... | collective-permute-start | bytes 1376264 | tf_op jit(solution)/shard_map/ppermute | solution.py:26
  95.5 26.0 %collective-permute-start.5 = (bf16[64,3584]{1,0:T(8,128)(2,1)S(1)}, bf16[64,3584]{1,0:T(8,128)(2,1)}, u32[]{:S(2)}, u32[]{:S(2)}) collective-permute-start(bf16[64,3584]{1,0:T(8,128)(2,1)S(1)} %copy-done.19), channel_id=1, source_target_pairs={{0,1},{1,0},{2,3},{3,2},{4,5},{5,4},{6,7},{7,6},{8,9},{9,8},{10,11... | collective-permute-start | bytes 1376264 | tf_op jit(solution)/shard_map/ppermute | solution.py:30
  95.9 26.1 %collective-permute-start.4 = (bf16[64,3584]{1,0:T(8,128)(2,1)}, bf16[64,3584]{1,0:T(8,128)(2,1)}, u32[]{:S(2)}, u32[]{:S(2)}) collective-permute-start(bf16[64,3584]{1,0:T(8,128)(2,1)} %collective-permute-done.3.refs_2_), channel_id=1, source_target_pairs={{0,2},{1,3},{2,4},{3,5},{4,6},{5,7},{6,0},{7,1},{8,10},{9,11},{10,... | collective-permute-start | bytes 1376264 | tf_op jit(solution)/shard_map/ppermute | solution.py:26
  95.9 48.9 %collective-permute-start.11 = (bf16[128,3584]{1,0:T(8,128)(2,1)S(1)}, bf16[128,3584]{1,0:T(8,128)(2,1)}, u32[]{:S(2)}, u32[]{:S(2)}) collective-permute-start(bf16[128,3584]{1,0:T(8,128)(2,1)S(1)} %constant_dynamic-update-slice_fusion.refs_8_.refs_0_), channel_id=1, source_target_pairs={{0,2},{1,3},{2,4},{3,5},{4,6},{5,7},{6,0},{7,1},{8,10},{9,11},{10,... | collective-permute-start | bytes 2752520 | tf_op jit(solution)/shard_map/ppermute | solution.py:26
  98.7 46.1 %collective-permute-start.12 = (bf16[128,3584]{1,0:T(8,128)(2,1)}, bf16[128,3584]{1,0:T(8,128)(2,1)}, u32[]{:S(2)}, u32[]{:S(2)}) collective-permute-start(bf16[128,3584]{1,0:T(8,128)(2,1)} %collective-permute-done.10.refs_9_.refs_1_), channel_id=1, source_target_pairs={{0,6},{1,7},{2,0},{3,1},{4,2},{5,3},{6,4},{7,5},{8,14},{9,15},{10,... | collective-permute-start | bytes 2752520 | tf_op jit(solution)/shard_map/ppermute | solution.py:26
  122.0 22.7 %collective-permute-start.8 = (bf16[64,3584]{1,0:T(8,128)(2,1)}, bf16[64,3584]{1,0:T(8,128)(2,1)S(1)}, u32[]{:S(2)}, u32[]{:S(2)}) collective-permute-start(bf16[64,3584]{1,0:T(8,128)(2,1)} %collective-permute-done.4.refs_3_), channel_id=1, source_target_pairs={{0,1},{1,0},{2,3},{3,2},{4,5},{5,4},{6,7},{7,6},{8,9},{9,8},{10,11... | collective-permute-start | bytes 1376264 | tf_op jit(solution)/shard_map/ppermute | solution.py:30
  135.9 58.0 %collective-permute-start.28 = (bf16[128,3584]{1,0:T(8,128)(2,1)}, bf16[128,3584]{1,0:T(8,128)(2,1)}, u32[]{:S(2)}, u32[]{:S(2)}) collective-permute-start(bf16[128,3584]{1,0:T(8,128)(2,1)} %get-tuple-element.29), channel_id=1, source_target_pairs={{0,6},{1,7},{2,0},{3,1},{4,2},{5,3},{6,4},{7,5},{8,14},{9,15},{10,... | collective-permute-start | bytes 2752520 | tf_op jit(solution)/shard_map/ppermute | solution.py:26
  139.9 76.9 %collective-permute-start.30 = (bf16[128,3584]{1,0:T(8,128)(2,1)}, bf16[128,3584]{1,0:T(8,128)(2,1)S(1)}, u32[]{:S(2)}, u32[]{:S(2)}) collective-permute-start(bf16[128,3584]{1,0:T(8,128)(2,1)} %get-tuple-element.30), channel_id=1, source_target_pairs={{0,2},{1,3},{2,4},{3,5},{4,6},{5,7},{6,0},{7,1},{8,10},{9,11},{10,... | collective-permute-start | bytes 2752520 | tf_op jit(solution)/shard_map/ppermute | solution.py:26
  177.5 38.0 %collective-permute-start.13 = (bf16[256,3584]{1,0:T(8,128)(2,1)}, bf16[256,3584]{1,0:T(8,128)(2,1)S(1)}, u32[]{:S(2)}, u32[]{:S(2)}) collective-permute-start(bf16[256,3584]{1,0:T(8,128)(2,1)} %get-tuple-element.21), channel_id=1, source_target_pairs={{0,1},{1,0},{2,3},{3,2},{4,5},{5,4},{6,7},{7,6},{8,9},{9,8},{10,11... | collective-permute-start | bytes 5505032 | tf_op jit(solution)/shard_map/ppermute | solution.py:30
  195.5 21.3 %collective-permute-start.29 = (bf16[128,3584]{1,0:T(8,128)(2,1)S(1)}, bf16[128,3584]{1,0:T(8,128)(2,1)S(1)}, u32[]{:S(2)}, u32[]{:S(2)}) collective-permute-start(bf16[128,3584]{1,0:T(8,128)(2,1)S(1)} %add_convert_fusion), channel_id=1, source_target_pairs={{0,6},{1,7},{2,0},{3,1},{4,2},{5,3},{6,4},{7,5},{8,14},{9,15},{10,... | collective-permute-start | bytes 2752520 | tf_op jit(solution)/shard_map/ppermute | solution.py:26
  217.8 25.1 %collective-permute-start.31 = (bf16[64,3584]{1,0:T(8,128)(2,1)}, bf16[64,3584]{1,0:T(8,128)(2,1)S(1)}, u32[]{:S(2)}, u32[]{:S(2)}) collective-permute-start(bf16[64,3584]{1,0:T(8,128)(2,1)} %add_convert_fusion.1), channel_id=1, source_target_pairs={{0,1},{1,0},{2,3},{3,2},{4,5},{5,4},{6,7},{7,6},{8,9},{9,8},{10,11... | collective-permute-start | bytes 1376264 | tf_op jit(solution)/shard_map/ppermute | solution.py:30
  218.6 24.3 %collective-permute-start.16 = (bf16[64,3584]{1,0:T(8,128)(2,1)}, bf16[64,3584]{1,0:T(8,128)(2,1)}, u32[]{:S(2)}, u32[]{:S(2)}) collective-permute-start(bf16[64,3584]{1,0:T(8,128)(2,1)} %get-tuple-element.41), channel_id=1, source_target_pairs={{0,6},{1,7},{2,0},{3,1},{4,2},{5,3},{6,4},{7,5},{8,14},{9,15},{10,... | collective-permute-start | bytes 1376264 | tf_op jit(solution)/shard_map/ppermute | solution.py:26
  (37 other events, 690.6 us)

commit v2 on v1

v2 whole, which is shorter than its diff:
```python
import functools

import jax
import jax.numpy as jnp
from jax import lax
from jax.experimental import pallas as pl
from jax.experimental.pallas import tpu as pltpu
from jax.sharding import PartitionSpec as P

FF = 14336
EPS = 1e-05
GELU_C = 0.7978845608028654
F32 = jnp.float32
BF16 = jnp.bfloat16
SIDE = 128
PAIR = 2
TREE = (
    (0, "y", "-"),
    (0, "+", "+"),
    (0, "-", "y"),
    (2, "+", "y"),
    (1, "-", "-"),
    (1, "+", "y"),
    (5, "-", "y"),
)
PIECES = 4
BACK = {"y": "y", "+": "-", "-": "+"}
ANY = pl.BlockSpec(memory_space=pl.ANY)
VMEM = pl.BlockSpec(memory_space=pltpu.VMEM)
SMEM = pl.BlockSpec(memory_space=pltpu.SMEM)
ROOM = 60 * 1024 * 1024
SMALL = pl.CostEstimate(flops=1024, bytes_accessed=1024, transcendentals=0)


def along(value, paths):
    sections, count = lax.axis_size("section"), lax.axis_size("tp")
    pairs = []
    for section in range(sections):
        for i in range(count):
            target = i
            for link in paths[section % 2]:
                target = target ^ 1 if link == "y" else (target + (2 if link == "+" else -2)) % count
            pairs.append((section * count + i, section * count + target))
    return lax.ppermute(value, ("section", "tp"), pairs)


def after(value, *earlier):
    return lax.optimization_barrier((value, *earlier))[0]


def from_next_section(value):
    count = lax.axis_size("section")
    return lax.ppermute(value, "section", [(i, (i - 1) % count) for i in range(count)])


def spread(pieces, steps, *earlier):
    for i in steps:
        parent, *links = TREE[i - 1]
        value = after(pieces[parent], *earlier) if earlier else pieces[parent]
        pieces[i] = along(value, links)


def returned(value, piece, until=0):
    paths = ["", ""]
    while piece != until:
        piece, *links = TREE[piece - 1]
        paths = [path + BACK[link] for path, link in zip(paths, links, strict=True)]
    return along(value, paths)


def lanes(block):
    return pl.ds(pl.multiple_of(block * SIDE, SIDE), SIDE)


def rounded_up(value, step):
    return -(-value // step) * step


def group_lists(index, count, key_column, width):
    length = index.shape[0]
    key, other = index[:, key_column], index[:, 1 - key_column]
    entry = jnp.arange(length, dtype=jnp.int32)
    live = entry < count
    same = (key[:, None] == key[None, :]) & live[None, :] & (entry[None, :] < entry[:, None])
    rank = jnp.sum(same.astype(jnp.int32), axis=1)
    opens = live & (rank % PAIR == 0)
    before = jnp.sum(((key[None, :] < key[:, None]) & opens[None, :]).astype(jnp.int32), axis=1)
    place = jnp.where(live, before * PAIR + rank, -1)
    at = jnp.arange(width, dtype=jnp.int32)
    empty = length * 32
    code = entry * 32 + other - empty
    codes = empty + jnp.sum(jnp.where(place[:, None] == at[None, :], code[:, None], 0), axis=0)
    keys = jnp.sum(jnp.where(place[:, None] == at[None, :] * PAIR, key[:, None], 0), axis=0)
    return codes, keys


def normed_kernel(inputs_ref, gain_ref, units_ref):
    for start in range(0, units_ref.shape[0], 16):
        at = pl.ds(start, 16)
        value = inputs_ref[at, :].astype(F32)
        rms_inv = lax.rsqrt(jnp.mean(value * value, axis=-1, keepdims=True) + EPS)
        units_ref[at, :] = (value * rms_inv * gain_ref[...]).astype(BF16)


def row_blocks(rows, features):
    return pl.BlockSpec((rows, features), lambda i: (i, 0))


def normed_units(inputs, gain):
    rows, features = inputs.shape
    return pl.pallas_call(
        normed_kernel,
        out_shape=jax.ShapeDtypeStruct((rows, features), BF16),
        grid=(rows // 32,),
        in_specs=[row_blocks(32, features), pl.BlockSpec((1, features), lambda i: (0, 0))],
        out_specs=row_blocks(32, features),
        compiler_params=pltpu.CompilerParams(vmem_limit_bytes=ROOM),
        cost_estimate=SMALL,
    )(inputs, gain)


def run_groups(count, unroll, one):
    whole = count // unroll

    @pl.loop(0, whole)
    def _(i):
        for j in range(unroll):
            one(i * unroll + j)

    for s in range(whole * unroll, count):
        one(s)


def start_tiles(tiles_ref, held, sem):
    count = tiles_ref.shape[0]
    copy = pltpu.make_async_copy(tiles_ref, held.at[pl.ds(0, count)], sem)
    copy.start()
    held[count] = jnp.zeros(held.shape[1:], BF16)
    return copy


def hidden_kernel(groups, codes_ref, keys_ref, *refs):
    unit_refs, (up_ref, hidden_ref, slope_ref, units, up, pre, sems) = refs[:PIECES], refs[PIECES:]
    rows = units.shape[0] // PIECES
    copies = [start_tiles(up_ref, up, sems.at[PIECES])]
    for i, ref in enumerate(unit_refs):
        copies.append(
            pltpu.make_async_copy(
                ref, units.at[pl.ds(i * rows, rows)], sems.at[i]
            )
        )
        copies[-1].start()
    pre[...] = jnp.zeros_like(pre)
    for copy in copies:
        copy.wait()

    def add(s):
        codes = [codes_ref[0, s * PAIR + i] for i in range(PAIR)]
        left = jnp.concatenate([units[:, lanes(code & 31)] for code in codes], axis=1)
        right = jnp.concatenate([up[code >> 5] for code in codes], axis=0)
        pre[:, lanes(keys_ref[0, s])] += jnp.dot(left, right, preferred_element_type=F32)

    run_groups(groups, 14, add)

    @pl.loop(0, pre.shape[0] // 32)
    def _(i):
        at = pl.ds(pl.multiple_of(i * 32, 32), 32)
        z = pre[at, :]
        square = z * z
        inner = jnp.tanh(GELU_C * (z + 0.044715 * square * z))
        hidden_ref[at, :] = (0.5 * z * (1.0 + inner)).astype(BF16)
        slope_ref[at, :] = 0.5 * (1.0 + inner) + 0.5 * z * (1.0 - inner * inner) * GELU_C * (
            1.0 + 3.0 * 0.044715 * square
        )


def hidden_of(codes, keys, units, up_tiles, unit_blocks, groups):
    rows, features = units[0].shape
    tokens, wide = PIECES * rows, unit_blocks * SIDE
    held = (up_tiles.shape[0] + 1,) + up_tiles.shape[1:]
    return pl.pallas_call(
        functools.partial(hidden_kernel, groups),
        out_shape=[
            jax.ShapeDtypeStruct((tokens, wide), BF16),
            jax.ShapeDtypeStruct((tokens, wide), F32),
        ],
        in_specs=[SMEM, SMEM] + [ANY] * (PIECES + 1),
        out_specs=[VMEM, VMEM],
        scratch_shapes=[
            pltpu.VMEM((tokens, features), BF16),
            pltpu.VMEM(held, BF16),
            pltpu.VMEM((tokens, wide), F32),
            pltpu.SemaphoreType.DMA((PIECES + 1,)),
        ],
        compiler_params=pltpu.CompilerParams(vmem_limit_bytes=ROOM),
        cost_estimate=SMALL,
    )(codes, keys, *units, up_tiles)


def pre_grad_kernel(pieces, start, groups, codes_ref, keys_ref, *refs):
    grad_refs, (down_ref, slope_ref, pre_grad_ref) = refs[:pieces], refs[pieces : pieces + 3]
    grads, down, slope, hidden_grad, sems = refs[pieces + 3 :]
    rows = grad_refs[0].shape[0]
    copies = [start_tiles(down_ref, down, sems.at[pieces])]
    for i, ref in enumerate(grad_refs):
        copies.append(
            pltpu.make_async_copy(ref, grads.at[pl.ds(i * rows, rows)], sems.at[i])
        )
        copies[-1].start()
    late = pltpu.make_async_copy(
        slope_ref.at[pl.ds(start, slope.shape[0])], slope, sems.at[pieces + 1]
    )
    late.start()
    hidden_grad[...] = jnp.zeros_like(hidden_grad)
    for copy in copies:
        copy.wait()

    def add(s):
        codes = [codes_ref[1, s * PAIR + i] for i in range(PAIR)]
        left = jnp.concatenate([grads[:, lanes(code & 31)] for code in codes], axis=1)
        right = jnp.concatenate([down[code >> 5] for code in codes], axis=1)
        hidden_grad[:, lanes(keys_ref[1, s])] += lax.dot_general(
            left, right, (((1,), (1,)), ((), ())), preferred_element_type=F32
        )

    run_groups(groups, 14, add)
    late.wait()

    @pl.loop(0, slope.shape[0] // 32)
    def _(i):
        at = pl.ds(pl.multiple_of(i * 32, 32), 32)
        pre_grad_ref[at, :] = (hidden_grad[at, :] * slope[at, :]).astype(BF16)


def pre_grad_of(codes, keys, grads, down_tiles, slope, groups, start=0):
    pieces = len(grads)
    rows, features = grads[0].shape
    tokens, wide = pieces * rows, slope.shape[1]
    held = (down_tiles.shape[0] + 1,) + down_tiles.shape[1:]
    return pl.pallas_call(
        functools.partial(pre_grad_kernel, pieces, start, groups),
        out_shape=jax.ShapeDtypeStruct((tokens, wide), BF16),
        in_specs=[SMEM, SMEM] + [ANY] * (pieces + 2),
        out_specs=VMEM,
        scratch_shapes=[
            pltpu.VMEM((tokens, features), BF16),
            pltpu.VMEM(held, BF16),
            pltpu.VMEM((tokens, wide), F32),
            pltpu.VMEM((tokens, wide), F32),
            pltpu.SemaphoreType.DMA((pieces + 2,)),
        ],
        compiler_params=pltpu.CompilerParams(vmem_limit_bytes=ROOM),
        cost_estimate=SMALL,
    )(codes, keys, *grads, down_tiles, slope)


def unit_grad_kernel(pieces, groups, codes_ref, keys_ref, pre_grad_ref, up_ref, *refs):
    out_refs, (up, total, sem) = refs[:pieces], refs[pieces:]
    rows = out_refs[0].shape[0]
    copy = start_tiles(up_ref, up, sem.at[0])
    total[...] = jnp.zeros_like(total)
    copy.wait()

    def add(s):
        codes = [codes_ref[2, s * PAIR + i] for i in range(PAIR)]
        left = jnp.concatenate([pre_grad_ref[:, lanes(code & 31)] for code in codes], axis=1)
        right = jnp.concatenate([up[code >> 5] for code in codes], axis=1)
        total[:, lanes(keys_ref[2, s])] += lax.dot_general(
            left, right, (((1,), (1,)), ((), ())), preferred_element_type=F32
        )

    run_groups(groups, 21, add)
    for piece, out_ref in enumerate(out_refs):

        @pl.loop(0, rows // 16)
        def _(i):
            step = pl.multiple_of(i * 16, 16)
            out_ref[pl.ds(step, 16), :] = total[pl.ds(piece * rows + step, 16), :].astype(BF16)


def unit_grad_of(codes, keys, pre_grad, up_tiles, rows, features, groups):
    tokens = pre_grad.shape[0]
    pieces = tokens // rows
    held = (up_tiles.shape[0] + 1,) + up_tiles.shape[1:]
    return pl.pallas_call(
        functools.partial(unit_grad_kernel, pieces, groups),
        out_shape=[jax.ShapeDtypeStruct((rows, features), BF16)] * pieces,
        in_specs=[SMEM, SMEM, VMEM, ANY],
        out_specs=[VMEM] * pieces,
        scratch_shapes=[
            pltpu.VMEM(held, BF16),
            pltpu.VMEM((tokens, features), F32),
            pltpu.SemaphoreType.DMA((1,)),
        ],
        compiler_params=pltpu.CompilerParams(vmem_limit_bytes=ROOM),
        cost_estimate=SMALL,
    )(codes, keys, pre_grad, up_tiles)


def up_grad_kernel(parts, groups, codes_ref, keys_ref, *refs):
    pieces = 2 * PIECES
    unit_refs, slope_refs = refs[:pieces], refs[pieces : pieces + parts]
    out_ref, units, slopes, held, sems = refs[pieces + parts :]
    rows, done = unit_refs[0].shape[0], 0
    copies = []
    for i, ref in enumerate(slope_refs):
        size = ref.shape[0]
        copies.append(
            pltpu.make_async_copy(ref, slopes.at[pl.ds(done, size)], sems.at[pieces + i])
        )
        done += size
    for i, ref in enumerate(unit_refs):
        copies.append(
            pltpu.make_async_copy(ref, units.at[pl.ds(i * rows, rows)], sems.at[i])
        )
    for copy in copies:
        copy.start()
    held[...] = jnp.zeros_like(held)
    for copy in copies:
        copy.wait()

    def one(s):
        codes = [codes_ref[0, s * PAIR + i] for i in range(PAIR)]
        left = jnp.concatenate([units[:, lanes(code & 31)] for code in codes], axis=1)
        summed = lax.dot_general(
            left,
            slopes[:, lanes(keys_ref[0, s])],
            (((0,), (0,)), ((), ())),
            preferred_element_type=F32,
        ).astype(BF16)
        for i, code in enumerate(codes):
            held[code >> 5] = summed[i * SIDE : (i + 1) * SIDE]

    run_groups(groups, 14, one)
    copy = pltpu.make_async_copy(held.at[pl.ds(0, out_ref.shape[0])], out_ref, sems.at[0])
    copy.start()
    copy.wait()


def up_grad_of(codes, keys, units, slopes, count, groups):
    pieces = len(units)
    rows, features = units[0].shape
    tokens, wide = pieces * rows, slopes[0].shape[1]
    return pl.pallas_call(
        functools.partial(up_grad_kernel, len(slopes), groups),
        out_shape=jax.ShapeDtypeStruct((count, SIDE, SIDE), BF16),
        in_specs=[SMEM, SMEM] + [ANY] * (pieces + len(slopes)),
        out_specs=ANY,
        scratch_shapes=[
            pltpu.VMEM((tokens, features), BF16),
            pltpu.VMEM((tokens, wide), BF16),
            pltpu.VMEM((count + 1, SIDE, SIDE), BF16),
            pltpu.SemaphoreType.DMA((pieces + len(slopes),)),
        ],
        compiler_params=pltpu.CompilerParams(vmem_limit_bytes=ROOM),
        cost_estimate=SMALL,
    )(codes, keys, *units, *slopes)


def down_grad_kernel(groups, codes_ref, keys_ref, *refs):
    pieces = 2 * PIECES
    grad_refs, hidden_refs = refs[:pieces], refs[pieces : pieces + 2]
    out_ref, grads, hidden, turned, held, sems = refs[pieces + 2 :]
    rows, half = grad_refs[0].shape[0], hidden_refs[0].shape[0]
    copies = []
    for i, ref in enumerate(hidden_refs):
        copies.append(pltpu.make_async_copy(ref, hidden.at[pl.ds(i * half, half)], sems.at[i]))
    late = []
    for i, ref in enumerate(grad_refs):
        late.append(
            pltpu.make_async_copy(ref, grads.at[pl.ds(i * rows, rows)], sems.at[2 + i])
        )
    for copy in copies + late:
        copy.start()
    held[...] = jnp.zeros_like(held)
    for copy in copies:
        copy.wait()

    @pl.loop(0, turned.shape[0])
    def _(c):
        turned[c] = hidden[:, lanes(c)].T

    for copy in late:
        copy.wait()

    def one(s):
        codes = [codes_ref[1, s * PAIR + i] for i in range(PAIR)]
        right = jnp.concatenate([grads[:, lanes(code & 31)] for code in codes], axis=1)
        summed = jnp.dot(turned[keys_ref[1, s]], right, preferred_element_type=F32).astype(BF16)
        for i, code in enumerate(codes):
            held[code >> 5] = summed[:, i * SIDE : (i + 1) * SIDE]

    run_groups(groups, 14, one)
    copy = pltpu.make_async_copy(held.at[pl.ds(0, out_ref.shape[0])], out_ref, sems.at[0])
    copy.start()
    copy.wait()


def down_grad_of(codes, keys, grads, hidden, count, groups):
    pieces = len(grads)
    rows, features = grads[0].shape
    tokens, wide = pieces * rows, hidden[0].shape[1]
    return pl.pallas_call(
        functools.partial(down_grad_kernel, groups),
        out_shape=jax.ShapeDtypeStruct((count, SIDE, SIDE), BF16),
        in_specs=[SMEM, SMEM] + [ANY] * (pieces + 2),
        out_specs=ANY,
        scratch_shapes=[
            pltpu.VMEM((tokens, features), BF16),
            pltpu.VMEM((tokens, wide), BF16),
            pltpu.VMEM((wide // SIDE, SIDE, tokens), BF16),
            pltpu.VMEM((count + 1, SIDE, SIDE), BF16),
            pltpu.SemaphoreType.DMA((2 + pieces,)),
        ],
        compiler_params=pltpu.CompilerParams(vmem_limit_bytes=ROOM),
        cost_estimate=SMALL,
    )(codes, keys, *grads, *hidden)


def input_grad_kernel(inputs_ref, gain_ref, grad_ref, *refs):
    term_refs, out_ref = refs[:-1], refs[-1]
    for start in range(0, out_ref.shape[0], 16):
        here = pl.ds(start, 16)
        value = inputs_ref[here, :].astype(F32)
        rms_inv = lax.rsqrt(jnp.mean(value * value, axis=-1, keepdims=True) + EPS)
        normed = value * rms_inv
        unit_grad = term_refs[0][here, :].astype(F32)
        for ref in term_refs[1:]:
            unit_grad = unit_grad + ref[here, :].astype(F32)
        scaled = unit_grad * gain_ref[...]
        mean = jnp.mean(scaled * normed, axis=-1, keepdims=True)
        result = grad_ref[here, :].astype(F32) + rms_inv * (scaled - normed * mean)
        out_ref[here, :] = result.astype(BF16)


def input_grad_of(inputs, gain, arriving, terms):
    rows, features = inputs.shape
    return pl.pallas_call(
        input_grad_kernel,
        out_shape=jax.ShapeDtypeStruct((rows, features), BF16),
        grid=(rows // 32,),
        in_specs=[row_blocks(32, features), pl.BlockSpec((1, features), lambda i: (0, 0))]
        + [row_blocks(32, features)] * (1 + len(terms)),
        out_specs=row_blocks(32, features),
        compiler_params=pltpu.CompilerParams(vmem_limit_bytes=ROOM),
        cost_estimate=SMALL,
    )(inputs, gain, arriving, *terms)


def body(
    inputs,
    norm_gain,
    incoming_grad,
    up_tiles,
    up_index,
    up_count,
    down_tiles,
    down_index,
    down_count,
):
    up, down = up_tiles[0], down_tiles[0]
    rows, features = inputs.shape[1:]
    count = up.shape[0]
    feature_blocks = features // SIDE
    unit_blocks = FF // lax.axis_size("tp") // SIDE
    by_unit = (count + unit_blocks * (PAIR - 1)) // PAIR
    by_feature = (count + feature_blocks * (PAIR - 1)) // PAIR
    width = rounded_up(PAIR * by_feature, SIDE)

    near, far = range(PIECES), range(PIECES, 2 * PIECES)

    units = {0: normed_units(inputs[0], norm_gain)}
    spread(units, (1, 2, 3))
    arriving = from_next_section(incoming_grad[0])
    lists = [
        group_lists(up_index[0], up_count[0, 0], 1, width),
        group_lists(down_index[0], down_count[0, 0], 0, width),
        group_lists(up_index[0], up_count[0, 0], 0, width),
    ]
    codes = jnp.stack([pair[0] for pair in lists])
    keys = jnp.stack([pair[1] for pair in lists])

    spread(units, (5, 4, 6), units[1], units[2], units[3])
    near_hidden, near_slope = hidden_of(
        codes, keys, [units[i] for i in near], up, unit_blocks, by_unit
    )
    last = (near_slope, units[4], units[5], units[6])
    spread(units, (7,), *last)
    grads = {0: after(arriving, *last)}
    spread(grads, (1, 2, 3))
    far_hidden, far_slope = hidden_of(
        codes, keys, [units[i] for i in far], up, unit_blocks, by_unit
    )
    spread(grads, (5, 4, 6), far_slope, grads[1], grads[2], grads[3])
    near_pre_grad = pre_grad_of(
        after(codes, far_slope), keys, [grads[i] for i in near], down, near_slope, by_unit
    )
    spread(grads, (7,), near_pre_grad)
    parts = unit_grad_of(
        after(codes, grads[4], grads[5], grads[6]), keys, near_pre_grad, up, rows, features, by_feature
    )
    terms = [parts[0]] + [returned(parts[i], i) for i in (1, 2, 3)]
    far_pre_grad = pre_grad_of(
        after(codes, *parts, grads[7]), keys, [grads[i] for i in far], down, far_slope, by_unit
    )
    parts += unit_grad_of(codes, keys, far_pre_grad, up, rows, features, by_feature)
    terms += [returned(after(parts[i], *terms[1:4]), i) for i in (7, 4, 5, 6)]
    pre_grads, hidden = [near_pre_grad, far_pre_grad], [near_hidden, far_hidden]
    up_grad = up_grad_of(
        after(codes, *parts), keys, [units[i] for i in range(2 * PIECES)], pre_grads, count, by_unit
    )
    down_grad = down_grad_of(
        after(codes, up_grad), keys, [grads[i] for i in range(2 * PIECES)], hidden, count, by_unit
    )
    input_grad = input_grad_of(inputs[0], norm_gain, arriving, terms)
    return (input_grad[None], up_grad[None], down_grad[None])


def solution(mesh):
    placed = (
        P("section", "tp", None),
        P("section", None),
        P("section", "tp", None),
        P("section", "tp", None, None),
        P("section", "tp", None),
        P("section", "tp"),
        P("section", "tp", None, None),
        P("section", "tp", None),
        P("section", "tp"),
    )
    return jax.shard_map(
        body,
        mesh=mesh,
        in_specs=placed,
        out_specs=(
            P("section", "tp", None),
            P("section", "tp", None, None),
            P("section", "tp", None, None),
        ),
        check_vma=False,
    )
```

time: 253 us -> 229 us (0.905)
  waiting for transfers between devices: 94.5 us -> 78.2 us
  Pallas kernels: 101 us -> 110 us
  starting transfers between devices: 37.8 us -> 30.5 us
  local copies, waits for them, and re-layouts: 6.49 us -> 0.98 us
  other arithmetic: 6.78 us -> 3.68 us
    ppermute x30 -> x21, waiting for transfers between devices: 88.3 us -> 78.2 us  [along(): return lax.ppermute(value, ('section', 'tp'), pairs)]
    pallas_call x8 -> x10, Pallas kernels: 101 us -> 110 us  [the longest x2 27.4 us: hidden_of(): pl.pallas_call(functools.partial(hidden_kernel, groups), out_shape=[jax.S...]
    ppermute x30 -> x21, starting transfers between devices: 36.8 us -> 30.5 us  [along(): return lax.ppermute(value, ('section', 'tp'), pairs)]
    ppermute x2 -> x1, waiting for transfers between devices: 6.19 us -> 0.01 us  [from_next_section(): lax.ppermute(value, 'section', [(i, (i - 1) % count) for i in range(count)])]
    convert_element_type x4 -> x0, other arithmetic: 4.63 us -> none  [the longest x3 3.68 us: plus(): return (left.astype(F32) + right.astype(F32)).astype(BF16)]
  transfers between devices with their start and end apart: 32 -> 22, of which waited for: 11 -> 9; matrix products, arithmetic and copies ran while one was open for 4% -> 2% of each run, Pallas kernels for 37% -> 44%
where the time goes in v2:
time: 229 us; the launch traced here: 226 us
  Pallas kernels  110 us (48%)
  waiting for transfers between devices  78.2 us (34%)
  starting transfers between devices  30.5 us (13%)
  other arithmetic  3.68 us (2%)
    ppermute x21, waiting for transfers between devices, along(): return lax.ppermute(value, ('section', 'tp'), pairs)  78.2 us
    ppermute x21, starting transfers between devices, along(): return lax.ppermute(value, ('section', 'tp'), pairs)  30.5 us
    pallas_call x2, Pallas kernels, hidden_of(): pl.pallas_call(functools.partial(hidden_kernel, groups), out_shape=[jax.S...  27.4 us
    pallas_call x2, Pallas kernels, unit_grad_of(): pl.pallas_call(functools.partial(unit_grad_kernel, pieces, groups), out_s...  24.2 us
    pallas_call x2, Pallas kernels, pre_grad_of(): pl.pallas_call(functools.partial(pre_grad_kernel, pieces, start, groups),...  20.9 us
    pallas_call x1, Pallas kernels, up_grad_of(): pl.pallas_call(functools.partial(up_grad_kernel, len(slopes), groups), ou...  15.1 us
    pallas_call x1, Pallas kernels, down_grad_of(): pl.pallas_call(functools.partial(down_grad_kernel, groups), out_shape=jax...  12.4 us
    pallas_call x1, Pallas kernels, input_grad_of(): pl.pallas_call(input_grad_kernel, out_shape=jax.ShapeDtypeStruct((rows, f...  6.17 us
  transfers between devices with their start and end apart: 22, of which 9 were waited for; matrix products, arithmetic and copies ran while one was open for 2% of the time, Pallas kernels for 44%

profile of v2, /device:TPU:14, one launch (start us, length us, event | category | flops | bytes accessed | tf_op | source)
XLA Modules:
  0.0 225.5 jit_solution(3143559938026549153)
XLA Ops:
  0.6 3.6 %shard_map.112.refs_0_ = bf16[128,3584]{1,0:T(8,128)(2,1)} custom-call(bf16[128,3584]{1,0:T(8,128)(2,1)} %bitcast.46, f32[1,3584]{1,0:T(1,128)} %gain_ref.3), custom_call_target="tpu_custom_call" | custom-call | flops 1024 | bytes 1024 | tf_op jit(solution)/shard_map/pallas_call | solution.py:111
  4.3 4.0 %collective-permute-start.3 = (bf16[128,3584]{1,0:T(8,128)(2,1)}, bf16[128,3584]{1,0:T(8,128)(2,1)S(1)}, u32[]{:S(2)}, u32[]{:S(2)}) collective-permute-start(bf16[128,3584]{1,0:T(8,128)(2,1)} %shard_map.112.refs_0_), channel_id=1, source_target_pairs={{0,6},{1,7},{2,0},{3,1},{4,2},{5,3},{6,4},{7,5},{8,9},{9,8},{10,11... | collective-permute-start | bytes 2752520 | tf_op jit(solution)/shard_map/ppermute | solution.py:44
  12.4 15.9 %collective-permute-done.3.refs_3_ = bf16[128,3584]{1,0:T(8,128)(2,1)S(1)} collective-permute-done((bf16[128,3584]{1,0:T(8,128)(2,1)}, bf16[128,3584]{1,0:T(8,128)(2,1)S(1)}, u32[]{:S(2)}, u32[]{:S(2)}) %collective-permute-start.3) | collective-permute-done | bytes 917536 | tf_op jit(solution)/shard_map/ppermute | solution.py:44
  29.1 9.7 %collective-permute-done.1.refs_1_ = bf16[128,3584]{1,0:T(8,128)(2,1)S(1)} collective-permute-done((bf16[128,3584]{1,0:T(8,128)(2,1)}, bf16[128,3584]{1,0:T(8,128)(2,1)S(1)}, u32[]{:S(2)}, u32[]{:S(2)}) %collective-permute-start.1) | collective-permute-done | bytes 917536 | tf_op jit(solution)/shard_map/ppermute | solution.py:44
  38.8 3.2 %collective-permute-start.5 = (bf16[128,3584]{1,0:T(8,128)(2,1)S(1)}, bf16[128,3584]{1,0:T(8,128)(2,1)}, u32[]{:S(2)}, u32[]{:S(2)}) collective-permute-start(bf16[128,3584]{1,0:T(8,128)(2,1)S(1)} %collective-permute-done.1.refs_1_), channel_id=1, source_target_pairs={{0,6},{1,7},{2,0},{3,1},{4,2},{5,3},{6,4},{7,5},{8,14},{9,15},{10,... | collective-permute-start | bytes 2752520 | tf_op jit(solution)/shard_map/ppermute | solution.py:44
  43.4 13.8 %shard_map.113 = (bf16[512,1792]{1,0:T(8,128)(2,1)}, f32[512,1792]{1,0:T(8,128)}) custom-call(s32[3,128]{1,0:T(4,128)} %pad_add_fusion.codes_ref, s32[3,128]{1,0:T(4,128)} %pad_add_fusion.1.keys_ref, bf16[128,3584]{1,0:T(8,128)(2,1)} %shard_map.112.refs_0_, bf16[128,3584]{1,0:T(8,128)(2,1)} %copy-done.8, bf16[128,3584]{1,0:T(8,128)(2,1)} %copy-done.7, ...), custom_call_target="tpu_custom_call" | custom-call | flops 1024 | bytes 1024 | tf_op jit(solution)/shard_map/pallas_call | solution.py:181
  57.2 6.1 %collective-permute-done.4.refs_0_.refs_4_ = bf16[128,3584]{1,0:T(8,128)(2,1)} collective-permute-done((bf16[128,3584]{1,0:T(8,128)(2,1)S(1)}, bf16[128,3584]{1,0:T(8,128)(2,1)}, u32[]{:S(2)}, u32[]{:S(2)}) %collective-permute-start.4) | collective-permute-done | bytes 917536 | tf_op jit(solution)/shard_map/ppermute | solution.py:44
  63.3 2.7 %collective-permute-start.8 = (bf16[128,3584]{1,0:T(8,128)(2,1)}, bf16[128,3584]{1,0:T(8,128)(2,1)}, u32[]{:S(2)}, u32[]{:S(2)}) collective-permute-start(bf16[128,3584]{1,0:T(8,128)(2,1)} %collective-permute-done.5.refs_1_.refs_5_), channel_id=1, source_target_pairs={{0,6},{1,7},{2,0},{3,1},{4,2},{5,3},{6,4},{7,5},{8,9},{9,8},{10,11... | collective-permute-start | bytes 2752520 | tf_op jit(solution)/shard_map/ppermute | solution.py:44
  68.5 13.3 %collective-permute-done.8.refs_3_.refs_7_ = bf16[128,3584]{1,0:T(8,128)(2,1)} collective-permute-done((bf16[128,3584]{1,0:T(8,128)(2,1)}, bf16[128,3584]{1,0:T(8,128)(2,1)}, u32[]{:S(2)}, u32[]{:S(2)}) %collective-permute-start.8) | collective-permute-done | bytes 917536 | tf_op jit(solution)/shard_map/ppermute | solution.py:44
  81.7 13.6 %shard_map.114 = (bf16[512,1792]{1,0:T(8,128)(2,1)}, f32[512,1792]{1,0:T(8,128)}) custom-call(s32[3,128]{1,0:T(4,128)} %pad_add_fusion.codes_ref, s32[3,128]{1,0:T(4,128)} %pad_add_fusion.1.keys_ref, bf16[128,3584]{1,0:T(8,128)(2,1)} %collective-permute-done.4.refs_0_.refs_4_, bf16[128,3584]{1,0:T(8,128)(2,1)} %collective-permute-done.5.refs_1_.refs_5_, ...), custom_call_target="tpu_custom_call" | custom-call | flops 1024 | bytes 1024 | tf_op jit(solution)/shard_map/pallas_call | solution.py:181
  95.5 3.8 %collective-permute-start.12 = (bf16[128,3584]{1,0:T(8,128)(2,1)S(1)}, bf16[128,3584]{1,0:T(8,128)(2,1)S(1)}, u32[]{:S(2)}, u32[]{:S(2)}) collective-permute-start(bf16[128,3584]{1,0:T(8,128)(2,1)S(1)} %collective-permute-done.9.refs_1_), channel_id=1, source_target_pairs={{0,6},{1,7},{2,0},{3,1},{4,2},{5,3},{6,4},{7,5},{8,14},{9,15},{10,... | collective-permute-start | bytes 2752520 | tf_op jit(solution)/shard_map/ppermute | solution.py:44
  99.3 10.5 %shard_map.115.pre_grad_ref.refs_8_ = bf16[512,1792]{1,0:T(8,128)(2,1)} custom-call(s32[3,128]{1,0:T(4,128)} %pad_add_fusion.codes_ref, s32[3,128]{1,0:T(4,128)} %pad_add_fusion.1.keys_ref, bf16[128,3584]{1,0:T(8,128)(2,1)} %copy-done, bf16[128,3584]{1,0:T(8,128)(2,1)} %copy-done.2, bf16[128,3584]{1,0:T(8,128)(2,1)} %copy-done.3, ...), custom_call_target="tpu_custom_call" | custom-call | flops 1024 | bytes 1024 | tf_op jit(solution)/shard_map/pallas_call | solution.py:240
  109.7 3.0 %collective-permute-done.12.refs_1_.refs_5_ = bf16[128,3584]{1,0:T(8,128)(2,1)S(1)} collective-permute-done((bf16[128,3584]{1,0:T(8,128)(2,1)S(1)}, bf16[128,3584]{1,0:T(8,128)(2,1)S(1)}, u32[]{:S(2)}, u32[]{:S(2)}) %collective-permute-start.12) | collective-permute-done | bytes 917536 | tf_op jit(solution)/shard_map/ppermute | solution.py:44
  112.7 3.7 %collective-permute-start.17 = (bf16[128,3584]{1,0:T(8,128)(2,1)S(1)}, bf16[128,3584]{1,0:T(8,128)(2,1)S(1)}, u32[]{:S(2)}, u32[]{:S(2)}) collective-permute-start(bf16[128,3584]{1,0:T(8,128)(2,1)S(1)} %collective-permute-done.12.refs_1_.refs_5_), channel_id=1, source_target_pairs={{0,6},{1,7},{2,0},{3,1},{4,2},{5,3},{6,4},{7,5},{8,9},{9,8},{10,11... | collective-permute-start | bytes 2752520 | tf_op jit(solution)/shard_map/ppermute | solution.py:44
  116.4 7.4 %collective-permute-done.13.refs_2_.refs_6_ = bf16[128,3584]{1,0:T(8,128)(2,1)} collective-permute-done((bf16[128,3584]{1,0:T(8,128)(2,1)S(1)}, bf16[128,3584]{1,0:T(8,128)(2,1)}, u32[]{:S(2)}, u32[]{:S(2)}) %collective-permute-start.13) | collective-permute-done | bytes 917536 | tf_op jit(solution)/shard_map/ppermute | solution.py:44
  123.8 12.1 %shard_map.116 = (bf16[128,3584]{1,0:T(8,128)(2,1)}, bf16[128,3584]{1,0:T(8,128)(2,1)}, bf16[128,3584]{1,0:T(8,128)(2,1)}, bf16[128,3584]{1,0:T(8,128)(2,1)}) custom-call(s32[3,128]{1,0:T(4,128)} %pad_add_fusion.codes_ref, s32[3,128]{1,0:T(4,128)} %pad_add_fusion.1.keys_ref, bf16[512,1792]{1,0:T(8,128)(2,1)} %shard_map.115.pre_grad_ref.refs_8_, ...), custom_call_target="tpu_custom_call" | custom-call | flops 1024 | bytes 1024 | tf_op jit(solution)/shard_map/pallas_call | solution.py:285
  139.5 10.5 %shard_map.117.pre_grad_ref.refs_9_ = bf16[512,1792]{1,0:T(8,128)(2,1)} custom-call(s32[3,128]{1,0:T(4,128)} %pad_add_fusion.codes_ref, s32[3,128]{1,0:T(4,128)} %pad_add_fusion.1.keys_ref, bf16[128,3584]{1,0:T(8,128)(2,1)} %collective-permute-done.11.refs_0_.refs_4_, bf16[128,3584]{1,0:T(8,128)(2,1)} %copy-done.4, ...), custom_call_target="tpu_custom_call" | custom-call | flops 1024 | bytes 1024 | tf_op jit(solution)/shard_map/pallas_call | solution.py:240
  150.0 12.1 %shard_map.118 = (bf16[128,3584]{1,0:T(8,128)(2,1)}, bf16[128,3584]{1,0:T(8,128)(2,1)}, bf16[128,3584]{1,0:T(8,128)(2,1)}, bf16[128,3584]{1,0:T(8,128)(2,1)}) custom-call(s32[3,128]{1,0:T(4,128)} %pad_add_fusion.codes_ref, s32[3,128]{1,0:T(4,128)} %pad_add_fusion.1.keys_ref, bf16[512,1792]{1,0:T(8,128)(2,1)} %shard_map.117.pre_grad_ref.refs_9_, ...), custom_call_target="tpu_custom_call" | custom-call | flops 1024 | bytes 1024 | tf_op jit(solution)/shard_map/pallas_call | solution.py:285
  166.0 3.7 %collective-permute-start.18 = (bf16[128,3584]{1,0:T(8,128)(2,1)}, bf16[128,3584]{1,0:T(8,128)(2,1)}, u32[]{:S(2)}, u32[]{:S(2)}) collective-permute-start(bf16[128,3584]{1,0:T(8,128)(2,1)} %get-tuple-element.48), channel_id=1, source_target_pairs={{0,5},{1,4},{2,7},{3,6},{4,1},{5,0},{6,3},{7,2},{8,13},{9,12},{10,... | collective-permute-start | bytes 2752520 | tf_op jit(solution)/shard_map/ppermute | solution.py:44
  169.7 15.1 %shard_map.120 = bf16[98,128,128]{2,1,0:T(8,128)(2,1)} custom-call(s32[3,128]{1,0:T(4,128)} %pad_add_fusion.codes_ref, s32[3,128]{1,0:T(4,128)} %pad_add_fusion.1.keys_ref, bf16[128,3584]{1,0:T(8,128)(2,1)} %shard_map.112.refs_0_, bf16[128,3584]{1,0:T(8,128)(2,1)} %copy-done.8, bf16[128,3584]{1,0:T(8,128)(2,1)} %copy-done.7, bf16[128,3584]{1,0:T(8,128)(2,1)} %copy-done.6, ...), custom_call_target="tpu_custom_call" | custom-call | flops 1024 | bytes 1024 | tf_op jit(solution)/shard_map/pallas_call | solution.py:344
  184.8 12.4 %shard_map.121 = bf16[98,128,128]{2,1,0:T(8,128)(2,1)} custom-call(s32[3,128]{1,0:T(4,128)} %pad_add_fusion.codes_ref, s32[3,128]{1,0:T(4,128)} %pad_add_fusion.1.keys_ref, bf16[128,3584]{1,0:T(8,128)(2,1)} %copy-done, bf16[128,3584]{1,0:T(8,128)(2,1)} %copy-done.2, bf16[128,3584]{1,0:T(8,128)(2,1)} %copy-done.3, bf16[128,3584]{1,0:T(8,128)(2,1)} %copy-done.1, ...), custom_call_target="tpu_custom_call" | custom-call | flops 1024 | bytes 1024 | tf_op jit(solution)/shard_map/pallas_call | solution.py:403
  197.2 9.1 %collective-permute-done.20.refs_6_ = bf16[128,3584]{1,0:T(8,128)(2,1)S(1)} collective-permute-done((bf16[128,3584]{1,0:T(8,128)(2,1)}, bf16[128,3584]{1,0:T(8,128)(2,1)S(1)}, u32[]{:S(2)}, u32[]{:S(2)}) %collective-permute-start.20) | collective-permute-done | bytes 917536 | tf_op jit(solution)/shard_map/ppermute | solution.py:44
  206.3 13.0 %collective-permute-done.18.refs_4_ = bf16[128,3584]{1,0:T(8,128)(2,1)} collective-permute-done((bf16[128,3584]{1,0:T(8,128)(2,1)}, bf16[128,3584]{1,0:T(8,128)(2,1)}, u32[]{:S(2)}, u32[]{:S(2)}) %collective-permute-start.18) | collective-permute-done | bytes 917536 | tf_op jit(solution)/shard_map/ppermute | solution.py:44
  219.3 6.2 %shard_map.119 = bf16[128,3584]{1,0:T(8,128)(2,1)} custom-call(bf16[128,3584]{1,0:T(8,128)(2,1)} %bitcast.47, f32[1,3584]{1,0:T(1,128)} %gain_ref.3, bf16[128,3584]{1,0:T(8,128)(2,1)} %copy-done, bf16[128,3584]{1,0:T(8,128)(2,1)} %get-tuple-element.41.refs_0_, bf16[128,3584]{1,0:T(8,128)(2,1)} %copy-done.9, bf16[128,3584]{1,0:T(8,128)(2,1)} %copy-done.10, ...), custom_call_target="tpu_custom_call" | custom-call | flops 1024 | bytes 1024 | tf_op jit(solution)/shard_map/pallas_call | solution.py:438
  (77 shorter events, 14.8 us)
Async XLA Ops:
  4.3 24.1 %collective-permute-start.3 = (bf16[128,3584]{1,0:T(8,128)(2,1)}, bf16[128,3584]{1,0:T(8,128)(2,1)S(1)}, u32[]{:S(2)}, u32[]{:S(2)}) collective-permute-start(bf16[128,3584]{1,0:T(8,128)(2,1)} %shard_map.112.refs_0_), channel_id=1, source_target_pairs={{0,6},{1,7},{2,0},{3,1},{4,2},{5,3},{6,4},{7,5},{8,9},{9,8},{10,11... | collective-permute-start | bytes 2752520 | tf_op jit(solution)/shard_map/ppermute | solution.py:44
  8.3 20.8 %collective-permute-start.2 = (bf16[128,3584]{1,0:T(8,128)(2,1)}, bf16[128,3584]{1,0:T(8,128)(2,1)S(1)}, u32[]{:S(2)}, u32[]{:S(2)}) collective-permute-start(bf16[128,3584]{1,0:T(8,128)(2,1)} %shard_map.112.refs_0_), channel_id=1, source_target_pairs={{0,2},{1,3},{2,4},{3,5},{4,6},{5,7},{6,0},{7,1},{8,10},{9,11},{10,... | collective-permute-start | bytes 2752520 | tf_op jit(solution)/shard_map/ppermute | solution.py:44
  8.3 30.5 %collective-permute-start.1 = (bf16[128,3584]{1,0:T(8,128)(2,1)}, bf16[128,3584]{1,0:T(8,128)(2,1)S(1)}, u32[]{:S(2)}, u32[]{:S(2)}) collective-permute-start(bf16[128,3584]{1,0:T(8,128)(2,1)} %shard_map.112.refs_0_), channel_id=1, source_target_pairs={{0,1},{1,0},{2,3},{3,2},{4,5},{5,4},{6,7},{7,6},{8,14},{9,15},{10,... | collective-permute-start | bytes 2752520 | tf_op jit(solution)/shard_map/ppermute | solution.py:44
  8.7 54.6 %collective-permute-start = (bf16[128,3584]{1,0:T(8,128)(2,1)}, bf16[128,3584]{1,0:T(8,128)(2,1)S(1)}, u32[]{:S(2)}, u32[]{:S(2)}) collective-permute-start(bf16[128,3584]{1,0:T(8,128)(2,1)} %bitcast.56), channel_id=1, source_target_pairs={{0,120},{8,0},{16,8},{24,16},{32,24},{40,32},{48,40},{56,48},{64,5... | collective-permute-start | bytes 2752520 | tf_op jit(solution)/shard_map/ppermute | solution.py:53
  38.8 24.5 %collective-permute-start.6 = (bf16[128,3584]{1,0:T(8,128)(2,1)S(1)}, bf16[128,3584]{1,0:T(8,128)(2,1)}, u32[]{:S(2)}, u32[]{:S(2)}) collective-permute-start(bf16[128,3584]{1,0:T(8,128)(2,1)S(1)} %collective-permute-done.1.refs_1_), channel_id=1, source_target_pairs={{0,2},{1,3},{2,4},{3,5},{4,6},{5,7},{6,0},{7,1},{8,9},{9,8},{10,11... | collective-permute-start | bytes 2752520 | tf_op jit(solution)/shard_map/ppermute | solution.py:44
  38.8 24.5 %collective-permute-start.5 = (bf16[128,3584]{1,0:T(8,128)(2,1)S(1)}, bf16[128,3584]{1,0:T(8,128)(2,1)}, u32[]{:S(2)}, u32[]{:S(2)}) collective-permute-start(bf16[128,3584]{1,0:T(8,128)(2,1)S(1)} %collective-permute-done.1.refs_1_), channel_id=1, source_target_pairs={{0,6},{1,7},{2,0},{3,1},{4,2},{5,3},{6,4},{7,5},{8,14},{9,15},{10,... | collective-permute-start | bytes 2752520 | tf_op jit(solution)/shard_map/ppermute | solution.py:44
  42.0 21.3 %collective-permute-start.4 = (bf16[128,3584]{1,0:T(8,128)(2,1)S(1)}, bf16[128,3584]{1,0:T(8,128)(2,1)}, u32[]{:S(2)}, u32[]{:S(2)}) collective-permute-start(bf16[128,3584]{1,0:T(8,128)(2,1)S(1)} %collective-permute-done.2.refs_2_), channel_id=1, source_target_pairs={{0,2},{1,3},{2,4},{3,5},{4,6},{5,7},{6,0},{7,1},{8,9},{9,8},{10,11... | collective-permute-start | bytes 2752520 | tf_op jit(solution)/shard_map/ppermute | solution.py:44
  63.3 32.1 %copy-start = (bf16[128,3584]{1,0:T(8,128)(2,1)}, bf16[128,3584]{1,0:T(8,128)(2,1)S(1)}, u32[]{:S(2)}) copy-start(bf16[128,3584]{1,0:T(8,128)(2,1)S(1)} %collective-permute-done.refs_0_.grad_ref) | copy-start | bytes 2752516
  63.3 18.4 %collective-permute-start.8 = (bf16[128,3584]{1,0:T(8,128)(2,1)}, bf16[128,3584]{1,0:T(8,128)(2,1)}, u32[]{:S(2)}, u32[]{:S(2)}) collective-permute-start(bf16[128,3584]{1,0:T(8,128)(2,1)} %collective-permute-done.5.refs_1_.refs_5_), channel_id=1, source_target_pairs={{0,6},{1,7},{2,0},{3,1},{4,2},{5,3},{6,4},{7,5},{8,9},{9,8},{10,11... | collective-permute-start | bytes 2752520 | tf_op jit(solution)/shard_map/ppermute | solution.py:44
  66.0 29.4 %collective-permute-start.10 = (bf16[128,3584]{1,0:T(8,128)(2,1)S(1)}, bf16[128,3584]{1,0:T(8,128)(2,1)S(1)}, u32[]{:S(2)}, u32[]{:S(2)}) collective-permute-start(bf16[128,3584]{1,0:T(8,128)(2,1)S(1)} %collective-permute-done.refs_0_.grad_ref), channel_id=1, source_target_pairs={{0,6},{1,7},{2,0},{3,1},{4,2},{5,3},{6,4},{7,5},{8,9},{9,8},{10,11... | collective-permute-start | bytes 2752520 | tf_op jit(solution)/shard_map/ppermute | solution.py:44
  66.1 29.3 %collective-permute-start.9 = (bf16[128,3584]{1,0:T(8,128)(2,1)S(1)}, bf16[128,3584]{1,0:T(8,128)(2,1)S(1)}, u32[]{:S(2)}, u32[]{:S(2)}) collective-permute-start(bf16[128,3584]{1,0:T(8,128)(2,1)S(1)} %collective-permute-done.refs_0_.grad_ref), channel_id=1, source_target_pairs={{0,1},{1,0},{2,3},{3,2},{4,5},{5,4},{6,7},{7,6},{8,14},{9,15},{10,... | collective-permute-start | bytes 2752520 | tf_op jit(solution)/shard_map/ppermute | solution.py:44
  66.5 28.9 %collective-permute-start.7 = (bf16[128,3584]{1,0:T(8,128)(2,1)S(1)}, bf16[128,3584]{1,0:T(8,128)(2,1)S(1)}, u32[]{:S(2)}, u32[]{:S(2)}) collective-permute-start(bf16[128,3584]{1,0:T(8,128)(2,1)S(1)} %collective-permute-done.refs_0_.grad_ref), channel_id=1, source_target_pairs={{0,2},{1,3},{2,4},{3,5},{4,6},{5,7},{6,0},{7,1},{8,10},{9,11},{10,... | collective-permute-start | bytes 2752520 | tf_op jit(solution)/shard_map/ppermute | solution.py:44
  95.5 17.2 %collective-permute-start.12 = (bf16[128,3584]{1,0:T(8,128)(2,1)S(1)}, bf16[128,3584]{1,0:T(8,128)(2,1)S(1)}, u32[]{:S(2)}, u32[]{:S(2)}) collective-permute-start(bf16[128,3584]{1,0:T(8,128)(2,1)S(1)} %collective-permute-done.9.refs_1_), channel_id=1, source_target_pairs={{0,6},{1,7},{2,0},{3,1},{4,2},{5,3},{6,4},{7,5},{8,14},{9,15},{10,... | collective-permute-start | bytes 2752520 | tf_op jit(solution)/shard_map/ppermute | solution.py:44
  99.2 17.1 %collective-permute-start.11 = (bf16[128,3584]{1,0:T(8,128)(2,1)S(1)}, bf16[128,3584]{1,0:T(8,128)(2,1)}, u32[]{:S(2)}, u32[]{:S(2)}) collective-permute-start(bf16[128,3584]{1,0:T(8,128)(2,1)S(1)} %collective-permute-done.7.refs_2_), channel_id=1, source_target_pairs={{0,2},{1,3},{2,4},{3,5},{4,6},{5,7},{6,0},{7,1},{8,9},{9,8},{10,11... | collective-permute-start | bytes 2752520 | tf_op jit(solution)/shard_map/ppermute | solution.py:44
  99.2 24.5 %collective-permute-start.13 = (bf16[128,3584]{1,0:T(8,128)(2,1)S(1)}, bf16[128,3584]{1,0:T(8,128)(2,1)}, u32[]{:S(2)}, u32[]{:S(2)}) collective-permute-start(bf16[128,3584]{1,0:T(8,128)(2,1)S(1)} %collective-permute-done.9.refs_1_), channel_id=1, source_target_pairs={{0,2},{1,3},{2,4},{3,5},{4,6},{5,7},{6,0},{7,1},{8,9},{9,8},{10,11... | collective-permute-start | bytes 2752520 | tf_op jit(solution)/shard_map/ppermute | solution.py:44
  112.7 25.9 %copy-start.4 = (bf16[128,3584]{1,0:T(8,128)(2,1)}, bf16[128,3584]{1,0:T(8,128)(2,1)S(1)}, u32[]{:S(2)}) copy-start(bf16[128,3584]{1,0:T(8,128)(2,1)S(1)} %collective-permute-done.12.refs_1_.refs_5_) | copy-start | bytes 2752516
  112.7 25.9 %collective-permute-start.17 = (bf16[128,3584]{1,0:T(8,128)(2,1)S(1)}, bf16[128,3584]{1,0:T(8,128)(2,1)S(1)}, u32[]{:S(2)}, u32[]{:S(2)}) collective-permute-start(bf16[128,3584]{1,0:T(8,128)(2,1)S(1)} %collective-permute-done.12.refs_1_.refs_5_), channel_id=1, source_target_pairs={{0,6},{1,7},{2,0},{3,1},{4,2},{5,3},{6,4},{7,5},{8,9},{9,8},{10,11... | collective-permute-start | bytes 2752520 | tf_op jit(solution)/shard_map/ppermute | solution.py:44
  135.9 26.2 %collective-permute-start.14 = (bf16[128,3584]{1,0:T(8,128)(2,1)}, bf16[128,3584]{1,0:T(8,128)(2,1)S(1)}, u32[]{:S(2)}, u32[]{:S(2)}) collective-permute-start(bf16[128,3584]{1,0:T(8,128)(2,1)} %get-tuple-element.42), channel_id=1, source_target_pairs={{0,1},{1,0},{2,3},{3,2},{4,5},{5,4},{6,7},{7,6},{8,10},{9,11},{10,... | collective-permute-start | bytes 2752520 | tf_op jit(solution)/shard_map/ppermute | solution.py:44
  136.5 25.6 %collective-permute-start.15 = (bf16[128,3584]{1,0:T(8,128)(2,1)}, bf16[128,3584]{1,0:T(8,128)(2,1)S(1)}, u32[]{:S(2)}, u32[]{:S(2)}) collective-permute-start(bf16[128,3584]{1,0:T(8,128)(2,1)} %get-tuple-element.43), channel_id=1, source_target_pairs={{0,6},{1,7},{2,0},{3,1},{4,2},{5,3},{6,4},{7,5},{8,14},{9,15},{10,... | collective-permute-start | bytes 2752520 | tf_op jit(solution)/shard_map/ppermute | solution.py:44
  136.5 25.6 %collective-permute-start.16 = (bf16[128,3584]{1,0:T(8,128)(2,1)}, bf16[128,3584]{1,0:T(8,128)(2,1)}, u32[]{:S(2)}, u32[]{:S(2)}) collective-permute-start(bf16[128,3584]{1,0:T(8,128)(2,1)} %get-tuple-element.44), channel_id=1, source_target_pairs={{0,2},{1,3},{2,4},{3,5},{4,6},{5,7},{6,0},{7,1},{8,9},{9,8},{10,11... | collective-permute-start | bytes 2752520 | tf_op jit(solution)/shard_map/ppermute | solution.py:44
  162.2 35.0 %collective-permute-start.21 = (bf16[128,3584]{1,0:T(8,128)(2,1)}, bf16[128,3584]{1,0:T(8,128)(2,1)S(1)}, u32[]{:S(2)}, u32[]{:S(2)}) collective-permute-start(bf16[128,3584]{1,0:T(8,128)(2,1)} %get-tuple-element.54), channel_id=1, source_target_pairs={{0,7},{1,6},{2,1},{3,0},{4,3},{5,2},{6,5},{7,4},{8,11},{9,10},{10,... | collective-permute-start | bytes 2752520 | tf_op jit(solution)/shard_map/ppermute | solution.py:44
  164.4 41.9 %collective-permute-start.20 = (bf16[128,3584]{1,0:T(8,128)(2,1)}, bf16[128,3584]{1,0:T(8,128)(2,1)S(1)}, u32[]{:S(2)}, u32[]{:S(2)}) collective-permute-start(bf16[128,3584]{1,0:T(8,128)(2,1)} %get-tuple-element.52), channel_id=1, source_target_pairs={{0,3},{1,2},{2,5},{3,4},{4,7},{5,6},{6,1},{7,0},{8,12},{9,13},{10,... | collective-permute-start | bytes 2752520 | tf_op jit(solution)/shard_map/ppermute | solution.py:44
  165.2 41.1 %collective-permute-start.19 = (bf16[128,3584]{1,0:T(8,128)(2,1)}, bf16[128,3584]{1,0:T(8,128)(2,1)}, u32[]{:S(2)}, u32[]{:S(2)}) collective-permute-start(bf16[128,3584]{1,0:T(8,128)(2,1)} %get-tuple-element.50), channel_id=1, source_target_pairs={{0,4},{1,5},{2,6},{3,7},{4,0},{5,1},{6,2},{7,3},{8,15},{9,14},{10,... | collective-permute-start | bytes 2752520 | tf_op jit(solution)/shard_map/ppermute | solution.py:44
  166.0 53.4 %collective-permute-start.18 = (bf16[128,3584]{1,0:T(8,128)(2,1)}, bf16[128,3584]{1,0:T(8,128)(2,1)}, u32[]{:S(2)}, u32[]{:S(2)}) collective-permute-start(bf16[128,3584]{1,0:T(8,128)(2,1)} %get-tuple-element.48), channel_id=1, source_target_pairs={{0,5},{1,4},{2,7},{3,6},{4,1},{5,0},{6,3},{7,2},{8,13},{9,12},{10,... | collective-permute-start | bytes 2752520 | tf_op jit(solution)/shard_map/ppermute | solution.py:44
  (11 other events, 126.8 us)

commit v3 on v2

--- a/solution.py
+++ b/solution.py
@@ -497,9 +497,9 @@
     )
     spread(grads, (7,), near_pre_grad)
     parts = unit_grad_of(
-        after(codes, grads[4], grads[5], grads[6]), keys, near_pre_grad, up, rows, features, by_feature
-    )
-    terms = [parts[0]] + [returned(parts[i], i) for i in (1, 2, 3)]
+        after(codes, grads[4], grads[5]), keys, near_pre_grad, up, rows, features, by_feature
+    )
+    terms = [parts[0]] + [returned(after(parts[i], grads[6]), i) for i in (1, 2, 3)]
     far_pre_grad = pre_grad_of(
         after(codes, *parts, grads[7]), keys, [grads[i] for i in far], down, far_slope, by_unit
     )

time: 229 us -> 221 us (0.965)
  waiting for transfers between devices: 78.2 us -> 72.8 us
    ppermute x21, waiting for transfers between devices: 78.2 us -> 72.8 us  [along(): return lax.ppermute(value, ('section', 'tp'), pairs)]
  transfers between devices with their start and end apart: 22 -> 22, of which waited for: 9 -> 10; matrix products, arithmetic and copies ran while one was open for 2% -> 2% of each run, Pallas kernels for 44% -> 46%
where the time goes in v3:
time: 221 us; the launch traced here: 219 us
  Pallas kernels  110 us (50%)
  waiting for transfers between devices  72.8 us (33%)
  starting transfers between devices  29.6 us (13%)
  other arithmetic  3.72 us (2%)
  between operations  2.27 us (1%)
    ppermute x21, waiting for transfers between devices, along(): return lax.ppermute(value, ('section', 'tp'), pairs)  72.8 us
    ppermute x21, starting transfers between devices, along(): return lax.ppermute(value, ('section', 'tp'), pairs)  29.6 us
    pallas_call x2, Pallas kernels, hidden_of(): pl.pallas_call(functools.partial(hidden_kernel, groups), out_shape=[jax.S...  27.5 us
    pallas_call x2, Pallas kernels, unit_grad_of(): pl.pallas_call(functools.partial(unit_grad_kernel, pieces, groups), out_s...  24.1 us
    pallas_call x2, Pallas kernels, pre_grad_of(): pl.pallas_call(functools.partial(pre_grad_kernel, pieces, start, groups),...  20.9 us
    pallas_call x1, Pallas kernels, up_grad_of(): pl.pallas_call(functools.partial(up_grad_kernel, len(slopes), groups), ou...  15.2 us
    pallas_call x1, Pallas kernels, down_grad_of(): pl.pallas_call(functools.partial(down_grad_kernel, groups), out_shape=jax...  12.3 us
    pallas_call x1, Pallas kernels, input_grad_of(): pl.pallas_call(input_grad_kernel, out_shape=jax.ShapeDtypeStruct((rows, f...  6.17 us
  transfers between devices with their start and end apart: 22, of which 10 were waited for; matrix products, arithmetic and copies ran while one was open for 2% of the time, Pallas kernels for 46%

profile of v3, /device:TPU:14, one launch (start us, length us, event | category | flops | bytes accessed | tf_op | source)
XLA Modules:
  0.0 219.2 jit_solution(5487696862072177568)
XLA Ops:
  0.6 3.6 %shard_map.112.refs_0_ = bf16[128,3584]{1,0:T(8,128)(2,1)} custom-call(bf16[128,3584]{1,0:T(8,128)(2,1)} %bitcast.46, f32[1,3584]{1,0:T(1,128)} %gain_ref.3), custom_call_target="tpu_custom_call" | custom-call | flops 1024 | bytes 1024 | tf_op jit(solution)/shard_map/pallas_call | solution.py:111
  4.3 4.0 %collective-permute-start.3 = (bf16[128,3584]{1,0:T(8,128)(2,1)}, bf16[128,3584]{1,0:T(8,128)(2,1)S(1)}, u32[]{:S(2)}, u32[]{:S(2)}) collective-permute-start(bf16[128,3584]{1,0:T(8,128)(2,1)} %shard_map.112.refs_0_), channel_id=1, source_target_pairs={{0,6},{1,7},{2,0},{3,1},{4,2},{5,3},{6,4},{7,5},{8,9},{9,8},{10,11... | collective-permute-start | bytes 2752520 | tf_op jit(solution)/shard_map/ppermute | solution.py:44
  12.5 15.9 %collective-permute-done.3.refs_3_ = bf16[128,3584]{1,0:T(8,128)(2,1)S(1)} collective-permute-done((bf16[128,3584]{1,0:T(8,128)(2,1)}, bf16[128,3584]{1,0:T(8,128)(2,1)S(1)}, u32[]{:S(2)}, u32[]{:S(2)}) %collective-permute-start.3) | collective-permute-done | bytes 917536 | tf_op jit(solution)/shard_map/ppermute | solution.py:44
  29.1 9.7 %collective-permute-done.1.refs_1_ = bf16[128,3584]{1,0:T(8,128)(2,1)S(1)} collective-permute-done((bf16[128,3584]{1,0:T(8,128)(2,1)}, bf16[128,3584]{1,0:T(8,128)(2,1)S(1)}, u32[]{:S(2)}, u32[]{:S(2)}) %collective-permute-start.1) | collective-permute-done | bytes 917536 | tf_op jit(solution)/shard_map/ppermute | solution.py:44
  38.8 3.2 %collective-permute-start.5 = (bf16[128,3584]{1,0:T(8,128)(2,1)S(1)}, bf16[128,3584]{1,0:T(8,128)(2,1)}, u32[]{:S(2)}, u32[]{:S(2)}) collective-permute-start(bf16[128,3584]{1,0:T(8,128)(2,1)S(1)} %collective-permute-done.1.refs_1_), channel_id=1, source_target_pairs={{0,6},{1,7},{2,0},{3,1},{4,2},{5,3},{6,4},{7,5},{8,14},{9,15},{10,... | collective-permute-start | bytes 2752520 | tf_op jit(solution)/shard_map/ppermute | solution.py:44
  43.4 13.8 %shard_map.113 = (bf16[512,1792]{1,0:T(8,128)(2,1)}, f32[512,1792]{1,0:T(8,128)}) custom-call(s32[3,128]{1,0:T(4,128)} %pad_add_fusion.codes_ref, s32[3,128]{1,0:T(4,128)} %pad_add_fusion.1.keys_ref, bf16[128,3584]{1,0:T(8,128)(2,1)} %shard_map.112.refs_0_, bf16[128,3584]{1,0:T(8,128)(2,1)} %copy-done.8, bf16[128,3584]{1,0:T(8,128)(2,1)} %copy-done.7, ...), custom_call_target="tpu_custom_call" | custom-call | flops 1024 | bytes 1024 | tf_op jit(solution)/shard_map/pallas_call | solution.py:181
  57.2 6.1 %collective-permute-done.4.refs_0_.refs_4_ = bf16[128,3584]{1,0:T(8,128)(2,1)} collective-permute-done((bf16[128,3584]{1,0:T(8,128)(2,1)S(1)}, bf16[128,3584]{1,0:T(8,128)(2,1)}, u32[]{:S(2)}, u32[]{:S(2)}) %collective-permute-start.4) | collective-permute-done | bytes 917536 | tf_op jit(solution)/shard_map/ppermute | solution.py:44
  63.3 2.7 %collective-permute-start.8 = (bf16[128,3584]{1,0:T(8,128)(2,1)}, bf16[128,3584]{1,0:T(8,128)(2,1)}, u32[]{:S(2)}, u32[]{:S(2)}) collective-permute-start(bf16[128,3584]{1,0:T(8,128)(2,1)} %collective-permute-done.5.refs_1_.refs_5_), channel_id=1, source_target_pairs={{0,6},{1,7},{2,0},{3,1},{4,2},{5,3},{6,4},{7,5},{8,9},{9,8},{10,11... | collective-permute-start | bytes 2752520 | tf_op jit(solution)/shard_map/ppermute | solution.py:44
  68.5 13.3 %collective-permute-done.8.refs_3_.refs_7_ = bf16[128,3584]{1,0:T(8,128)(2,1)} collective-permute-done((bf16[128,3584]{1,0:T(8,128)(2,1)}, bf16[128,3584]{1,0:T(8,128)(2,1)}, u32[]{:S(2)}, u32[]{:S(2)}) %collective-permute-start.8) | collective-permute-done | bytes 917536 | tf_op jit(solution)/shard_map/ppermute | solution.py:44
  81.8 13.7 %shard_map.114 = (bf16[512,1792]{1,0:T(8,128)(2,1)}, f32[512,1792]{1,0:T(8,128)}) custom-call(s32[3,128]{1,0:T(4,128)} %pad_add_fusion.codes_ref, s32[3,128]{1,0:T(4,128)} %pad_add_fusion.1.keys_ref, bf16[128,3584]{1,0:T(8,128)(2,1)} %collective-permute-done.4.refs_0_.refs_4_, bf16[128,3584]{1,0:T(8,128)(2,1)} %collective-permute-done.5.refs_1_.refs_5_, ...), custom_call_target="tpu_custom_call" | custom-call | flops 1024 | bytes 1024 | tf_op jit(solution)/shard_map/pallas_call | solution.py:181
  95.6 3.8 %collective-permute-start.12 = (bf16[128,3584]{1,0:T(8,128)(2,1)S(1)}, bf16[128,3584]{1,0:T(8,128)(2,1)S(1)}, u32[]{:S(2)}, u32[]{:S(2)}) collective-permute-start(bf16[128,3584]{1,0:T(8,128)(2,1)S(1)} %collective-permute-done.9.refs_1_), channel_id=1, source_target_pairs={{0,6},{1,7},{2,0},{3,1},{4,2},{5,3},{6,4},{7,5},{8,14},{9,15},{10,... | collective-permute-start | bytes 2752520 | tf_op jit(solution)/shard_map/ppermute | solution.py:44
  99.4 10.5 %shard_map.115.pre_grad_ref.refs_8_ = bf16[512,1792]{1,0:T(8,128)(2,1)} custom-call(s32[3,128]{1,0:T(4,128)} %pad_add_fusion.codes_ref, s32[3,128]{1,0:T(4,128)} %pad_add_fusion.1.keys_ref, bf16[128,3584]{1,0:T(8,128)(2,1)} %copy-done, bf16[128,3584]{1,0:T(8,128)(2,1)} %copy-done.2, bf16[128,3584]{1,0:T(8,128)(2,1)} %copy-done.3, ...), custom_call_target="tpu_custom_call" | custom-call | flops 1024 | bytes 1024 | tf_op jit(solution)/shard_map/pallas_call | solution.py:240
  109.9 2.8 %collective-permute-done.12.refs_1_.refs_5_ = bf16[128,3584]{1,0:T(8,128)(2,1)S(1)} collective-permute-done((bf16[128,3584]{1,0:T(8,128)(2,1)S(1)}, bf16[128,3584]{1,0:T(8,128)(2,1)S(1)}, u32[]{:S(2)}, u32[]{:S(2)}) %collective-permute-start.12) | collective-permute-done | bytes 917536 | tf_op jit(solution)/shard_map/ppermute | solution.py:44
  114.1 2.3 %collective-permute-start.17 = (bf16[128,3584]{1,0:T(8,128)(2,1)S(1)}, bf16[128,3584]{1,0:T(8,128)(2,1)S(1)}, u32[]{:S(2)}, u32[]{:S(2)}) collective-permute-start(bf16[128,3584]{1,0:T(8,128)(2,1)S(1)} %collective-permute-done.12.refs_1_.refs_5_), channel_id=1, source_target_pairs={{0,6},{1,7},{2,0},{3,1},{4,2},{5,3},{6,4},{7,5},{8,9},{9,8},{10,11... | collective-permute-start | bytes 2752520 | tf_op jit(solution)/shard_map/ppermute | solution.py:44
  116.4 12.0 %shard_map.116 = (bf16[128,3584]{1,0:T(8,128)(2,1)}, bf16[128,3584]{1,0:T(8,128)(2,1)}, bf16[128,3584]{1,0:T(8,128)(2,1)}, bf16[128,3584]{1,0:T(8,128)(2,1)}) custom-call(s32[3,128]{1,0:T(4,128)} %pad_add_fusion.codes_ref, s32[3,128]{1,0:T(4,128)} %pad_add_fusion.1.keys_ref, bf16[512,1792]{1,0:T(8,128)(2,1)} %shard_map.115.pre_grad_ref.refs_8_, ...), custom_call_target="tpu_custom_call" | custom-call | flops 1024 | bytes 1024 | tf_op jit(solution)/shard_map/pallas_call | solution.py:285
  128.5 3.2 %collective-permute-start.15 = (bf16[128,3584]{1,0:T(8,128)(2,1)}, bf16[128,3584]{1,0:T(8,128)(2,1)S(1)}, u32[]{:S(2)}, u32[]{:S(2)}) collective-permute-start(bf16[128,3584]{1,0:T(8,128)(2,1)} %get-tuple-element.48), channel_id=1, source_target_pairs={{0,6},{1,7},{2,0},{3,1},{4,2},{5,3},{6,4},{7,5},{8,14},{9,15},{10,... | collective-permute-start | bytes 2752520 | tf_op jit(solution)/shard_map/ppermute | solution.py:44
  133.9 10.4 %shard_map.117.pre_grad_ref.refs_9_ = bf16[512,1792]{1,0:T(8,128)(2,1)} custom-call(s32[3,128]{1,0:T(4,128)} %pad_add_fusion.codes_ref, s32[3,128]{1,0:T(4,128)} %pad_add_fusion.1.keys_ref, bf16[128,3584]{1,0:T(8,128)(2,1)} %collective-permute-done.11.refs_0_.refs_4_, bf16[128,3584]{1,0:T(8,128)(2,1)} %copy-done.4, ...), custom_call_target="tpu_custom_call" | custom-call | flops 1024 | bytes 1024 | tf_op jit(solution)/shard_map/pallas_call | solution.py:240
  144.4 12.0 %shard_map.118 = (bf16[128,3584]{1,0:T(8,128)(2,1)}, bf16[128,3584]{1,0:T(8,128)(2,1)}, bf16[128,3584]{1,0:T(8,128)(2,1)}, bf16[128,3584]{1,0:T(8,128)(2,1)}) custom-call(s32[3,128]{1,0:T(4,128)} %pad_add_fusion.codes_ref, s32[3,128]{1,0:T(4,128)} %pad_add_fusion.1.keys_ref, bf16[512,1792]{1,0:T(8,128)(2,1)} %shard_map.117.pre_grad_ref.refs_9_, ...), custom_call_target="tpu_custom_call" | custom-call | flops 1024 | bytes 1024 | tf_op jit(solution)/shard_map/pallas_call | solution.py:285
  160.2 3.1 %collective-permute-start.18 = (bf16[128,3584]{1,0:T(8,128)(2,1)}, bf16[128,3584]{1,0:T(8,128)(2,1)}, u32[]{:S(2)}, u32[]{:S(2)}) collective-permute-start(bf16[128,3584]{1,0:T(8,128)(2,1)} %get-tuple-element.54), channel_id=1, source_target_pairs={{0,5},{1,4},{2,7},{3,6},{4,1},{5,0},{6,3},{7,2},{8,13},{9,12},{10,... | collective-permute-start | bytes 2752520 | tf_op jit(solution)/shard_map/ppermute | solution.py:44
  163.3 15.2 %shard_map.120 = bf16[98,128,128]{2,1,0:T(8,128)(2,1)} custom-call(s32[3,128]{1,0:T(4,128)} %pad_add_fusion.codes_ref, s32[3,128]{1,0:T(4,128)} %pad_add_fusion.1.keys_ref, bf16[128,3584]{1,0:T(8,128)(2,1)} %shard_map.112.refs_0_, bf16[128,3584]{1,0:T(8,128)(2,1)} %copy-done.8, bf16[128,3584]{1,0:T(8,128)(2,1)} %copy-done.7, bf16[128,3584]{1,0:T(8,128)(2,1)} %copy-done.6, ...), custom_call_target="tpu_custom_call" | custom-call | flops 1024 | bytes 1024 | tf_op jit(solution)/shard_map/pallas_call | solution.py:344
  178.5 12.3 %shard_map.121 = bf16[98,128,128]{2,1,0:T(8,128)(2,1)} custom-call(s32[3,128]{1,0:T(4,128)} %pad_add_fusion.codes_ref, s32[3,128]{1,0:T(4,128)} %pad_add_fusion.1.keys_ref, bf16[128,3584]{1,0:T(8,128)(2,1)} %copy-done, bf16[128,3584]{1,0:T(8,128)(2,1)} %copy-done.2, bf16[128,3584]{1,0:T(8,128)(2,1)} %copy-done.3, bf16[128,3584]{1,0:T(8,128)(2,1)} %copy-done.1, ...), custom_call_target="tpu_custom_call" | custom-call | flops 1024 | bytes 1024 | tf_op jit(solution)/shard_map/pallas_call | solution.py:403
  190.8 9.6 %collective-permute-done.20.refs_6_ = bf16[128,3584]{1,0:T(8,128)(2,1)S(1)} collective-permute-done((bf16[128,3584]{1,0:T(8,128)(2,1)}, bf16[128,3584]{1,0:T(8,128)(2,1)S(1)}, u32[]{:S(2)}, u32[]{:S(2)}) %collective-permute-start.20) | collective-permute-done | bytes 917536 | tf_op jit(solution)/shard_map/ppermute | solution.py:44
  200.5 12.6 %collective-permute-done.18.refs_4_ = bf16[128,3584]{1,0:T(8,128)(2,1)} collective-permute-done((bf16[128,3584]{1,0:T(8,128)(2,1)}, bf16[128,3584]{1,0:T(8,128)(2,1)}, u32[]{:S(2)}, u32[]{:S(2)}) %collective-permute-start.18) | collective-permute-done | bytes 917536 | tf_op jit(solution)/shard_map/ppermute | solution.py:44
  213.1 6.2 %shard_map.119 = bf16[128,3584]{1,0:T(8,128)(2,1)} custom-call(bf16[128,3584]{1,0:T(8,128)(2,1)} %bitcast.47, f32[1,3584]{1,0:T(1,128)} %gain_ref.3, bf16[128,3584]{1,0:T(8,128)(2,1)} %copy-done, bf16[128,3584]{1,0:T(8,128)(2,1)} %get-tuple-element.44.refs_0_, bf16[128,3584]{1,0:T(8,128)(2,1)} %collective-permute-done.14.refs_1_, ...), custom_call_target="tpu_custom_call" | custom-call | flops 1024 | bytes 1024 | tf_op jit(solution)/shard_map/pallas_call | solution.py:438
  (77 shorter events, 14.7 us)
Async XLA Ops:
  4.3 24.1 %collective-permute-start.3 = (bf16[128,3584]{1,0:T(8,128)(2,1)}, bf16[128,3584]{1,0:T(8,128)(2,1)S(1)}, u32[]{:S(2)}, u32[]{:S(2)}) collective-permute-start(bf16[128,3584]{1,0:T(8,128)(2,1)} %shard_map.112.refs_0_), channel_id=1, source_target_pairs={{0,6},{1,7},{2,0},{3,1},{4,2},{5,3},{6,4},{7,5},{8,9},{9,8},{10,11... | collective-permute-start | bytes 2752520 | tf_op jit(solution)/shard_map/ppermute | solution.py:44
  8.3 20.8 %collective-permute-start.2 = (bf16[128,3584]{1,0:T(8,128)(2,1)}, bf16[128,3584]{1,0:T(8,128)(2,1)S(1)}, u32[]{:S(2)}, u32[]{:S(2)}) collective-permute-start(bf16[128,3584]{1,0:T(8,128)(2,1)} %shard_map.112.refs_0_), channel_id=1, source_target_pairs={{0,2},{1,3},{2,4},{3,5},{4,6},{5,7},{6,0},{7,1},{8,10},{9,11},{10,... | collective-permute-start | bytes 2752520 | tf_op jit(solution)/shard_map/ppermute | solution.py:44
  8.3 30.5 %collective-permute-start.1 = (bf16[128,3584]{1,0:T(8,128)(2,1)}, bf16[128,3584]{1,0:T(8,128)(2,1)S(1)}, u32[]{:S(2)}, u32[]{:S(2)}) collective-permute-start(bf16[128,3584]{1,0:T(8,128)(2,1)} %shard_map.112.refs_0_), channel_id=1, source_target_pairs={{0,1},{1,0},{2,3},{3,2},{4,5},{5,4},{6,7},{7,6},{8,14},{9,15},{10,... | collective-permute-start | bytes 2752520 | tf_op jit(solution)/shard_map/ppermute | solution.py:44
  8.8 54.6 %collective-permute-start = (bf16[128,3584]{1,0:T(8,128)(2,1)}, bf16[128,3584]{1,0:T(8,128)(2,1)S(1)}, u32[]{:S(2)}, u32[]{:S(2)}) collective-permute-start(bf16[128,3584]{1,0:T(8,128)(2,1)} %bitcast.56), channel_id=1, source_target_pairs={{0,120},{8,0},{16,8},{24,16},{32,24},{40,32},{48,40},{56,48},{64,5... | collective-permute-start | bytes 2752520 | tf_op jit(solution)/shard_map/ppermute | solution.py:53
  38.8 24.5 %collective-permute-start.6 = (bf16[128,3584]{1,0:T(8,128)(2,1)S(1)}, bf16[128,3584]{1,0:T(8,128)(2,1)}, u32[]{:S(2)}, u32[]{:S(2)}) collective-permute-start(bf16[128,3584]{1,0:T(8,128)(2,1)S(1)} %collective-permute-done.1.refs_1_), channel_id=1, source_target_pairs={{0,2},{1,3},{2,4},{3,5},{4,6},{5,7},{6,0},{7,1},{8,9},{9,8},{10,11... | collective-permute-start | bytes 2752520 | tf_op jit(solution)/shard_map/ppermute | solution.py:44
  38.8 24.5 %collective-permute-start.5 = (bf16[128,3584]{1,0:T(8,128)(2,1)S(1)}, bf16[128,3584]{1,0:T(8,128)(2,1)}, u32[]{:S(2)}, u32[]{:S(2)}) collective-permute-start(bf16[128,3584]{1,0:T(8,128)(2,1)S(1)} %collective-permute-done.1.refs_1_), channel_id=1, source_target_pairs={{0,6},{1,7},{2,0},{3,1},{4,2},{5,3},{6,4},{7,5},{8,14},{9,15},{10,... | collective-permute-start | bytes 2752520 | tf_op jit(solution)/shard_map/ppermute | solution.py:44
  42.0 21.3 %collective-permute-start.4 = (bf16[128,3584]{1,0:T(8,128)(2,1)S(1)}, bf16[128,3584]{1,0:T(8,128)(2,1)}, u32[]{:S(2)}, u32[]{:S(2)}) collective-permute-start(bf16[128,3584]{1,0:T(8,128)(2,1)S(1)} %collective-permute-done.2.refs_2_), channel_id=1, source_target_pairs={{0,2},{1,3},{2,4},{3,5},{4,6},{5,7},{6,0},{7,1},{8,9},{9,8},{10,11... | collective-permute-start | bytes 2752520 | tf_op jit(solution)/shard_map/ppermute | solution.py:44
  63.3 32.2 %copy-start = (bf16[128,3584]{1,0:T(8,128)(2,1)}, bf16[128,3584]{1,0:T(8,128)(2,1)S(1)}, u32[]{:S(2)}) copy-start(bf16[128,3584]{1,0:T(8,128)(2,1)S(1)} %collective-permute-done.refs_0_.grad_ref) | copy-start | bytes 2752516
  63.3 18.4 %collective-permute-start.8 = (bf16[128,3584]{1,0:T(8,128)(2,1)}, bf16[128,3584]{1,0:T(8,128)(2,1)}, u32[]{:S(2)}, u32[]{:S(2)}) collective-permute-start(bf16[128,3584]{1,0:T(8,128)(2,1)} %collective-permute-done.5.refs_1_.refs_5_), channel_id=1, source_target_pairs={{0,6},{1,7},{2,0},{3,1},{4,2},{5,3},{6,4},{7,5},{8,9},{9,8},{10,11... | collective-permute-start | bytes 2752520 | tf_op jit(solution)/shard_map/ppermute | solution.py:44
  66.0 29.5 %collective-permute-start.10 = (bf16[128,3584]{1,0:T(8,128)(2,1)S(1)}, bf16[128,3584]{1,0:T(8,128)(2,1)S(1)}, u32[]{:S(2)}, u32[]{:S(2)}) collective-permute-start(bf16[128,3584]{1,0:T(8,128)(2,1)S(1)} %collective-permute-done.refs_0_.grad_ref), channel_id=1, source_target_pairs={{0,6},{1,7},{2,0},{3,1},{4,2},{5,3},{6,4},{7,5},{8,9},{9,8},{10,11... | collective-permute-start | bytes 2752520 | tf_op jit(solution)/shard_map/ppermute | solution.py:44
  66.1 29.4 %collective-permute-start.9 = (bf16[128,3584]{1,0:T(8,128)(2,1)S(1)}, bf16[128,3584]{1,0:T(8,128)(2,1)S(1)}, u32[]{:S(2)}, u32[]{:S(2)}) collective-permute-start(bf16[128,3584]{1,0:T(8,128)(2,1)S(1)} %collective-permute-done.refs_0_.grad_ref), channel_id=1, source_target_pairs={{0,1},{1,0},{2,3},{3,2},{4,5},{5,4},{6,7},{7,6},{8,14},{9,15},{10,... | collective-permute-start | bytes 2752520 | tf_op jit(solution)/shard_map/ppermute | solution.py:44
  66.5 29.0 %collective-permute-start.7 = (bf16[128,3584]{1,0:T(8,128)(2,1)S(1)}, bf16[128,3584]{1,0:T(8,128)(2,1)S(1)}, u32[]{:S(2)}, u32[]{:S(2)}) collective-permute-start(bf16[128,3584]{1,0:T(8,128)(2,1)S(1)} %collective-permute-done.refs_0_.grad_ref), channel_id=1, source_target_pairs={{0,2},{1,3},{2,4},{3,5},{4,6},{5,7},{6,0},{7,1},{8,10},{9,11},{10,... | collective-permute-start | bytes 2752520 | tf_op jit(solution)/shard_map/ppermute | solution.py:44
  95.6 17.1 %collective-permute-start.12 = (bf16[128,3584]{1,0:T(8,128)(2,1)S(1)}, bf16[128,3584]{1,0:T(8,128)(2,1)S(1)}, u32[]{:S(2)}, u32[]{:S(2)}) collective-permute-start(bf16[128,3584]{1,0:T(8,128)(2,1)S(1)} %collective-permute-done.9.refs_1_), channel_id=1, source_target_pairs={{0,6},{1,7},{2,0},{3,1},{4,2},{5,3},{6,4},{7,5},{8,14},{9,15},{10,... | collective-permute-start | bytes 2752520 | tf_op jit(solution)/shard_map/ppermute | solution.py:44
  99.4 14.7 %collective-permute-start.11 = (bf16[128,3584]{1,0:T(8,128)(2,1)S(1)}, bf16[128,3584]{1,0:T(8,128)(2,1)}, u32[]{:S(2)}, u32[]{:S(2)}) collective-permute-start(bf16[128,3584]{1,0:T(8,128)(2,1)S(1)} %collective-permute-done.7.refs_2_), channel_id=1, source_target_pairs={{0,2},{1,3},{2,4},{3,5},{4,6},{5,7},{6,0},{7,1},{8,9},{9,8},{10,11... | collective-permute-start | bytes 2752520 | tf_op jit(solution)/shard_map/ppermute | solution.py:44
  99.4 29.1 %collective-permute-start.13 = (bf16[128,3584]{1,0:T(8,128)(2,1)S(1)}, bf16[128,3584]{1,0:T(8,128)(2,1)}, u32[]{:S(2)}, u32[]{:S(2)}) collective-permute-start(bf16[128,3584]{1,0:T(8,128)(2,1)S(1)} %collective-permute-done.9.refs_1_), channel_id=1, source_target_pairs={{0,2},{1,3},{2,4},{3,5},{4,6},{5,7},{6,0},{7,1},{8,9},{9,8},{10,11... | collective-permute-start | bytes 2752520 | tf_op jit(solution)/shard_map/ppermute | solution.py:44
  114.1 18.9 %collective-permute-start.17 = (bf16[128,3584]{1,0:T(8,128)(2,1)S(1)}, bf16[128,3584]{1,0:T(8,128)(2,1)S(1)}, u32[]{:S(2)}, u32[]{:S(2)}) collective-permute-start(bf16[128,3584]{1,0:T(8,128)(2,1)S(1)} %collective-permute-done.12.refs_1_.refs_5_), channel_id=1, source_target_pairs={{0,6},{1,7},{2,0},{3,1},{4,2},{5,3},{6,4},{7,5},{8,9},{9,8},{10,11... | collective-permute-start | bytes 2752520 | tf_op jit(solution)/shard_map/ppermute | solution.py:44
  128.5 28.0 %collective-permute-start.16 = (bf16[128,3584]{1,0:T(8,128)(2,1)}, bf16[128,3584]{1,0:T(8,128)(2,1)S(1)}, u32[]{:S(2)}, u32[]{:S(2)}) collective-permute-start(bf16[128,3584]{1,0:T(8,128)(2,1)} %get-tuple-element.50), channel_id=1, source_target_pairs={{0,2},{1,3},{2,4},{3,5},{4,6},{5,7},{6,0},{7,1},{8,9},{9,8},{10,11... | collective-permute-start | bytes 2752520 | tf_op jit(solution)/shard_map/ppermute | solution.py:44
  128.5 27.9 %collective-permute-start.15 = (bf16[128,3584]{1,0:T(8,128)(2,1)}, bf16[128,3584]{1,0:T(8,128)(2,1)S(1)}, u32[]{:S(2)}, u32[]{:S(2)}) collective-permute-start(bf16[128,3584]{1,0:T(8,128)(2,1)} %get-tuple-element.48), channel_id=1, source_target_pairs={{0,6},{1,7},{2,0},{3,1},{4,2},{5,3},{6,4},{7,5},{8,14},{9,15},{10,... | collective-permute-start | bytes 2752520 | tf_op jit(solution)/shard_map/ppermute | solution.py:44
  131.8 24.7 %collective-permute-start.14 = (bf16[128,3584]{1,0:T(8,128)(2,1)}, bf16[128,3584]{1,0:T(8,128)(2,1)}, u32[]{:S(2)}, u32[]{:S(2)}) collective-permute-start(bf16[128,3584]{1,0:T(8,128)(2,1)} %get-tuple-element.46), channel_id=1, source_target_pairs={{0,1},{1,0},{2,3},{3,2},{4,5},{5,4},{6,7},{7,6},{8,10},{9,11},{10,... | collective-permute-start | bytes 2752520 | tf_op jit(solution)/shard_map/ppermute | solution.py:44
  156.5 34.4 %collective-permute-start.21 = (bf16[128,3584]{1,0:T(8,128)(2,1)}, bf16[128,3584]{1,0:T(8,128)(2,1)S(1)}, u32[]{:S(2)}, u32[]{:S(2)}) collective-permute-start(bf16[128,3584]{1,0:T(8,128)(2,1)} %get-tuple-element.60), channel_id=1, source_target_pairs={{0,7},{1,6},{2,1},{3,0},{4,3},{5,2},{6,5},{7,4},{8,11},{9,10},{10,... | collective-permute-start | bytes 2752520 | tf_op jit(solution)/shard_map/ppermute | solution.py:44
  158.6 41.8 %collective-permute-start.20 = (bf16[128,3584]{1,0:T(8,128)(2,1)}, bf16[128,3584]{1,0:T(8,128)(2,1)S(1)}, u32[]{:S(2)}, u32[]{:S(2)}) collective-permute-start(bf16[128,3584]{1,0:T(8,128)(2,1)} %get-tuple-element.58), channel_id=1, source_target_pairs={{0,3},{1,2},{2,5},{3,4},{4,7},{5,6},{6,1},{7,0},{8,12},{9,13},{10,... | collective-permute-start | bytes 2752520 | tf_op jit(solution)/shard_map/ppermute | solution.py:44
  159.5 41.0 %collective-permute-start.19 = (bf16[128,3584]{1,0:T(8,128)(2,1)}, bf16[128,3584]{1,0:T(8,128)(2,1)}, u32[]{:S(2)}, u32[]{:S(2)}) collective-permute-start(bf16[128,3584]{1,0:T(8,128)(2,1)} %get-tuple-element.56), channel_id=1, source_target_pairs={{0,4},{1,5},{2,6},{3,7},{4,0},{5,1},{6,2},{7,3},{8,15},{9,14},{10,... | collective-permute-start | bytes 2752520 | tf_op jit(solution)/shard_map/ppermute | solution.py:44
  160.2 52.9 %collective-permute-start.18 = (bf16[128,3584]{1,0:T(8,128)(2,1)}, bf16[128,3584]{1,0:T(8,128)(2,1)}, u32[]{:S(2)}, u32[]{:S(2)}) collective-permute-start(bf16[128,3584]{1,0:T(8,128)(2,1)} %get-tuple-element.54), channel_id=1, source_target_pairs={{0,5},{1,4},{2,7},{3,6},{4,1},{5,0},{6,3},{7,2},{8,13},{9,12},{10,... | collective-permute-start | bytes 2752520 | tf_op jit(solution)/shard_map/ppermute | solution.py:44
  190.8 22.2 %copy-start.11 = (bf16[128,3584]{1,0:T(8,128)(2,1)}, bf16[128,3584]{1,0:T(8,128)(2,1)S(1)}, u32[]{:S(2)}) copy-start(bf16[128,3584]{1,0:T(8,128)(2,1)S(1)} %collective-permute-done.21.refs_7_) | copy-start | bytes 2752516
  (11 other events, 123.6 us)

commit v4 on v3

--- a/solution.py
+++ b/solution.py
@@ -297,6 +297,86 @@
     )(codes, keys, pre_grad, up_tiles)
 
 
+def both_grads_kernel(pieces, by_unit, by_feature, codes_ref, keys_ref, *refs):
+    grad_refs, (down_ref, slope_ref, up_ref, pre_grad_ref) = refs[:pieces], refs[pieces : pieces + 4]
+    out_refs = refs[pieces + 4 : 2 * pieces + 4]
+    grads, down, slope, hidden_grad, up, total, sems = refs[2 * pieces + 4 :]
+    rows = grad_refs[0].shape[0]
+    copies = [start_tiles(down_ref, down, sems.at[pieces])]
+    for i, ref in enumerate(grad_refs):
+        copies.append(
+            pltpu.make_async_copy(ref, grads.at[pl.ds(i * rows, rows)], sems.at[i])
+        )
+        copies[-1].start()
+    slope_copy = pltpu.make_async_copy(slope_ref, slope, sems.at[pieces + 1])
+    slope_copy.start()
+    up_copy = start_tiles(up_ref, up, sems.at[pieces + 2])
+    hidden_grad[...] = jnp.zeros_like(hidden_grad)
+    total[...] = jnp.zeros_like(total)
+    for copy in copies:
+        copy.wait()
+
+    def add_hidden_grad(s):
+        codes = [codes_ref[1, s * PAIR + i] for i in range(PAIR)]
+        left = jnp.concatenate([grads[:, lanes(code & 31)] for code in codes], axis=1)
+        right = jnp.concatenate([down[code >> 5] for code in codes], axis=1)
+        hidden_grad[:, lanes(keys_ref[1, s])] += lax.dot_general(
+            left, right, (((1,), (1,)), ((), ())), preferred_element_type=F32
+        )
+
+    run_groups(by_unit, 14, add_hidden_grad)
+    slope_copy.wait()
+
+    @pl.loop(0, slope.shape[0] // 32)
+    def _(i):
+        at = pl.ds(pl.multiple_of(i * 32, 32), 32)
+        pre_grad_ref[at, :] = (hidden_grad[at, :] * slope[at, :]).astype(BF16)
+
+    up_copy.wait()
+
+    def add_unit_grad(s):
+        codes = [codes_ref[2, s * PAIR + i] for i in range(PAIR)]
+        left = jnp.concatenate([pre_grad_ref[:, lanes(code & 31)] for code in codes], axis=1)
+        right = jnp.concatenate([up[code >> 5] for code in codes], axis=1)
+        total[:, lanes(keys_ref[2, s])] += lax.dot_general(
+            left, right, (((1,), (1,)), ((), ())), preferred_element_type=F32
+        )
+
+    run_groups(by_feature, 21, add_unit_grad)
+    for piece, out_ref in enumerate(out_refs):
+
+        @pl.loop(0, rows // 16)
+        def _(i):
+            step = pl.multiple_of(i * 16, 16)
+            out_ref[pl.ds(step, 16), :] = total[pl.ds(piece * rows + step, 16), :].astype(BF16)
+
+
+def both_grads_of(codes, keys, grads, down_tiles, slope, up_tiles, by_unit, by_feature):
+    pieces = len(grads)
+    rows, features = grads[0].shape
+    tokens, wide = slope.shape
+    held = (up_tiles.shape[0] + 1,) + up_tiles.shape[1:]
+    pre_grad, *parts = pl.pallas_call(
+        functools.partial(both_grads_kernel, pieces, by_unit, by_feature),
+        out_shape=[jax.ShapeDtypeStruct((tokens, wide), BF16)]
+        + [jax.ShapeDtypeStruct((rows, features), BF16)] * pieces,
+        in_specs=[SMEM, SMEM] + [ANY] * (pieces + 3),
+        out_specs=[VMEM] * (1 + pieces),
+        scratch_shapes=[
+            pltpu.VMEM((tokens, features), BF16),
+            pltpu.VMEM(held, BF16),
+            pltpu.VMEM((tokens, wide), F32),
+            pltpu.VMEM((tokens, wide), F32),
+            pltpu.VMEM(held, BF16),
+            pltpu.VMEM((tokens, features), F32),
+            pltpu.SemaphoreType.DMA((pieces + 3,)),
+        ],
+        compiler_params=pltpu.CompilerParams(vmem_limit_bytes=ROOM),
+        cost_estimate=SMALL,
+    )(codes, keys, *grads, down_tiles, slope, up_tiles)
+    return pre_grad, parts
+
+
 def up_grad_kernel(parts, groups, codes_ref, keys_ref, *refs):
     pieces = 2 * PIECES
     unit_refs, slope_refs = refs[:pieces], refs[pieces : pieces + parts]
@@ -500,10 +580,17 @@
         after(codes, grads[4], grads[5]), keys, near_pre_grad, up, rows, features, by_feature
     )
     terms = [parts[0]] + [returned(after(parts[i], grads[6]), i) for i in (1, 2, 3)]
-    far_pre_grad = pre_grad_of(
-        after(codes, *parts, grads[7]), keys, [grads[i] for i in far], down, far_slope, by_unit
-    )
-    parts += unit_grad_of(codes, keys, far_pre_grad, up, rows, features, by_feature)
+    far_pre_grad, far_parts = both_grads_of(
+        after(codes, *parts, grads[7]),
+        keys,
+        [grads[i] for i in far],
+        down,
+        far_slope,
+        up,
+        by_unit,
+        by_feature,
+    )
+    parts = [*parts, *far_parts]
     terms += [returned(after(parts[i], *terms[1:4]), i) for i in (7, 4, 5, 6)]
     pre_grads, hidden = [near_pre_grad, far_pre_grad], [near_hidden, far_hidden]
     up_grad = up_grad_of(

time: 221 us -> 220 us (level)
  waiting for transfers between devices: 72.8 us -> 77.7 us
  Pallas kernels: 110 us -> 106 us
    pallas_call x0 -> x1, Pallas kernels: none -> 18.5 us  [both_grads_of(): pl.pallas_call(functools.partial(both_grads_kernel, pieces, by_unit, by_f...]
    pallas_call x2 -> x1, Pallas kernels: 24.1 us -> 12.1 us  [unit_grad_of(): pl.pallas_call(functools.partial(unit_grad_kernel, pieces, groups), out_s...]
    pallas_call x2 -> x1, Pallas kernels: 20.9 us -> 10.5 us  [pre_grad_of(): pl.pallas_call(functools.partial(pre_grad_kernel, pieces, start, groups),...]
    ppermute x21, waiting for transfers between devices: 72.8 us -> 77.7 us  [along(): return lax.ppermute(value, ('section', 'tp'), pairs)]
  transfers between devices with their start and end apart: 22 -> 22, of which waited for: 10 -> 7; matrix products, arithmetic and copies ran while one was open for 2% -> 2% of each run, Pallas kernels for 46% -> 44%
where the time goes in v4:
time: 220 us
  Pallas kernels  106 us (48%)
  waiting for transfers between devices  77.7 us (35%)
  starting transfers between devices  29.3 us (13%)
  other arithmetic  3.68 us (2%)
  between operations  2.26 us (1%)
    ppermute x21, waiting for transfers between devices, along(): return lax.ppermute(value, ('section', 'tp'), pairs)  77.7 us
    ppermute x21, starting transfers between devices, along(): return lax.ppermute(value, ('section', 'tp'), pairs)  29.3 us
    pallas_call x2, Pallas kernels, hidden_of(): pl.pallas_call(functools.partial(hidden_kernel, groups), out_shape=[jax.S...  27.5 us
    pallas_call x1, Pallas kernels, both_grads_of(): pl.pallas_call(functools.partial(both_grads_kernel, pieces, by_unit, by_f...  18.5 us
    pallas_call x1, Pallas kernels, up_grad_of(): pl.pallas_call(functools.partial(up_grad_kernel, len(slopes), groups), ou...  15.1 us
    pallas_call x1, Pallas kernels, down_grad_of(): pl.pallas_call(functools.partial(down_grad_kernel, groups), out_shape=jax...  12.5 us
    pallas_call x1, Pallas kernels, unit_grad_of(): pl.pallas_call(functools.partial(unit_grad_kernel, pieces, groups), out_s...  12.1 us
    pallas_call x1, Pallas kernels, pre_grad_of(): pl.pallas_call(functools.partial(pre_grad_kernel, pieces, start, groups),...  10.5 us
  transfers between devices with their start and end apart: 22, of which 7 were waited for; matrix products, arithmetic and copies ran while one was open for 2% of the time, Pallas kernels for 44%

profile of v4, /device:TPU:14, one launch (start us, length us, event | category | flops | bytes accessed | tf_op | source)
XLA Modules:
  0.0 219.9 jit_solution(11103952951646644318)
XLA Ops:
  0.6 3.6 %shard_map.112.refs_0_ = bf16[128,3584]{1,0:T(8,128)(2,1)} custom-call(bf16[128,3584]{1,0:T(8,128)(2,1)} %bitcast.46, f32[1,3584]{1,0:T(1,128)} %gain_ref.3), custom_call_target="tpu_custom_call" | custom-call | flops 1024 | bytes 1024 | tf_op jit(solution)/shard_map/pallas_call | solution.py:111
  4.7 1.9 collective-permute-start.2
  6.6 2.1 collective-permute-start.3
  12.4 22.4 %collective-permute-done.1.refs_1_ = bf16[128,3584]{1,0:T(8,128)(2,1)S(1)} collective-permute-done((bf16[128,3584]{1,0:T(8,128)(2,1)}, bf16[128,3584]{1,0:T(8,128)(2,1)S(1)}, u32[]{:S(2)}, u32[]{:S(2)}) %collective-permute-start.1) | collective-permute-done | bytes 917536 | tf_op jit(solution)/shard_map/ppermute | solution.py:44
  34.9 5.2 %collective-permute-start.5 = (bf16[128,3584]{1,0:T(8,128)(2,1)S(1)}, bf16[128,3584]{1,0:T(8,128)(2,1)}, u32[]{:S(2)}, u32[]{:S(2)}) collective-permute-start(bf16[128,3584]{1,0:T(8,128)(2,1)S(1)} %collective-permute-done.1.refs_1_), channel_id=1, source_target_pairs={{0,6},{1,7},{2,0},{3,1},{4,2},{5,3},{6,4},{7,5},{8,14},{9,15},{10,... | collective-permute-start | bytes 2752520 | tf_op jit(solution)/shard_map/ppermute | solution.py:44
  42.6 13.8 %shard_map.113 = (bf16[512,1792]{1,0:T(8,128)(2,1)}, f32[512,1792]{1,0:T(8,128)}) custom-call(s32[3,128]{1,0:T(4,128)} %pad_add_fusion.codes_ref, s32[3,128]{1,0:T(4,128)} %pad_add_fusion.1.keys_ref, bf16[128,3584]{1,0:T(8,128)(2,1)} %shard_map.112.refs_0_, bf16[128,3584]{1,0:T(8,128)(2,1)} %copy-done.6, bf16[128,3584]{1,0:T(8,128)(2,1)} %copy-done.7, ...), custom_call_target="tpu_custom_call" | custom-call | flops 1024 | bytes 1024 | tf_op jit(solution)/shard_map/pallas_call | solution.py:181
  56.4 4.1 %collective-permute-done.5.refs_1_.refs_5_ = bf16[128,3584]{1,0:T(8,128)(2,1)} collective-permute-done((bf16[128,3584]{1,0:T(8,128)(2,1)S(1)}, bf16[128,3584]{1,0:T(8,128)(2,1)}, u32[]{:S(2)}, u32[]{:S(2)}) %collective-permute-start.5) | collective-permute-done | bytes 917536 | tf_op jit(solution)/shard_map/ppermute | solution.py:44
  60.5 4.1 %collective-permute-done.4.refs_0_.refs_4_ = bf16[128,3584]{1,0:T(8,128)(2,1)} collective-permute-done((bf16[128,3584]{1,0:T(8,128)(2,1)S(1)}, bf16[128,3584]{1,0:T(8,128)(2,1)}, u32[]{:S(2)}, u32[]{:S(2)}) %collective-permute-start.4) | collective-permute-done | bytes 917536 | tf_op jit(solution)/shard_map/ppermute | solution.py:44
  65.1 1.9 collective-permute-start.7
  67.5 19.9 %collective-permute-done.8.refs_3_.refs_7_ = bf16[128,3584]{1,0:T(8,128)(2,1)} collective-permute-done((bf16[128,3584]{1,0:T(8,128)(2,1)}, bf16[128,3584]{1,0:T(8,128)(2,1)}, u32[]{:S(2)}, u32[]{:S(2)}) %collective-permute-start.8) | collective-permute-done | bytes 917536 | tf_op jit(solution)/shard_map/ppermute | solution.py:44
  87.4 13.7 %shard_map.114 = (bf16[512,1792]{1,0:T(8,128)(2,1)}, f32[512,1792]{1,0:T(8,128)}) custom-call(s32[3,128]{1,0:T(4,128)} %pad_add_fusion.codes_ref, s32[3,128]{1,0:T(4,128)} %pad_add_fusion.1.keys_ref, bf16[128,3584]{1,0:T(8,128)(2,1)} %collective-permute-done.4.refs_0_.refs_4_, bf16[128,3584]{1,0:T(8,128)(2,1)} %collective-permute-done.5.refs_1_.refs_5_, ...), custom_call_target="tpu_custom_call" | custom-call | flops 1024 | bytes 1024 | tf_op jit(solution)/shard_map/pallas_call | solution.py:181
  103.3 10.5 %shard_map.115.pre_grad_ref.refs_8_ = bf16[512,1792]{1,0:T(8,128)(2,1)} custom-call(s32[3,128]{1,0:T(4,128)} %pad_add_fusion.codes_ref, s32[3,128]{1,0:T(4,128)} %pad_add_fusion.1.keys_ref, bf16[128,3584]{1,0:T(8,128)(2,1)} %copy-done, bf16[128,3584]{1,0:T(8,128)(2,1)} %copy-done.3, bf16[128,3584]{1,0:T(8,128)(2,1)} %copy-done.2, ...), custom_call_target="tpu_custom_call" | custom-call | flops 1024 | bytes 1024 | tf_op jit(solution)/shard_map/pallas_call | solution.py:240
  113.8 4.6 %collective-permute-done.12.refs_1_.refs_5_ = bf16[128,3584]{1,0:T(8,128)(2,1)S(1)} collective-permute-done((bf16[128,3584]{1,0:T(8,128)(2,1)S(1)}, bf16[128,3584]{1,0:T(8,128)(2,1)S(1)}, u32[]{:S(2)}, u32[]{:S(2)}) %collective-permute-start.12) | collective-permute-done | bytes 917536 | tf_op jit(solution)/shard_map/ppermute | solution.py:44
  118.3 2.0 collective-permute-start.17
  120.4 12.1 %shard_map.116 = (bf16[128,3584]{1,0:T(8,128)(2,1)}, bf16[128,3584]{1,0:T(8,128)(2,1)}, bf16[128,3584]{1,0:T(8,128)(2,1)}, bf16[128,3584]{1,0:T(8,128)(2,1)}) custom-call(s32[3,128]{1,0:T(4,128)} %pad_add_fusion.codes_ref, s32[3,128]{1,0:T(4,128)} %pad_add_fusion.1.keys_ref, bf16[512,1792]{1,0:T(8,128)(2,1)} %shard_map.115.pre_grad_ref.refs_8_, ...), custom_call_target="tpu_custom_call" | custom-call | flops 1024 | bytes 1024 | tf_op jit(solution)/shard_map/pallas_call | solution.py:285
  132.7 3.2 %collective-permute-start.15 = (bf16[128,3584]{1,0:T(8,128)(2,1)}, bf16[128,3584]{1,0:T(8,128)(2,1)S(1)}, u32[]{:S(2)}, u32[]{:S(2)}) collective-permute-start(bf16[128,3584]{1,0:T(8,128)(2,1)} %get-tuple-element.49), channel_id=1, source_target_pairs={{0,6},{1,7},{2,0},{3,1},{4,2},{5,3},{6,4},{7,5},{8,14},{9,15},{10,... | collective-permute-start | bytes 2752520 | tf_op jit(solution)/shard_map/ppermute | solution.py:44
  137.3 18.5 %shard_map.117 = (bf16[512,1792]{1,0:T(8,128)(2,1)}, bf16[128,3584]{1,0:T(8,128)(2,1)}, bf16[128,3584]{1,0:T(8,128)(2,1)}, bf16[128,3584]{1,0:T(8,128)(2,1)}, bf16[128,3584]{1,0:T(8,128)(2,1)}) custom-call(s32[3,128]{1,0:T(4,128)} %pad_add_fusion.codes_ref, s32[3,128]{1,0:T(4,128)} %pad_add_fusion.1.keys_ref, ...), custom_call_target="tpu_custom_call" | custom-call | flops 1024 | bytes 1024 | tf_op jit(solution)/shard_map/pallas_call | solution.py:359
  157.0 1.8 collective-permute-start.20
  158.8 4.5 %collective-permute-start.18 = (bf16[128,3584]{1,0:T(8,128)(2,1)}, bf16[128,3584]{1,0:T(8,128)(2,1)}, u32[]{:S(2)}, u32[]{:S(2)}) collective-permute-start(bf16[128,3584]{1,0:T(8,128)(2,1)} %get-tuple-element.55), channel_id=1, source_target_pairs={{0,5},{1,4},{2,7},{3,6},{4,1},{5,0},{6,3},{7,2},{8,13},{9,12},{10,... | collective-permute-start | bytes 2752520 | tf_op jit(solution)/shard_map/ppermute | solution.py:44
  163.3 15.1 %shard_map.119 = bf16[98,128,128]{2,1,0:T(8,128)(2,1)} custom-call(s32[3,128]{1,0:T(4,128)} %pad_add_fusion.codes_ref, s32[3,128]{1,0:T(4,128)} %pad_add_fusion.1.keys_ref, bf16[128,3584]{1,0:T(8,128)(2,1)} %shard_map.112.refs_0_, bf16[128,3584]{1,0:T(8,128)(2,1)} %copy-done.6, bf16[128,3584]{1,0:T(8,128)(2,1)} %copy-done.7, bf16[128,3584]{1,0:T(8,128)(2,1)} %copy-done.8, ...), custom_call_target="tpu_custom_call" | custom-call | flops 1024 | bytes 1024 | tf_op jit(solution)/shard_map/pallas_call | solution.py:424
  178.5 12.5 %shard_map.120 = bf16[98,128,128]{2,1,0:T(8,128)(2,1)} custom-call(s32[3,128]{1,0:T(4,128)} %pad_add_fusion.codes_ref, s32[3,128]{1,0:T(4,128)} %pad_add_fusion.1.keys_ref, bf16[128,3584]{1,0:T(8,128)(2,1)} %copy-done, bf16[128,3584]{1,0:T(8,128)(2,1)} %copy-done.3, bf16[128,3584]{1,0:T(8,128)(2,1)} %copy-done.2, bf16[128,3584]{1,0:T(8,128)(2,1)} %copy-done.1, ...), custom_call_target="tpu_custom_call" | custom-call | flops 1024 | bytes 1024 | tf_op jit(solution)/shard_map/pallas_call | solution.py:483
  191.0 7.2 %collective-permute-done.20.refs_6_ = bf16[128,3584]{1,0:T(8,128)(2,1)S(1)} collective-permute-done((bf16[128,3584]{1,0:T(8,128)(2,1)}, bf16[128,3584]{1,0:T(8,128)(2,1)S(1)}, u32[]{:S(2)}, u32[]{:S(2)}) %collective-permute-start.20) | collective-permute-done | bytes 917536 | tf_op jit(solution)/shard_map/ppermute | solution.py:44
  198.3 15.5 %collective-permute-done.18.refs_4_ = bf16[128,3584]{1,0:T(8,128)(2,1)} collective-permute-done((bf16[128,3584]{1,0:T(8,128)(2,1)}, bf16[128,3584]{1,0:T(8,128)(2,1)}, u32[]{:S(2)}, u32[]{:S(2)}) %collective-permute-start.18) | collective-permute-done | bytes 917536 | tf_op jit(solution)/shard_map/ppermute | solution.py:44
  213.7 6.2 %shard_map.118 = bf16[128,3584]{1,0:T(8,128)(2,1)} custom-call(bf16[128,3584]{1,0:T(8,128)(2,1)} %bitcast.47, f32[1,3584]{1,0:T(1,128)} %gain_ref.3, bf16[128,3584]{1,0:T(8,128)(2,1)} %copy-done, bf16[128,3584]{1,0:T(8,128)(2,1)} %get-tuple-element.45.refs_0_, bf16[128,3584]{1,0:T(8,128)(2,1)} %collective-permute-done.14.refs_1_, ...), custom_call_target="tpu_custom_call" | custom-call | flops 1024 | bytes 1024 | tf_op jit(solution)/shard_map/pallas_call | solution.py:518
  (76 shorter events, 11.2 us)
Async XLA Ops:
  4.3 30.6 %collective-permute-start.1 = (bf16[128,3584]{1,0:T(8,128)(2,1)}, bf16[128,3584]{1,0:T(8,128)(2,1)S(1)}, u32[]{:S(2)}, u32[]{:S(2)}) collective-permute-start(bf16[128,3584]{1,0:T(8,128)(2,1)} %shard_map.112.refs_0_), channel_id=1, source_target_pairs={{0,1},{1,0},{2,3},{3,2},{4,5},{5,4},{6,7},{7,6},{8,14},{9,15},{10,... | collective-permute-start | bytes 2752520 | tf_op jit(solution)/shard_map/ppermute | solution.py:44
  4.7 30.1 %collective-permute-start.2 = (bf16[128,3584]{1,0:T(8,128)(2,1)}, bf16[128,3584]{1,0:T(8,128)(2,1)S(1)}, u32[]{:S(2)}, u32[]{:S(2)}) collective-permute-start(bf16[128,3584]{1,0:T(8,128)(2,1)} %shard_map.112.refs_0_), channel_id=1, source_target_pairs={{0,2},{1,3},{2,4},{3,5},{4,6},{5,7},{6,0},{7,1},{8,10},{9,11},{10,... | collective-permute-start | bytes 2752520 | tf_op jit(solution)/shard_map/ppermute | solution.py:44
  6.6 28.2 %collective-permute-start.3 = (bf16[128,3584]{1,0:T(8,128)(2,1)}, bf16[128,3584]{1,0:T(8,128)(2,1)S(1)}, u32[]{:S(2)}, u32[]{:S(2)}) collective-permute-start(bf16[128,3584]{1,0:T(8,128)(2,1)} %shard_map.112.refs_0_), channel_id=1, source_target_pairs={{0,6},{1,7},{2,0},{3,1},{4,2},{5,3},{6,4},{7,5},{8,9},{9,8},{10,11... | collective-permute-start | bytes 2752520 | tf_op jit(solution)/shard_map/ppermute | solution.py:44
  8.7 56.3 %collective-permute-start = (bf16[128,3584]{1,0:T(8,128)(2,1)}, bf16[128,3584]{1,0:T(8,128)(2,1)S(1)}, u32[]{:S(2)}, u32[]{:S(2)}) collective-permute-start(bf16[128,3584]{1,0:T(8,128)(2,1)} %bitcast.56), channel_id=1, source_target_pairs={{0,120},{8,0},{16,8},{24,16},{32,24},{40,32},{48,40},{56,48},{64,5... | collective-permute-start | bytes 2752520 | tf_op jit(solution)/shard_map/ppermute | solution.py:53
  34.9 25.6 %collective-permute-start.5 = (bf16[128,3584]{1,0:T(8,128)(2,1)S(1)}, bf16[128,3584]{1,0:T(8,128)(2,1)}, u32[]{:S(2)}, u32[]{:S(2)}) collective-permute-start(bf16[128,3584]{1,0:T(8,128)(2,1)S(1)} %collective-permute-done.1.refs_1_), channel_id=1, source_target_pairs={{0,6},{1,7},{2,0},{3,1},{4,2},{5,3},{6,4},{7,5},{8,14},{9,15},{10,... | collective-permute-start | bytes 2752520 | tf_op jit(solution)/shard_map/ppermute | solution.py:44
  40.0 20.5 %collective-permute-start.6 = (bf16[128,3584]{1,0:T(8,128)(2,1)S(1)}, bf16[128,3584]{1,0:T(8,128)(2,1)}, u32[]{:S(2)}, u32[]{:S(2)}) collective-permute-start(bf16[128,3584]{1,0:T(8,128)(2,1)S(1)} %collective-permute-done.1.refs_1_), channel_id=1, source_target_pairs={{0,2},{1,3},{2,4},{3,5},{4,6},{5,7},{6,0},{7,1},{8,9},{9,8},{10,11... | collective-permute-start | bytes 2752520 | tf_op jit(solution)/shard_map/ppermute | solution.py:44
  40.0 24.5 %collective-permute-start.4 = (bf16[128,3584]{1,0:T(8,128)(2,1)S(1)}, bf16[128,3584]{1,0:T(8,128)(2,1)}, u32[]{:S(2)}, u32[]{:S(2)}) collective-permute-start(bf16[128,3584]{1,0:T(8,128)(2,1)S(1)} %collective-permute-done.2.refs_2_), channel_id=1, source_target_pairs={{0,2},{1,3},{2,4},{3,5},{4,6},{5,7},{6,0},{7,1},{8,9},{9,8},{10,11... | collective-permute-start | bytes 2752520 | tf_op jit(solution)/shard_map/ppermute | solution.py:44
  64.6 22.8 %collective-permute-start.8 = (bf16[128,3584]{1,0:T(8,128)(2,1)}, bf16[128,3584]{1,0:T(8,128)(2,1)}, u32[]{:S(2)}, u32[]{:S(2)}) collective-permute-start(bf16[128,3584]{1,0:T(8,128)(2,1)} %collective-permute-done.5.refs_1_.refs_5_), channel_id=1, source_target_pairs={{0,6},{1,7},{2,0},{3,1},{4,2},{5,3},{6,4},{7,5},{8,9},{9,8},{10,11... | collective-permute-start | bytes 2752520 | tf_op jit(solution)/shard_map/ppermute | solution.py:44
  65.1 36.0 %copy-start = (bf16[128,3584]{1,0:T(8,128)(2,1)}, bf16[128,3584]{1,0:T(8,128)(2,1)S(1)}, u32[]{:S(2)}) copy-start(bf16[128,3584]{1,0:T(8,128)(2,1)S(1)} %collective-permute-done.refs_0_.grad_ref) | copy-start | bytes 2752516
  65.1 36.0 %collective-permute-start.10 = (bf16[128,3584]{1,0:T(8,128)(2,1)S(1)}, bf16[128,3584]{1,0:T(8,128)(2,1)S(1)}, u32[]{:S(2)}, u32[]{:S(2)}) collective-permute-start(bf16[128,3584]{1,0:T(8,128)(2,1)S(1)} %collective-permute-done.refs_0_.grad_ref), channel_id=1, source_target_pairs={{0,6},{1,7},{2,0},{3,1},{4,2},{5,3},{6,4},{7,5},{8,9},{9,8},{10,11... | collective-permute-start | bytes 2752520 | tf_op jit(solution)/shard_map/ppermute | solution.py:44
  65.1 36.0 %collective-permute-start.7 = (bf16[128,3584]{1,0:T(8,128)(2,1)S(1)}, bf16[128,3584]{1,0:T(8,128)(2,1)S(1)}, u32[]{:S(2)}, u32[]{:S(2)}) collective-permute-start(bf16[128,3584]{1,0:T(8,128)(2,1)S(1)} %collective-permute-done.refs_0_.grad_ref), channel_id=1, source_target_pairs={{0,2},{1,3},{2,4},{3,5},{4,6},{5,7},{6,0},{7,1},{8,10},{9,11},{10,... | collective-permute-start | bytes 2752520 | tf_op jit(solution)/shard_map/ppermute | solution.py:44
  67.1 34.0 %collective-permute-start.9 = (bf16[128,3584]{1,0:T(8,128)(2,1)S(1)}, bf16[128,3584]{1,0:T(8,128)(2,1)S(1)}, u32[]{:S(2)}, u32[]{:S(2)}) collective-permute-start(bf16[128,3584]{1,0:T(8,128)(2,1)S(1)} %collective-permute-done.refs_0_.grad_ref), channel_id=1, source_target_pairs={{0,1},{1,0},{2,3},{3,2},{4,5},{5,4},{6,7},{7,6},{8,14},{9,15},{10,... | collective-permute-start | bytes 2752520 | tf_op jit(solution)/shard_map/ppermute | solution.py:44
  101.1 17.2 %collective-permute-start.12 = (bf16[128,3584]{1,0:T(8,128)(2,1)S(1)}, bf16[128,3584]{1,0:T(8,128)(2,1)S(1)}, u32[]{:S(2)}, u32[]{:S(2)}) collective-permute-start(bf16[128,3584]{1,0:T(8,128)(2,1)S(1)} %collective-permute-done.9.refs_1_), channel_id=1, source_target_pairs={{0,6},{1,7},{2,0},{3,1},{4,2},{5,3},{6,4},{7,5},{8,14},{9,15},{10,... | collective-permute-start | bytes 2752520 | tf_op jit(solution)/shard_map/ppermute | solution.py:44
  101.7 18.6 %collective-permute-start.11 = (bf16[128,3584]{1,0:T(8,128)(2,1)S(1)}, bf16[128,3584]{1,0:T(8,128)(2,1)}, u32[]{:S(2)}, u32[]{:S(2)}) collective-permute-start(bf16[128,3584]{1,0:T(8,128)(2,1)S(1)} %collective-permute-done.7.refs_2_), channel_id=1, source_target_pairs={{0,2},{1,3},{2,4},{3,5},{4,6},{5,7},{6,0},{7,1},{8,9},{9,8},{10,11... | collective-permute-start | bytes 2752520 | tf_op jit(solution)/shard_map/ppermute | solution.py:44
  103.2 29.3 %collective-permute-start.13 = (bf16[128,3584]{1,0:T(8,128)(2,1)S(1)}, bf16[128,3584]{1,0:T(8,128)(2,1)}, u32[]{:S(2)}, u32[]{:S(2)}) collective-permute-start(bf16[128,3584]{1,0:T(8,128)(2,1)S(1)} %collective-permute-done.9.refs_1_), channel_id=1, source_target_pairs={{0,2},{1,3},{2,4},{3,5},{4,6},{5,7},{6,0},{7,1},{8,9},{9,8},{10,11... | collective-permute-start | bytes 2752520 | tf_op jit(solution)/shard_map/ppermute | solution.py:44
  118.3 18.0 %collective-permute-start.17 = (bf16[128,3584]{1,0:T(8,128)(2,1)S(1)}, bf16[128,3584]{1,0:T(8,128)(2,1)S(1)}, u32[]{:S(2)}, u32[]{:S(2)}) collective-permute-start(bf16[128,3584]{1,0:T(8,128)(2,1)S(1)} %collective-permute-done.12.refs_1_.refs_5_), channel_id=1, source_target_pairs={{0,6},{1,7},{2,0},{3,1},{4,2},{5,3},{6,4},{7,5},{8,9},{9,8},{10,11... | collective-permute-start | bytes 2752520 | tf_op jit(solution)/shard_map/ppermute | solution.py:44
  132.5 23.2 %collective-permute-start.16 = (bf16[128,3584]{1,0:T(8,128)(2,1)}, bf16[128,3584]{1,0:T(8,128)(2,1)S(1)}, u32[]{:S(2)}, u32[]{:S(2)}) collective-permute-start(bf16[128,3584]{1,0:T(8,128)(2,1)} %get-tuple-element.51), channel_id=1, source_target_pairs={{0,2},{1,3},{2,4},{3,5},{4,6},{5,7},{6,0},{7,1},{8,9},{9,8},{10,11... | collective-permute-start | bytes 2752520 | tf_op jit(solution)/shard_map/ppermute | solution.py:44
  132.7 23.1 %collective-permute-start.15 = (bf16[128,3584]{1,0:T(8,128)(2,1)}, bf16[128,3584]{1,0:T(8,128)(2,1)S(1)}, u32[]{:S(2)}, u32[]{:S(2)}) collective-permute-start(bf16[128,3584]{1,0:T(8,128)(2,1)} %get-tuple-element.49), channel_id=1, source_target_pairs={{0,6},{1,7},{2,0},{3,1},{4,2},{5,3},{6,4},{7,5},{8,14},{9,15},{10,... | collective-permute-start | bytes 2752520 | tf_op jit(solution)/shard_map/ppermute | solution.py:44
  135.8 20.0 %collective-permute-start.14 = (bf16[128,3584]{1,0:T(8,128)(2,1)}, bf16[128,3584]{1,0:T(8,128)(2,1)}, u32[]{:S(2)}, u32[]{:S(2)}) collective-permute-start(bf16[128,3584]{1,0:T(8,128)(2,1)} %get-tuple-element.47), channel_id=1, source_target_pairs={{0,1},{1,0},{2,3},{3,2},{4,5},{5,4},{6,7},{7,6},{8,10},{9,11},{10,... | collective-permute-start | bytes 2752520 | tf_op jit(solution)/shard_map/ppermute | solution.py:44
  155.8 22.7 %copy-start.9 = (bf16[128,3584]{1,0:T(8,128)(2,1)}, bf16[128,3584]{1,0:T(8,128)(2,1)S(1)}, u32[]{:S(2)}) copy-start(bf16[128,3584]{1,0:T(8,128)(2,1)S(1)} %collective-permute-done.16.refs_3_) | copy-start | bytes 2752516
  155.8 35.2 %collective-permute-start.21 = (bf16[128,3584]{1,0:T(8,128)(2,1)}, bf16[128,3584]{1,0:T(8,128)(2,1)S(1)}, u32[]{:S(2)}, u32[]{:S(2)}) collective-permute-start(bf16[128,3584]{1,0:T(8,128)(2,1)} %get-tuple-element.61), channel_id=1, source_target_pairs={{0,7},{1,6},{2,1},{3,0},{4,3},{5,2},{6,5},{7,4},{8,11},{9,10},{10,... | collective-permute-start | bytes 2752520 | tf_op jit(solution)/shard_map/ppermute | solution.py:44
  157.0 41.3 %collective-permute-start.20 = (bf16[128,3584]{1,0:T(8,128)(2,1)}, bf16[128,3584]{1,0:T(8,128)(2,1)S(1)}, u32[]{:S(2)}, u32[]{:S(2)}) collective-permute-start(bf16[128,3584]{1,0:T(8,128)(2,1)} %get-tuple-element.59), channel_id=1, source_target_pairs={{0,3},{1,2},{2,5},{3,4},{4,7},{5,6},{6,1},{7,0},{8,12},{9,13},{10,... | collective-permute-start | bytes 2752520 | tf_op jit(solution)/shard_map/ppermute | solution.py:44
  158.8 39.4 %collective-permute-start.19 = (bf16[128,3584]{1,0:T(8,128)(2,1)}, bf16[128,3584]{1,0:T(8,128)(2,1)}, u32[]{:S(2)}, u32[]{:S(2)}) collective-permute-start(bf16[128,3584]{1,0:T(8,128)(2,1)} %get-tuple-element.57), channel_id=1, source_target_pairs={{0,4},{1,5},{2,6},{3,7},{4,0},{5,1},{6,2},{7,3},{8,15},{9,14},{10,... | collective-permute-start | bytes 2752520 | tf_op jit(solution)/shard_map/ppermute | solution.py:44
  158.8 54.9 %collective-permute-start.18 = (bf16[128,3584]{1,0:T(8,128)(2,1)}, bf16[128,3584]{1,0:T(8,128)(2,1)}, u32[]{:S(2)}, u32[]{:S(2)}) collective-permute-start(bf16[128,3584]{1,0:T(8,128)(2,1)} %get-tuple-element.55), channel_id=1, source_target_pairs={{0,5},{1,4},{2,7},{3,6},{4,1},{5,0},{6,3},{7,2},{8,13},{9,12},{10,... | collective-permute-start | bytes 2752520 | tf_op jit(solution)/shard_map/ppermute | solution.py:44
  (11 other events, 109.6 us)

commit v5 on v4

--- a/solution.py
+++ b/solution.py
@@ -160,7 +160,7 @@
         right = jnp.concatenate([up[code >> 5] for code in codes], axis=0)
         pre[:, lanes(keys_ref[0, s])] += jnp.dot(left, right, preferred_element_type=F32)
 
-    run_groups(groups, 14, add)
+    run_groups(groups, 28, add)
 
     @pl.loop(0, pre.shape[0] // 32)
     def _(i):
@@ -223,7 +223,7 @@
             left, right, (((1,), (1,)), ((), ())), preferred_element_type=F32
         )
 
-    run_groups(groups, 14, add)
+    run_groups(groups, 28, add)
     late.wait()
 
     @pl.loop(0, slope.shape[0] // 32)
@@ -324,7 +324,7 @@
             left, right, (((1,), (1,)), ((), ())), preferred_element_type=F32
         )
 
-    run_groups(by_unit, 14, add_hidden_grad)
+    run_groups(by_unit, 28, add_hidden_grad)
     slope_copy.wait()
 
     @pl.loop(0, slope.shape[0] // 32)

time: 220 us -> 220 us (level)
  transfers between devices with their start and end apart: 22 -> 22, of which waited for: 7 -> 7; matrix products, arithmetic and copies ran while one was open for 2% -> 2% of each run, Pallas kernels for 44% -> 43%
where the time goes in v5:
time: 220 us
  Pallas kernels  104 us (47%)
  waiting for transfers between devices  79 us (36%)
  starting transfers between devices  29.3 us (13%)
  other arithmetic  3.68 us (2%)
  between operations  2.27 us (1%)
    ppermute x21, waiting for transfers between devices, along(): return lax.ppermute(value, ('section', 'tp'), pairs)  79 us
    ppermute x21, starting transfers between devices, along(): return lax.ppermute(value, ('section', 'tp'), pairs)  29.3 us
    pallas_call x2, Pallas kernels, hidden_of(): pl.pallas_call(functools.partial(hidden_kernel, groups), out_shape=[jax.S...  26.8 us
    pallas_call x1, Pallas kernels, both_grads_of(): pl.pallas_call(functools.partial(both_grads_kernel, pieces, by_unit, by_f...  18.1 us
    pallas_call x1, Pallas kernels, up_grad_of(): pl.pallas_call(functools.partial(up_grad_kernel, len(slopes), groups), ou...  15.1 us
    pallas_call x1, Pallas kernels, down_grad_of(): pl.pallas_call(functools.partial(down_grad_kernel, groups), out_shape=jax...  12.4 us
    pallas_call x1, Pallas kernels, unit_grad_of(): pl.pallas_call(functools.partial(unit_grad_kernel, pieces, groups), out_s...  12.1 us
    pallas_call x1, Pallas kernels, pre_grad_of(): pl.pallas_call(functools.partial(pre_grad_kernel, pieces, start, groups),...  10.1 us
  transfers between devices with their start and end apart: 22, of which 7 were waited for; matrix products, arithmetic and copies ran while one was open for 2% of the time, Pallas kernels for 43%

profile of v5, /device:TPU:14, one launch (start us, length us, event | category | flops | bytes accessed | tf_op | source)
XLA Modules:
  0.0 219.7 jit_solution(390185458912988037)
XLA Ops:
  0.6 3.6 %shard_map.112.refs_0_ = bf16[128,3584]{1,0:T(8,128)(2,1)} custom-call(bf16[128,3584]{1,0:T(8,128)(2,1)} %bitcast.46, f32[1,3584]{1,0:T(1,128)} %gain_ref.3), custom_call_target="tpu_custom_call" | custom-call | flops 1024 | bytes 1024 | tf_op jit(solution)/shard_map/pallas_call | solution.py:111
  4.7 1.9 collective-permute-start.2
  6.6 2.1 collective-permute-start.3
  12.4 22.4 %collective-permute-done.1.refs_1_ = bf16[128,3584]{1,0:T(8,128)(2,1)S(1)} collective-permute-done((bf16[128,3584]{1,0:T(8,128)(2,1)}, bf16[128,3584]{1,0:T(8,128)(2,1)S(1)}, u32[]{:S(2)}, u32[]{:S(2)}) %collective-permute-start.1) | collective-permute-done | bytes 917536 | tf_op jit(solution)/shard_map/ppermute | solution.py:44
  34.9 5.2 %collective-permute-start.5 = (bf16[128,3584]{1,0:T(8,128)(2,1)S(1)}, bf16[128,3584]{1,0:T(8,128)(2,1)}, u32[]{:S(2)}, u32[]{:S(2)}) collective-permute-start(bf16[128,3584]{1,0:T(8,128)(2,1)S(1)} %collective-permute-done.1.refs_1_), channel_id=1, source_target_pairs={{0,6},{1,7},{2,0},{3,1},{4,2},{5,3},{6,4},{7,5},{8,14},{9,15},{10,... | collective-permute-start | bytes 2752520 | tf_op jit(solution)/shard_map/ppermute | solution.py:44
  42.6 13.5 %shard_map.113 = (bf16[512,1792]{1,0:T(8,128)(2,1)}, f32[512,1792]{1,0:T(8,128)}) custom-call(s32[3,128]{1,0:T(4,128)} %pad_add_fusion.codes_ref, s32[3,128]{1,0:T(4,128)} %pad_add_fusion.1.keys_ref, bf16[128,3584]{1,0:T(8,128)(2,1)} %shard_map.112.refs_0_, bf16[128,3584]{1,0:T(8,128)(2,1)} %copy-done.6, bf16[128,3584]{1,0:T(8,128)(2,1)} %copy-done.7, ...), custom_call_target="tpu_custom_call" | custom-call | flops 1024 | bytes 1024 | tf_op jit(solution)/shard_map/pallas_call | solution.py:181
  56.1 4.4 %collective-permute-done.5.refs_1_.refs_5_ = bf16[128,3584]{1,0:T(8,128)(2,1)} collective-permute-done((bf16[128,3584]{1,0:T(8,128)(2,1)S(1)}, bf16[128,3584]{1,0:T(8,128)(2,1)}, u32[]{:S(2)}, u32[]{:S(2)}) %collective-permute-start.5) | collective-permute-done | bytes 917536 | tf_op jit(solution)/shard_map/ppermute | solution.py:44
  60.5 4.1 %collective-permute-done.4.refs_0_.refs_4_ = bf16[128,3584]{1,0:T(8,128)(2,1)} collective-permute-done((bf16[128,3584]{1,0:T(8,128)(2,1)S(1)}, bf16[128,3584]{1,0:T(8,128)(2,1)}, u32[]{:S(2)}, u32[]{:S(2)}) %collective-permute-start.4) | collective-permute-done | bytes 917536 | tf_op jit(solution)/shard_map/ppermute | solution.py:44
  65.1 1.9 collective-permute-start.7
  67.5 19.9 %collective-permute-done.8.refs_3_.refs_7_ = bf16[128,3584]{1,0:T(8,128)(2,1)} collective-permute-done((bf16[128,3584]{1,0:T(8,128)(2,1)}, bf16[128,3584]{1,0:T(8,128)(2,1)}, u32[]{:S(2)}, u32[]{:S(2)}) %collective-permute-start.8) | collective-permute-done | bytes 917536 | tf_op jit(solution)/shard_map/ppermute | solution.py:44
  87.4 13.3 %shard_map.114 = (bf16[512,1792]{1,0:T(8,128)(2,1)}, f32[512,1792]{1,0:T(8,128)}) custom-call(s32[3,128]{1,0:T(4,128)} %pad_add_fusion.codes_ref, s32[3,128]{1,0:T(4,128)} %pad_add_fusion.1.keys_ref, bf16[128,3584]{1,0:T(8,128)(2,1)} %collective-permute-done.4.refs_0_.refs_4_, bf16[128,3584]{1,0:T(8,128)(2,1)} %collective-permute-done.5.refs_1_.refs_5_, ...), custom_call_target="tpu_custom_call" | custom-call | flops 1024 | bytes 1024 | tf_op jit(solution)/shard_map/pallas_call | solution.py:181
  103.0 10.1 %shard_map.115.pre_grad_ref.refs_8_ = bf16[512,1792]{1,0:T(8,128)(2,1)} custom-call(s32[3,128]{1,0:T(4,128)} %pad_add_fusion.codes_ref, s32[3,128]{1,0:T(4,128)} %pad_add_fusion.1.keys_ref, bf16[128,3584]{1,0:T(8,128)(2,1)} %copy-done, bf16[128,3584]{1,0:T(8,128)(2,1)} %copy-done.3, bf16[128,3584]{1,0:T(8,128)(2,1)} %copy-done.2, ...), custom_call_target="tpu_custom_call" | custom-call | flops 1024 | bytes 1024 | tf_op jit(solution)/shard_map/pallas_call | solution.py:240
  113.1 5.3 %collective-permute-done.12.refs_1_.refs_5_ = bf16[128,3584]{1,0:T(8,128)(2,1)S(1)} collective-permute-done((bf16[128,3584]{1,0:T(8,128)(2,1)S(1)}, bf16[128,3584]{1,0:T(8,128)(2,1)S(1)}, u32[]{:S(2)}, u32[]{:S(2)}) %collective-permute-start.12) | collective-permute-done | bytes 917536 | tf_op jit(solution)/shard_map/ppermute | solution.py:44
  118.3 2.0 collective-permute-start.17
  120.4 12.1 %shard_map.116 = (bf16[128,3584]{1,0:T(8,128)(2,1)}, bf16[128,3584]{1,0:T(8,128)(2,1)}, bf16[128,3584]{1,0:T(8,128)(2,1)}, bf16[128,3584]{1,0:T(8,128)(2,1)}) custom-call(s32[3,128]{1,0:T(4,128)} %pad_add_fusion.codes_ref, s32[3,128]{1,0:T(4,128)} %pad_add_fusion.1.keys_ref, bf16[512,1792]{1,0:T(8,128)(2,1)} %shard_map.115.pre_grad_ref.refs_8_, ...), custom_call_target="tpu_custom_call" | custom-call | flops 1024 | bytes 1024 | tf_op jit(solution)/shard_map/pallas_call | solution.py:285
  132.6 3.2 %collective-permute-start.15 = (bf16[128,3584]{1,0:T(8,128)(2,1)}, bf16[128,3584]{1,0:T(8,128)(2,1)S(1)}, u32[]{:S(2)}, u32[]{:S(2)}) collective-permute-start(bf16[128,3584]{1,0:T(8,128)(2,1)} %get-tuple-element.49), channel_id=1, source_target_pairs={{0,6},{1,7},{2,0},{3,1},{4,2},{5,3},{6,4},{7,5},{8,14},{9,15},{10,... | collective-permute-start | bytes 2752520 | tf_op jit(solution)/shard_map/ppermute | solution.py:44
  137.3 18.1 %shard_map.117 = (bf16[512,1792]{1,0:T(8,128)(2,1)}, bf16[128,3584]{1,0:T(8,128)(2,1)}, bf16[128,3584]{1,0:T(8,128)(2,1)}, bf16[128,3584]{1,0:T(8,128)(2,1)}, bf16[128,3584]{1,0:T(8,128)(2,1)}) custom-call(s32[3,128]{1,0:T(4,128)} %pad_add_fusion.codes_ref, s32[3,128]{1,0:T(4,128)} %pad_add_fusion.1.keys_ref, ...), custom_call_target="tpu_custom_call" | custom-call | flops 1024 | bytes 1024 | tf_op jit(solution)/shard_map/pallas_call | solution.py:359
  156.6 1.8 collective-permute-start.20
  158.4 4.6 %collective-permute-start.18 = (bf16[128,3584]{1,0:T(8,128)(2,1)}, bf16[128,3584]{1,0:T(8,128)(2,1)}, u32[]{:S(2)}, u32[]{:S(2)}) collective-permute-start(bf16[128,3584]{1,0:T(8,128)(2,1)} %get-tuple-element.55), channel_id=1, source_target_pairs={{0,5},{1,4},{2,7},{3,6},{4,1},{5,0},{6,3},{7,2},{8,13},{9,12},{10,... | collective-permute-start | bytes 2752520 | tf_op jit(solution)/shard_map/ppermute | solution.py:44
  163.0 15.1 %shard_map.119 = bf16[98,128,128]{2,1,0:T(8,128)(2,1)} custom-call(s32[3,128]{1,0:T(4,128)} %pad_add_fusion.codes_ref, s32[3,128]{1,0:T(4,128)} %pad_add_fusion.1.keys_ref, bf16[128,3584]{1,0:T(8,128)(2,1)} %shard_map.112.refs_0_, bf16[128,3584]{1,0:T(8,128)(2,1)} %copy-done.6, bf16[128,3584]{1,0:T(8,128)(2,1)} %copy-done.7, bf16[128,3584]{1,0:T(8,128)(2,1)} %copy-done.8, ...), custom_call_target="tpu_custom_call" | custom-call | flops 1024 | bytes 1024 | tf_op jit(solution)/shard_map/pallas_call | solution.py:424
  178.1 12.4 %shard_map.120 = bf16[98,128,128]{2,1,0:T(8,128)(2,1)} custom-call(s32[3,128]{1,0:T(4,128)} %pad_add_fusion.codes_ref, s32[3,128]{1,0:T(4,128)} %pad_add_fusion.1.keys_ref, bf16[128,3584]{1,0:T(8,128)(2,1)} %copy-done, bf16[128,3584]{1,0:T(8,128)(2,1)} %copy-done.3, bf16[128,3584]{1,0:T(8,128)(2,1)} %copy-done.2, bf16[128,3584]{1,0:T(8,128)(2,1)} %copy-done.1, ...), custom_call_target="tpu_custom_call" | custom-call | flops 1024 | bytes 1024 | tf_op jit(solution)/shard_map/pallas_call | solution.py:483
  190.6 7.2 %collective-permute-done.20.refs_6_ = bf16[128,3584]{1,0:T(8,128)(2,1)S(1)} collective-permute-done((bf16[128,3584]{1,0:T(8,128)(2,1)}, bf16[128,3584]{1,0:T(8,128)(2,1)S(1)}, u32[]{:S(2)}, u32[]{:S(2)}) %collective-permute-start.20) | collective-permute-done | bytes 917536 | tf_op jit(solution)/shard_map/ppermute | solution.py:44
  197.8 15.8 %collective-permute-done.18.refs_4_ = bf16[128,3584]{1,0:T(8,128)(2,1)} collective-permute-done((bf16[128,3584]{1,0:T(8,128)(2,1)}, bf16[128,3584]{1,0:T(8,128)(2,1)}, u32[]{:S(2)}, u32[]{:S(2)}) %collective-permute-start.18) | collective-permute-done | bytes 917536 | tf_op jit(solution)/shard_map/ppermute | solution.py:44
  213.5 6.2 %shard_map.118 = bf16[128,3584]{1,0:T(8,128)(2,1)} custom-call(bf16[128,3584]{1,0:T(8,128)(2,1)} %bitcast.47, f32[1,3584]{1,0:T(1,128)} %gain_ref.3, bf16[128,3584]{1,0:T(8,128)(2,1)} %copy-done, bf16[128,3584]{1,0:T(8,128)(2,1)} %get-tuple-element.45.refs_0_, bf16[128,3584]{1,0:T(8,128)(2,1)} %collective-permute-done.14.refs_1_, ...), custom_call_target="tpu_custom_call" | custom-call | flops 1024 | bytes 1024 | tf_op jit(solution)/shard_map/pallas_call | solution.py:518
  (76 shorter events, 11.2 us)
Async XLA Ops:
  4.3 30.6 %collective-permute-start.1 = (bf16[128,3584]{1,0:T(8,128)(2,1)}, bf16[128,3584]{1,0:T(8,128)(2,1)S(1)}, u32[]{:S(2)}, u32[]{:S(2)}) collective-permute-start(bf16[128,3584]{1,0:T(8,128)(2,1)} %shard_map.112.refs_0_), channel_id=1, source_target_pairs={{0,1},{1,0},{2,3},{3,2},{4,5},{5,4},{6,7},{7,6},{8,14},{9,15},{10,... | collective-permute-start | bytes 2752520 | tf_op jit(solution)/shard_map/ppermute | solution.py:44
  4.7 30.1 %collective-permute-start.2 = (bf16[128,3584]{1,0:T(8,128)(2,1)}, bf16[128,3584]{1,0:T(8,128)(2,1)S(1)}, u32[]{:S(2)}, u32[]{:S(2)}) collective-permute-start(bf16[128,3584]{1,0:T(8,128)(2,1)} %shard_map.112.refs_0_), channel_id=1, source_target_pairs={{0,2},{1,3},{2,4},{3,5},{4,6},{5,7},{6,0},{7,1},{8,10},{9,11},{10,... | collective-permute-start | bytes 2752520 | tf_op jit(solution)/shard_map/ppermute | solution.py:44
  6.6 28.2 %collective-permute-start.3 = (bf16[128,3584]{1,0:T(8,128)(2,1)}, bf16[128,3584]{1,0:T(8,128)(2,1)S(1)}, u32[]{:S(2)}, u32[]{:S(2)}) collective-permute-start(bf16[128,3584]{1,0:T(8,128)(2,1)} %shard_map.112.refs_0_), channel_id=1, source_target_pairs={{0,6},{1,7},{2,0},{3,1},{4,2},{5,3},{6,4},{7,5},{8,9},{9,8},{10,11... | collective-permute-start | bytes 2752520 | tf_op jit(solution)/shard_map/ppermute | solution.py:44
  8.7 56.3 %collective-permute-start = (bf16[128,3584]{1,0:T(8,128)(2,1)}, bf16[128,3584]{1,0:T(8,128)(2,1)S(1)}, u32[]{:S(2)}, u32[]{:S(2)}) collective-permute-start(bf16[128,3584]{1,0:T(8,128)(2,1)} %bitcast.56), channel_id=1, source_target_pairs={{0,120},{8,0},{16,8},{24,16},{32,24},{40,32},{48,40},{56,48},{64,5... | collective-permute-start | bytes 2752520 | tf_op jit(solution)/shard_map/ppermute | solution.py:53
  34.9 25.6 %collective-permute-start.5 = (bf16[128,3584]{1,0:T(8,128)(2,1)S(1)}, bf16[128,3584]{1,0:T(8,128)(2,1)}, u32[]{:S(2)}, u32[]{:S(2)}) collective-permute-start(bf16[128,3584]{1,0:T(8,128)(2,1)S(1)} %collective-permute-done.1.refs_1_), channel_id=1, source_target_pairs={{0,6},{1,7},{2,0},{3,1},{4,2},{5,3},{6,4},{7,5},{8,14},{9,15},{10,... | collective-permute-start | bytes 2752520 | tf_op jit(solution)/shard_map/ppermute | solution.py:44
  40.0 20.5 %collective-permute-start.6 = (bf16[128,3584]{1,0:T(8,128)(2,1)S(1)}, bf16[128,3584]{1,0:T(8,128)(2,1)}, u32[]{:S(2)}, u32[]{:S(2)}) collective-permute-start(bf16[128,3584]{1,0:T(8,128)(2,1)S(1)} %collective-permute-done.1.refs_1_), channel_id=1, source_target_pairs={{0,2},{1,3},{2,4},{3,5},{4,6},{5,7},{6,0},{7,1},{8,9},{9,8},{10,11... | collective-permute-start | bytes 2752520 | tf_op jit(solution)/shard_map/ppermute | solution.py:44
  40.0 24.5 %collective-permute-start.4 = (bf16[128,3584]{1,0:T(8,128)(2,1)S(1)}, bf16[128,3584]{1,0:T(8,128)(2,1)}, u32[]{:S(2)}, u32[]{:S(2)}) collective-permute-start(bf16[128,3584]{1,0:T(8,128)(2,1)S(1)} %collective-permute-done.2.refs_2_), channel_id=1, source_target_pairs={{0,2},{1,3},{2,4},{3,5},{4,6},{5,7},{6,0},{7,1},{8,9},{9,8},{10,11... | collective-permute-start | bytes 2752520 | tf_op jit(solution)/shard_map/ppermute | solution.py:44
  64.6 22.8 %collective-permute-start.8 = (bf16[128,3584]{1,0:T(8,128)(2,1)}, bf16[128,3584]{1,0:T(8,128)(2,1)}, u32[]{:S(2)}, u32[]{:S(2)}) collective-permute-start(bf16[128,3584]{1,0:T(8,128)(2,1)} %collective-permute-done.5.refs_1_.refs_5_), channel_id=1, source_target_pairs={{0,6},{1,7},{2,0},{3,1},{4,2},{5,3},{6,4},{7,5},{8,9},{9,8},{10,11... | collective-permute-start | bytes 2752520 | tf_op jit(solution)/shard_map/ppermute | solution.py:44
  65.1 35.7 %copy-start = (bf16[128,3584]{1,0:T(8,128)(2,1)}, bf16[128,3584]{1,0:T(8,128)(2,1)S(1)}, u32[]{:S(2)}) copy-start(bf16[128,3584]{1,0:T(8,128)(2,1)S(1)} %collective-permute-done.refs_0_.grad_ref) | copy-start | bytes 2752516
  65.1 35.7 %collective-permute-start.10 = (bf16[128,3584]{1,0:T(8,128)(2,1)S(1)}, bf16[128,3584]{1,0:T(8,128)(2,1)S(1)}, u32[]{:S(2)}, u32[]{:S(2)}) collective-permute-start(bf16[128,3584]{1,0:T(8,128)(2,1)S(1)} %collective-permute-done.refs_0_.grad_ref), channel_id=1, source_target_pairs={{0,6},{1,7},{2,0},{3,1},{4,2},{5,3},{6,4},{7,5},{8,9},{9,8},{10,11... | collective-permute-start | bytes 2752520 | tf_op jit(solution)/shard_map/ppermute | solution.py:44
  65.1 35.7 %collective-permute-start.7 = (bf16[128,3584]{1,0:T(8,128)(2,1)S(1)}, bf16[128,3584]{1,0:T(8,128)(2,1)S(1)}, u32[]{:S(2)}, u32[]{:S(2)}) collective-permute-start(bf16[128,3584]{1,0:T(8,128)(2,1)S(1)} %collective-permute-done.refs_0_.grad_ref), channel_id=1, source_target_pairs={{0,2},{1,3},{2,4},{3,5},{4,6},{5,7},{6,0},{7,1},{8,10},{9,11},{10,... | collective-permute-start | bytes 2752520 | tf_op jit(solution)/shard_map/ppermute | solution.py:44
  67.1 33.7 %collective-permute-start.9 = (bf16[128,3584]{1,0:T(8,128)(2,1)S(1)}, bf16[128,3584]{1,0:T(8,128)(2,1)S(1)}, u32[]{:S(2)}, u32[]{:S(2)}) collective-permute-start(bf16[128,3584]{1,0:T(8,128)(2,1)S(1)} %collective-permute-done.refs_0_.grad_ref), channel_id=1, source_target_pairs={{0,1},{1,0},{2,3},{3,2},{4,5},{5,4},{6,7},{7,6},{8,14},{9,15},{10,... | collective-permute-start | bytes 2752520 | tf_op jit(solution)/shard_map/ppermute | solution.py:44
  100.8 17.5 %collective-permute-start.12 = (bf16[128,3584]{1,0:T(8,128)(2,1)S(1)}, bf16[128,3584]{1,0:T(8,128)(2,1)S(1)}, u32[]{:S(2)}, u32[]{:S(2)}) collective-permute-start(bf16[128,3584]{1,0:T(8,128)(2,1)S(1)} %collective-permute-done.9.refs_1_), channel_id=1, source_target_pairs={{0,6},{1,7},{2,0},{3,1},{4,2},{5,3},{6,4},{7,5},{8,14},{9,15},{10,... | collective-permute-start | bytes 2752520 | tf_op jit(solution)/shard_map/ppermute | solution.py:44
  101.5 18.9 %collective-permute-start.11 = (bf16[128,3584]{1,0:T(8,128)(2,1)S(1)}, bf16[128,3584]{1,0:T(8,128)(2,1)}, u32[]{:S(2)}, u32[]{:S(2)}) collective-permute-start(bf16[128,3584]{1,0:T(8,128)(2,1)S(1)} %collective-permute-done.7.refs_2_), channel_id=1, source_target_pairs={{0,2},{1,3},{2,4},{3,5},{4,6},{5,7},{6,0},{7,1},{8,9},{9,8},{10,11... | collective-permute-start | bytes 2752520 | tf_op jit(solution)/shard_map/ppermute | solution.py:44
  102.9 29.6 %collective-permute-start.13 = (bf16[128,3584]{1,0:T(8,128)(2,1)S(1)}, bf16[128,3584]{1,0:T(8,128)(2,1)}, u32[]{:S(2)}, u32[]{:S(2)}) collective-permute-start(bf16[128,3584]{1,0:T(8,128)(2,1)S(1)} %collective-permute-done.9.refs_1_), channel_id=1, source_target_pairs={{0,2},{1,3},{2,4},{3,5},{4,6},{5,7},{6,0},{7,1},{8,9},{9,8},{10,11... | collective-permute-start | bytes 2752520 | tf_op jit(solution)/shard_map/ppermute | solution.py:44
  118.3 17.9 %collective-permute-start.17 = (bf16[128,3584]{1,0:T(8,128)(2,1)S(1)}, bf16[128,3584]{1,0:T(8,128)(2,1)S(1)}, u32[]{:S(2)}, u32[]{:S(2)}) collective-permute-start(bf16[128,3584]{1,0:T(8,128)(2,1)S(1)} %collective-permute-done.12.refs_1_.refs_5_), channel_id=1, source_target_pairs={{0,6},{1,7},{2,0},{3,1},{4,2},{5,3},{6,4},{7,5},{8,9},{9,8},{10,11... | collective-permute-start | bytes 2752520 | tf_op jit(solution)/shard_map/ppermute | solution.py:44
  132.5 22.8 %collective-permute-start.16 = (bf16[128,3584]{1,0:T(8,128)(2,1)}, bf16[128,3584]{1,0:T(8,128)(2,1)S(1)}, u32[]{:S(2)}, u32[]{:S(2)}) collective-permute-start(bf16[128,3584]{1,0:T(8,128)(2,1)} %get-tuple-element.51), channel_id=1, source_target_pairs={{0,2},{1,3},{2,4},{3,5},{4,6},{5,7},{6,0},{7,1},{8,9},{9,8},{10,11... | collective-permute-start | bytes 2752520 | tf_op jit(solution)/shard_map/ppermute | solution.py:44
  132.6 22.8 %collective-permute-start.15 = (bf16[128,3584]{1,0:T(8,128)(2,1)}, bf16[128,3584]{1,0:T(8,128)(2,1)S(1)}, u32[]{:S(2)}, u32[]{:S(2)}) collective-permute-start(bf16[128,3584]{1,0:T(8,128)(2,1)} %get-tuple-element.49), channel_id=1, source_target_pairs={{0,6},{1,7},{2,0},{3,1},{4,2},{5,3},{6,4},{7,5},{8,14},{9,15},{10,... | collective-permute-start | bytes 2752520 | tf_op jit(solution)/shard_map/ppermute | solution.py:44
  135.8 19.6 %collective-permute-start.14 = (bf16[128,3584]{1,0:T(8,128)(2,1)}, bf16[128,3584]{1,0:T(8,128)(2,1)}, u32[]{:S(2)}, u32[]{:S(2)}) collective-permute-start(bf16[128,3584]{1,0:T(8,128)(2,1)} %get-tuple-element.47), channel_id=1, source_target_pairs={{0,1},{1,0},{2,3},{3,2},{4,5},{5,4},{6,7},{7,6},{8,10},{9,11},{10,... | collective-permute-start | bytes 2752520 | tf_op jit(solution)/shard_map/ppermute | solution.py:44
  155.4 35.1 %collective-permute-start.21 = (bf16[128,3584]{1,0:T(8,128)(2,1)}, bf16[128,3584]{1,0:T(8,128)(2,1)S(1)}, u32[]{:S(2)}, u32[]{:S(2)}) collective-permute-start(bf16[128,3584]{1,0:T(8,128)(2,1)} %get-tuple-element.61), channel_id=1, source_target_pairs={{0,7},{1,6},{2,1},{3,0},{4,3},{5,2},{6,5},{7,4},{8,11},{9,10},{10,... | collective-permute-start | bytes 2752520 | tf_op jit(solution)/shard_map/ppermute | solution.py:44
  156.6 41.2 %collective-permute-start.20 = (bf16[128,3584]{1,0:T(8,128)(2,1)}, bf16[128,3584]{1,0:T(8,128)(2,1)S(1)}, u32[]{:S(2)}, u32[]{:S(2)}) collective-permute-start(bf16[128,3584]{1,0:T(8,128)(2,1)} %get-tuple-element.59), channel_id=1, source_target_pairs={{0,3},{1,2},{2,5},{3,4},{4,7},{5,6},{6,1},{7,0},{8,12},{9,13},{10,... | collective-permute-start | bytes 2752520 | tf_op jit(solution)/shard_map/ppermute | solution.py:44
  158.4 39.3 %collective-permute-start.19 = (bf16[128,3584]{1,0:T(8,128)(2,1)}, bf16[128,3584]{1,0:T(8,128)(2,1)}, u32[]{:S(2)}, u32[]{:S(2)}) collective-permute-start(bf16[128,3584]{1,0:T(8,128)(2,1)} %get-tuple-element.57), channel_id=1, source_target_pairs={{0,4},{1,5},{2,6},{3,7},{4,0},{5,1},{6,2},{7,3},{8,15},{9,14},{10,... | collective-permute-start | bytes 2752520 | tf_op jit(solution)/shard_map/ppermute | solution.py:44
  158.4 55.1 %collective-permute-start.18 = (bf16[128,3584]{1,0:T(8,128)(2,1)}, bf16[128,3584]{1,0:T(8,128)(2,1)}, u32[]{:S(2)}, u32[]{:S(2)}) collective-permute-start(bf16[128,3584]{1,0:T(8,128)(2,1)} %get-tuple-element.55), channel_id=1, source_target_pairs={{0,5},{1,4},{2,7},{3,6},{4,1},{5,0},{6,3},{7,2},{8,13},{9,12},{10,... | collective-permute-start | bytes 2752520 | tf_op jit(solution)/shard_map/ppermute | solution.py:44
  190.6 23.0 %copy-start.11 = (bf16[128,3584]{1,0:T(8,128)(2,1)}, bf16[128,3584]{1,0:T(8,128)(2,1)S(1)}, u32[]{:S(2)}) copy-start(bf16[128,3584]{1,0:T(8,128)(2,1)S(1)} %collective-permute-done.21.refs_7_) | copy-start | bytes 2752516
  (11 other events, 110.0 us)
